TPU v7x, 32 devices: a whole 2x2x4 slice. The times are simulated.
32 devices in a mesh: blk: 16 (over z, y, core), uly: 2 (over x).
Axes of the slice: x: 2, y: 2, z: 4, core: 2. Of those that a mesh axis runs over, the one named last changes fastest.
Arguments:
- hidden: bfloat16 [2, 2048, 1024], P('uly', 'blk'), may hold values from -6 to 6
- skip_in: bfloat16 [2, 2048, 1024], P('uly', 'blk'), may hold values from -6 to 6
- time_embed: bfloat16 [2, 1, 1024], P('uly'), may hold values from -6 to 6
- lengths: int32 [2, 1], replicated, may hold values from 0 to 2048, as said below
- cotangent: bfloat16 [2, 2048, 1024], P('uly', 'blk'), may hold values from -6 to 6
- w_skip: bfloat16 [2048, 1024], P(('blk', 'uly')), may hold values from -0.125 to 0.125
- b_skip: bfloat16 [1024], P(('blk', 'uly')), may hold values from -3 to 3
- w_mod: bfloat16 [1024, 4096], P(('blk', 'uly')), may hold values from -0.0625 to 0.0625
- w_qkv: bfloat16 [1024, 3072], P(('blk', 'uly')), may hold values from -0.1875 to 0.1875
- w_out: bfloat16 [1024, 1024], P(('blk', 'uly')), may hold values from -0.1875 to 0.1875
- w_up: bfloat16 [1024, 4096], P(('blk', 'uly')), may hold values from -0.1875 to 0.1875
- b_up: bfloat16 [4096], P(('blk', 'uly')), may hold values from -3 to 3
- w_down: bfloat16 [4096, 1024], P(('blk', 'uly')), may hold values from -0.09375 to 0.09375
- b_down: bfloat16 [1024], P(('blk', 'uly')), may hold values from -3 to 3
Outputs:
- output: bfloat16 [2, 2048, 1024], P('uly', 'blk')
- hidden_grad: bfloat16 [2, 2048, 1024], P('uly', 'blk')
- skip_grad: bfloat16 [2, 2048, 1024], P('uly', 'blk')
- time_grad: float32 [2, 1, 1024], P('uly')
- w_skip_grad: float32 [2048, 1024], P(('blk', 'uly'))
- b_skip_grad: float32 [1024], P(('blk', 'uly'))
- w_mod_grad: float32 [1024, 4096], P(('blk', 'uly'))
- w_qkv_grad: float32 [1024, 3072], P(('blk', 'uly'))
- w_out_grad: float32 [1024, 1024], P(('blk', 'uly'))
- w_up_grad: float32 [1024, 4096], P(('blk', 'uly'))
- b_up_grad: float32 [4096], P(('blk', 'uly'))
- w_down_grad: float32 [4096, 1024], P(('blk', 'uly'))
- b_down_grad: float32 [1024], P(('blk', 'uly'))
Inputs may be any that keep to these rules, and one draw needn't show every extreme that they name: Each row's lengths are its utterances in frame order; their sum is at most 2048, and the frames after it are padding. In one row, drawn from the seed, a single utterance fills all 2048 frames and the row's other entries are 0; in the other rows each entry is between 1024 and 2048.
All inputs are finite; a program needn't handle non-finite values.
Results may differ from a plain program's by a relative error of at most 0.013.
Values may be sent and summed in bfloat16 or wider, within the bound.
A program may use at most 256 MiB of HBM per device.

v0:
```python
import math

import jax
import jax.numpy as jnp
from jax import lax
from jax.sharding import PartitionSpec as P

HEADS = 16
HEAD_DIM = 64


exact_mode = lax.Precision.HIGHEST
epsilon = 1e-05


def passed_along(x, axis, by):
    devices = lax.axis_size(axis)
    return lax.ppermute(x, axis, [(i, (i + by) % devices) for i in range(devices)])


def segment_info(len_row, positions):
    slots = len_row.shape[0]
    ends = jnp.cumsum(len_row)
    starts = ends - len_row
    total = ends[-1]
    seg_ids = jnp.sum((positions[:, None] >= ends[None, :]).astype(jnp.int32), axis=1)
    onehot = seg_ids[:, None] == jnp.arange(slots, dtype=jnp.int32)[None, :]
    begin = jnp.sum(jnp.where(onehot, starts[None, :], 0), axis=1)
    begin = begin + jnp.where(seg_ids == slots, total, 0)
    return (seg_ids, positions - begin, seg_ids < slots)


def rotary(values, offsets):
    half = values.shape[-1] // 2
    freq = 10000.0 ** (-jnp.arange(half, dtype=jnp.float32) / half)
    angle = offsets.astype(jnp.float32)[:, None] * freq[None, :]
    cosine = jnp.cos(angle)[:, None, :]
    sine = jnp.sin(angle)[:, None, :]
    first = values[..., :half]
    second = values[..., half:]
    return jnp.concatenate([first * cosine - second * sine, second * cosine + first * sine], -1)


def modulate(values, scale, shift):
    center = values - jnp.mean(values, -1, keepdims=True)
    spread = jnp.mean(center * center, -1, keepdims=True)
    return center * lax.rsqrt(spread + epsilon) * (1.0 + scale) + shift


def contract_rows(left, right):
    return lax.dot_general(
        left, right, (((0,), (0,)), ((), ())), preferred_element_type=jnp.float32
    )


def contract_cols(left, right):
    return lax.dot_general(
        left, right, (((1,), (1,)), ((), ())), preferred_element_type=jnp.float32
    )


def gelu_exact(values):
    return jax.nn.gelu(values, approximate=False)


def per_device(
    hidden,
    skip_in,
    time_embed,
    lengths,
    cotangent,
    w_skip,
    b_skip,
    w_mod,
    w_qkv,
    w_out,
    w_up,
    b_up,
    w_down,
    b_down,
):
    gathered = (
        lax.all_gather(w_skip, ("blk", "uly"), axis=0, tiled=True),
        lax.all_gather(b_skip, ("blk", "uly"), axis=0, tiled=True),
        lax.all_gather(w_mod, ("blk", "uly"), axis=0, tiled=True),
        lax.all_gather(w_qkv, ("blk", "uly"), axis=0, tiled=True),
        lax.all_gather(w_out, ("blk", "uly"), axis=0, tiled=True),
        lax.all_gather(w_up, ("blk", "uly"), axis=0, tiled=True),
        lax.all_gather(b_up, ("blk", "uly"), axis=0, tiled=True),
        lax.all_gather(w_down, ("blk", "uly"), axis=0, tiled=True),
        lax.all_gather(b_down, ("blk", "uly"), axis=0, tiled=True),
    )
    (
        skip_full,
        bskip_full,
        mod_full,
        qkv_full,
        out_full,
        up_full,
        bup_full,
        down_full,
        bdown_full,
    ) = gathered
    group_count = lax.axis_size("uly")
    cycle_size = lax.axis_size("blk")
    frame_count = hidden.shape[1]
    row_count = lengths.shape[0]
    slot_count = lengths.shape[1]
    local_heads = HEADS // group_count
    span = local_heads * HEAD_DIM
    scaling = HEAD_DIM ** (-0.5)
    block_index = lax.axis_index("blk")
    row_index = lax.axis_index("uly")
    frame_pos = block_index * frame_count + jnp.arange(frame_count, dtype=jnp.int32)
    all_seg, all_offsets, all_valid = jax.vmap(lambda len_row: segment_info(len_row, frame_pos))(
        lengths
    )
    own_seg = lax.dynamic_index_in_dim(all_seg, row_index, 0, keepdims=False)
    own_offsets = lax.dynamic_index_in_dim(all_offsets, row_index, 0, keepdims=False)
    joined = jnp.concatenate([hidden[0], skip_in[0]], 1)
    base = jnp.dot(joined, skip_full, preferred_element_type=jnp.float32) + bskip_full.astype(
        jnp.float32
    )
    time_row = time_embed[0]
    mods = jnp.dot(time_row, mod_full, preferred_element_type=jnp.float32)
    selector = (own_seg[:, None] == jnp.arange(slot_count, dtype=jnp.int32)[None, :]).astype(
        jnp.float32
    )
    frame_mod = jnp.dot(selector, mods, precision=exact_mode)
    a_scale, a_shift, f_scale, f_shift = jnp.split(frame_mod, 4, 1)
    normed_full, norm_back = jax.vjp(modulate, base, a_scale, a_shift)
    normed = normed_full.astype(jnp.bfloat16)
    projected = jnp.dot(normed, qkv_full, preferred_element_type=jnp.float32).reshape(
        frame_count, 3, HEADS, HEAD_DIM
    )

    def place(parts):
        return jnp.stack(
            [rotary(parts[:, 0], own_offsets), rotary(parts[:, 1], own_offsets), parts[:, 2]], 1
        )

    turned, unturn = jax.vjp(place, projected)
    sending = turned.astype(jnp.bfloat16).reshape(1, frame_count, 3, group_count, span)
    head_data = lax.all_to_all(sending, "uly", split_axis=3, concat_axis=0, tiled=True)
    query = head_data[:, :, 0, 0].reshape(row_count, frame_count, local_heads, HEAD_DIM)
    kv_pairs = head_data[:, :, 1:, 0]

    def key_segments(start, count):
        key_pos = start + jnp.arange(count, dtype=jnp.int32)
        return jax.vmap(lambda len_row: segment_info(len_row, key_pos)[0])(lengths)

    start_state = (
        jnp.full((row_count, local_heads, frame_count), -1e30, jnp.float32),
        jnp.zeros((row_count, local_heads, frame_count), jnp.float32),
        jnp.zeros((row_count, frame_count, local_heads, HEAD_DIM), jnp.float32),
    )
    piece = lax.all_gather(kv_pairs, "blk", axis=1, tiled=True)
    total = piece.shape[1]
    step = math.gcd(total, max(frame_count, 1024))

    def sub_step(step_index, state):
        run_max, run_total, run_acc = state
        offset = step_index * step
        section = lax.dynamic_slice_in_dim(piece, offset, step, 1)
        key_seg = key_segments(offset, step)
        key_part = section[:, :, 0].reshape(row_count, step, local_heads, HEAD_DIM)
        value_part = section[:, :, 1].reshape(row_count, step, local_heads, HEAD_DIM)
        mask = all_seg[:, None, :, None] == key_seg[:, None, None, :]
        score = (
            jnp.einsum("rqhd,rkhd->rhqk", query, key_part, preferred_element_type=jnp.float32)
            * scaling
        )
        masked = jnp.where(mask, score, -1e30)
        fresh = jnp.maximum(run_max, jnp.max(masked, -1))
        weights = jnp.where(mask, jnp.exp(masked - fresh[..., None]), 0.0)
        decay = jnp.exp(run_max - fresh)
        run_total = run_total * decay + jnp.sum(weights, -1)
        run_acc = run_acc * jnp.swapaxes(decay, 1, 2)[..., None] + jnp.einsum(
            "rhqk,rkhd->rqhd",
            weights.astype(jnp.bfloat16),
            value_part,
            preferred_element_type=jnp.float32,
        )
        return (fresh, run_total, run_acc)

    run_max, run_total, run_acc = lax.fori_loop(0, total // step, sub_step, start_state)
    attended = run_acc / jnp.swapaxes(run_total, 1, 2)[..., None]
    log_total = run_max + jnp.log(run_total)
    valid_half = all_valid.astype(jnp.bfloat16)[:, :, None, None]
    leaving = (attended * all_valid.astype(jnp.float32)[:, :, None, None]).astype(jnp.bfloat16)
    leaving = leaving.reshape(row_count, frame_count, 1, span)
    mixed = lax.all_to_all(leaving, "uly", split_axis=0, concat_axis=2, tiled=True).reshape(
        frame_count, HEADS * HEAD_DIM
    )
    branch = jnp.dot(mixed, out_full, preferred_element_type=jnp.float32)
    middle = base + branch
    normed2_full, norm2_back = jax.vjp(modulate, middle, f_scale, f_shift)
    normed2 = normed2_full.astype(jnp.bfloat16)
    inner = jnp.dot(normed2, up_full, preferred_element_type=jnp.float32) + bup_full.astype(
        jnp.float32
    )
    act_full, act_back = jax.vjp(gelu_exact, inner)
    act = act_full.astype(jnp.bfloat16)
    result = (
        middle
        + jnp.dot(act, down_full, preferred_element_type=jnp.float32)
        + bdown_full.astype(jnp.float32)
    )
    output = result.astype(jnp.bfloat16)[None]
    again = (
        lax.all_gather(w_skip, ("blk", "uly"), axis=0, tiled=True),
        lax.all_gather(w_mod, ("blk", "uly"), axis=0, tiled=True),
        lax.all_gather(w_qkv, ("blk", "uly"), axis=0, tiled=True),
        lax.all_gather(w_out, ("blk", "uly"), axis=0, tiled=True),
        lax.all_gather(w_up, ("blk", "uly"), axis=0, tiled=True),
        lax.all_gather(w_down, ("blk", "uly"), axis=0, tiled=True),
    )
    skip_back, mod_back, qkv_back, out_back, up_back, down_back = again
    upstream = cotangent[0]
    upstream_full = upstream.astype(jnp.float32)
    grad_down = contract_rows(act, upstream)
    grad_bdown = jnp.sum(upstream_full, 0)
    grad_act = contract_cols(upstream, down_back)
    grad_inner = act_back(grad_act)[0].astype(jnp.bfloat16)
    grad_up = contract_rows(normed2, grad_inner)
    grad_bup = jnp.sum(grad_inner.astype(jnp.float32), 0)
    grad_normed2 = contract_cols(grad_inner, up_back)
    grad_mid_norm, grad_fscale, grad_fshift = norm2_back(grad_normed2)
    grad_middle = upstream_full + grad_mid_norm
    grad_branch = grad_middle.astype(jnp.bfloat16)
    grad_out = contract_rows(mixed, grad_branch)
    grad_mixed = (
        contract_cols(grad_branch, out_back)
        .astype(jnp.bfloat16)
        .reshape(1, frame_count, group_count, span)
    )
    returning = lax.all_to_all(grad_mixed, "uly", split_axis=2, concat_axis=0, tiled=True)
    grad_attn = returning.reshape(row_count, frame_count, local_heads, HEAD_DIM) * valid_half
    delta_rows = jnp.swapaxes(jnp.sum(grad_attn.astype(jnp.float32) * attended, -1), 1, 2)

    def contribution(held_pairs, key_start):
        count = held_pairs.shape[1]
        key_seg = key_segments(key_start, count)
        key_part = held_pairs[:, :, 0].reshape(row_count, count, local_heads, HEAD_DIM)
        value_part = held_pairs[:, :, 1].reshape(row_count, count, local_heads, HEAD_DIM)
        mask = all_seg[:, None, :, None] == key_seg[:, None, None, :]
        score = (
            jnp.einsum("rqhd,rkhd->rhqk", query, key_part, preferred_element_type=jnp.float32)
            * scaling
        )
        weights = jnp.exp(jnp.where(mask, score - log_total[..., None], -1e30))
        grad_weights = jnp.einsum(
            "rqhd,rkhd->rhqk", grad_attn, value_part, preferred_element_type=jnp.float32
        )
        grad_score = (weights * (grad_weights - delta_rows[..., None])).astype(jnp.bfloat16)
        more_query = (
            jnp.einsum("rhqk,rkhd->rqhd", grad_score, key_part, preferred_element_type=jnp.float32)
            * scaling
        )
        more_key = (
            jnp.einsum("rhqk,rqhd->rkhd", grad_score, query, preferred_element_type=jnp.float32)
            * scaling
        )
        more_value = jnp.einsum(
            "rhqk,rqhd->rkhd",
            weights.astype(jnp.bfloat16),
            grad_attn,
            preferred_element_type=jnp.float32,
        )
        more_pairs = jnp.stack(
            [more_key.reshape(row_count, count, span), more_value.reshape(row_count, count, span)],
            2,
        )
        return (more_query, more_pairs)

    def pass_grads(held_grads):
        return passed_along(held_grads.astype(jnp.bfloat16), "blk", 1).astype(held_grads.dtype)

    def cycle_step(turn, state):
        held_pairs, held_grads, query_grad = state
        more_query, more_pairs = contribution(
            held_pairs, (block_index - turn) % cycle_size * frame_count
        )
        held_pairs = passed_along(held_pairs, "blk", 1)
        held_grads = pass_grads(held_grads + more_pairs)
        return (held_pairs, held_grads, query_grad + more_query)

    cycle_start = (
        kv_pairs,
        jnp.zeros((row_count, frame_count, 2, span), jnp.float32),
        jnp.zeros((row_count, frame_count, local_heads, HEAD_DIM), jnp.float32),
    )
    held_pairs, held_grads, query_grad = lax.fori_loop(0, cycle_size - 1, cycle_step, cycle_start)
    last_query, last_pairs = contribution(
        held_pairs, (block_index - (cycle_size - 1)) % cycle_size * frame_count
    )
    pair_grads = pass_grads(held_grads + last_pairs)
    query_grad = query_grad + last_query
    head_grads = jnp.concatenate(
        [
            query_grad.astype(jnp.bfloat16).reshape(row_count, frame_count, 1, span),
            pair_grads.astype(jnp.bfloat16),
        ],
        2,
    ).reshape(row_count, frame_count, 3, 1, span)
    frames_grad = lax.all_to_all(head_grads, "uly", split_axis=0, concat_axis=3, tiled=True)
    frames_grad = frames_grad.reshape(frame_count, 3, HEADS, HEAD_DIM).astype(jnp.float32)
    grad_projected = (
        unturn(frames_grad)[0].astype(jnp.bfloat16).reshape(frame_count, 3 * HEADS * HEAD_DIM)
    )
    grad_qkv = contract_rows(normed, grad_projected)
    grad_normed = contract_cols(grad_projected, qkv_back)
    grad_base_norm, grad_ascale, grad_ashift = norm_back(grad_normed)
    grad_base = (grad_middle + grad_base_norm).astype(jnp.bfloat16)
    grad_skip_w = contract_rows(joined, grad_base)
    grad_bskip = jnp.sum(grad_base.astype(jnp.float32), 0)
    grad_joined = contract_cols(grad_base, skip_back).astype(jnp.bfloat16)
    model_width = hidden.shape[2]
    hidden_grad = grad_joined[:, :model_width][None]
    skip_grad = grad_joined[:, model_width:][None]
    frame_mod_grad = jnp.concatenate([grad_ascale, grad_ashift, grad_fscale, grad_fshift], 1)
    slot_grad = lax.dot_general(
        selector, frame_mod_grad, (((0,), (0,)), ((), ())), precision=exact_mode
    )
    grad_mod = lax.dot_general(
        time_row.astype(jnp.float32), slot_grad, (((0,), (0,)), ((), ())), precision=exact_mode
    )
    slot_total = lax.psum(slot_grad, "blk")
    time_grad = lax.dot_general(
        slot_total, mod_back.astype(jnp.float32), (((1,), (1,)), ((), ())), precision=exact_mode
    )[None]
    owned = (
        lax.psum_scatter(grad_skip_w, ("blk", "uly"), scatter_dimension=0, tiled=True),
        lax.psum_scatter(grad_bskip, ("blk", "uly"), scatter_dimension=0, tiled=True),
        lax.psum_scatter(grad_mod, ("blk", "uly"), scatter_dimension=0, tiled=True),
        lax.psum_scatter(grad_qkv, ("blk", "uly"), scatter_dimension=0, tiled=True),
        lax.psum_scatter(grad_out, ("blk", "uly"), scatter_dimension=0, tiled=True),
        lax.psum_scatter(grad_up, ("blk", "uly"), scatter_dimension=0, tiled=True),
        lax.psum_scatter(grad_bup, ("blk", "uly"), scatter_dimension=0, tiled=True),
        lax.psum_scatter(grad_down, ("blk", "uly"), scatter_dimension=0, tiled=True),
        lax.psum_scatter(grad_bdown, ("blk", "uly"), scatter_dimension=0, tiled=True),
    )
    return (
        output,
        hidden_grad,
        skip_grad,
        time_grad,
        owned[0],
        owned[1],
        owned[2],
        owned[3],
        owned[4],
        owned[5],
        owned[6],
        owned[7],
        owned[8],
    )


def solution(mesh):
    placed = (
        P("uly", "blk", None),
        P("uly", "blk", None),
        P("uly", None, None),
        P(),
        P("uly", "blk", None),
        P(("blk", "uly"), None),
        P(("blk", "uly")),
        P(("blk", "uly"), None),
        P(("blk", "uly"), None),
        P(("blk", "uly"), None),
        P(("blk", "uly"), None),
        P(("blk", "uly")),
        P(("blk", "uly"), None),
        P(("blk", "uly")),
    )
    return jax.shard_map(
        per_device,
        mesh=mesh,
        in_specs=placed,
        out_specs=(
            P("uly", "blk", None),
            P("uly", "blk", None),
            P("uly", "blk", None),
            P("uly", None, None),
            P(("blk", "uly"), None),
            P(("blk", "uly")),
            P(("blk", "uly"), None),
            P(("blk", "uly"), None),
            P(("blk", "uly"), None),
            P(("blk", "uly"), None),
            P(("blk", "uly")),
            P(("blk", "uly"), None),
            P(("blk", "uly")),
        ),
        check_vma=False,
    )
```

profile of v0, /device:TPU:0, one launch (start us, length us, event | category | flops | bytes accessed | tf_op | source)
XLA Modules:
  0.0 2367.6 jit_solution(8851013903226999265)
XLA Ops:
  11.1 42.1 %all-reduce.13 = (bf16[1024]{0:T(1024)(128)(2,1)S(1)}, bf16[1024]{0:T(1024)(128)(2,1)}) all-reduce(bf16[1024]{0:T(1024)(128)(2,1)S(1)} %dynamic-update-slice, bf16[1024]{0:T(1024)(128)(2,1)S(1)} %dynamic-update-slice.1), channel_id=1, replica_groups=mesh['blk'=16,'uly'=2] {'blk','uly'}, use_global_device_ids=true, to_apply=%add.7 | all-reduce | flops 2048 | bytes 8192
  56.0 19.8 all-gather.10.cloned.1.call-done
  79.2 75.4 %all-gather.12.cloned.1.call-done = bf16[1024,4096]{1,0:T(8,128)(2,1)} async-done(((bf16[32,4096]{1,0:T(8,128)(2,1)}), bf16[1024,4096]{1,0:T(8,128)(2,1)}) %all-gather.12.cloned.1.call-update) | async-done | bytes 8388624 | tf_op jit(solution)/shard_map/all_gather | solution.py:85
  161.1 64.6 %all-gather.14.cloned.1.call-done = bf16[1024,3072]{1,0:T(8,128)(2,1)} async-done(((bf16[32,3072]{1,0:T(8,128)(2,1)}), bf16[1024,3072]{1,0:T(8,128)(2,1)}) %all-gather.14.cloned.1.call-update) | async-done | bytes 6291472 | tf_op jit(solution)/shard_map/all_gather | solution.py:86
  231.6 13.9 all_to_all.57
  248.5 65.5 %all-gather.1 = bf16[32,1,128]{2,1,0:T(2,128)(2,1)S(1)} all-gather(bf16[1,1,128]{2,1,0:T(2,128)(2,1)S(1)} %bitcast.310), channel_id=1, replica_groups=mesh['blk'=16,'uly'=2] {'blk','uly'}, dimensions={0}, use_global_device_ids=true | all-gather | bytes 8448 | tf_op jit(solution)/shard_map/all_gather | solution.py:89
  323.3 36.4 %while.38 = (s32[]{:T(128)}, f32[2,8,128]{2,1,0:T(8,128)S(1)}, f32[2,8,128]{2,1,0:T(8,128)S(1)}, f32[2,128,8,64]{1,3,2,0:T(8,128)}, s32[2,1]{0,1:T(1,128)S(1)}, ...) while((s32[]{:T(128)}, f32[2,8,128]{2,1,0:T(8,128)S(1)}, ...), condition=%wide.region_5.6_spmd.clone, body=%wide.region_2.5_spmd.clone.sunk | while | flops 564807168 | bytes 73820936 | solution.py:186
  365.2 17.2 all-gather.16.cloned.1.call-done
  385.6 75.2 %all-gather.18.cloned.1.call-done = bf16[1024,4096]{1,0:T(8,128)(2,1)} async-done(((bf16[32,4096]{1,0:T(8,128)(2,1)}), bf16[1024,4096]{1,0:T(8,128)(2,1)}) %all-gather.18.cloned.1.call-update) | async-done | bytes 8388624 | tf_op jit(solution)/shard_map/all_gather | solution.py:88
  466.9 72.8 %all-gather.20.cloned.1.call-done = bf16[4096,1024]{1,0:T(8,128)(2,1)} async-done(((bf16[128,1024]{1,0:T(8,128)(2,1)}), bf16[4096,1024]{1,0:T(8,128)(2,1)}) %all-gather.20.cloned.1.call-update) | async-done | bytes 8388624 | tf_op jit(solution)/shard_map/all_gather | solution.py:90
  566.1 328.7 %while.39 = (s32[]{:T(128)}, bf16[2,128,2,512]{1,3,0,2:T(8,128)(2,1)}, f32[2,128,2,512]{1,3,0,2:T(8,128)S(1)}, f32[2,128,8,64]{1,3,2,0:T(8,128)}, s32[]{:T(128)}...) while((s32[]{:T(128)}, ...), condition=%wide.region_12.13_spmd.clone, body=%wide.region_11.12_spmd.clone.sunk | while | flops 171476112 | bytes 19224464 | solution.py:293
  595.7 10.2 collective-permute-done.1
  641.6 10.4 collective-permute-done.1
  687.7 10.7 collective-permute-done.1
  898.8 10.2 collective-permute-done.2
  909.1 14.6 all_to_all.58
  951.3 11.0 fusion.65
  983.3 38.6 %all-reduce.12 = (f32[1024]{0:T(1024)S(1)}, f32[4096]{0:T(1024)S(1)}, f32[1024]{0:T(1024)S(1)}) all-reduce(f32[1024]{0:T(1024)S(1)} %get-tuple-element.595, f32[4096]{0:T(1024)S(1)} %get-tuple-element.649, f32[1024]{0:T(1024)S(1)} %get-tuple-element.630), channel_id=4, replica_groups=mesh['blk'=16,'uly'=2] {'blk','uly'}, use_global_device_ids=true, to_apply=%region_18.19.clone | all-reduce | flops 6144 | bytes 49152
  1023.7 59.5 %psum.7 = f32[4096]{0:T(1024)S(1)} all-reduce(f32[4096]{0:T(1024)S(1)} %bitcast.309), channel_id=1, replica_groups=mesh['blk'=16,'uly'=2] {'blk'}, use_global_device_ids=true, to_apply=%region_15.16 | all-reduce | flops 4096 | bytes 32768 | tf_op jit(solution)/shard_map/psum | solution.py:328
  1097.2 18.0 reduce-scatter.7.cloned.1.call-done
  1115.2 163.1 %reduce-scatter.11.cloned.1.call-done = f32[32,3072]{1,0:T(8,128)} async-done(((f32[1024,3072]{1,0:T(8,128)}), f32[32,3072]{1,0:T(8,128)}) %reduce-scatter.11.cloned.1.call-update) | async-done | bytes 393232 | tf_op jit(solution)/shard_map/reduce_scatter | solution.py:336
  1278.3 359.4 %reduce-scatter.15.cloned.1.call-done = f32[32,4096]{1,0:T(8,128)} async-done(((f32[1024,4096]{1,0:T(8,128)}), f32[32,4096]{1,0:T(8,128)}) %reduce-scatter.15.cloned.1.call-update) | async-done | bytes 524304 | tf_op jit(solution)/shard_map/reduce_scatter | solution.py:338
  1637.7 361.5 %reduce-scatter.17.cloned.1.call-done = f32[128,1024]{1,0:T(8,128)} async-done(((f32[4096,1024]{1,0:T(8,128)}), f32[128,1024]{1,0:T(8,128)}) %reduce-scatter.17.cloned.1.call-update) | async-done | bytes 524304 | tf_op jit(solution)/shard_map/reduce_scatter | solution.py:340
  1999.2 361.6 %reduce-scatter.9.cloned.1.call-done = f32[32,4096]{1,0:T(8,128)} async-done(((f32[1024,4096]{1,0:T(8,128)}), f32[32,4096]{1,0:T(8,128)}) %reduce-scatter.9.cloned.1.call-update) | async-done | bytes 524304 | tf_op jit(solution)/shard_map/reduce_scatter | solution.py:335
  (478 shorter events, 476.6 us)
Async XLA Ops:
  7.2 68.7 %all-gather.10.cloned.1.call-start = ((), (), s32[]{:S(2)}) async-start(), calls=%async_computation.10 | async-start | bytes 4325376 | tf_op jit(solution)/shard_map/all_gather | solution.py:83
  7.9 146.8 %all-gather.12.cloned.1.call-start = ((), (), s32[]{:S(2)}) async-start(), calls=%async_computation.11 | async-start | bytes 8650752 | tf_op jit(solution)/shard_map/all_gather | solution.py:85
  8.7 217.0 %all-gather.14.cloned.1.call-start = ((), (), s32[]{:S(2)}) async-start(), calls=%async_computation.12 | async-start | bytes 6488064 | tf_op jit(solution)/shard_map/all_gather | solution.py:86
  9.4 313.9 %all-gather.22.cloned.1.call-start = ((), (), s32[]{:S(2)}) async-start(), calls=%async_computation.22 | async-start | bytes 8912896 | tf_op jit(solution)/shard_map/all_gather | solution.py:157
  246.5 135.9 %all-gather.16.cloned.1.call-start = ((), (), s32[]{:S(2)}) async-start(), calls=%async_computation.13 | async-start | bytes 2162688 | tf_op jit(solution)/shard_map/all_gather | solution.py:87
  247.1 213.7 %all-gather.18.cloned.1.call-start = ((), (), s32[]{:S(2)}) async-start(), calls=%async_computation.14 | async-start | bytes 8650752 | tf_op jit(solution)/shard_map/all_gather | solution.py:88
  247.7 292.0 %all-gather.20.cloned.1.call-start = ((), (), s32[]{:S(2)}) async-start(), calls=%async_computation.15 | async-start | bytes 8650752 | tf_op jit(solution)/shard_map/all_gather | solution.py:90
  361.5 20.9 all-to-all-start.1
  560.0 537.3 %reduce-scatter.13.cloned.1.call-start = ((), (), s32[]{:S(2)}) async-start(), calls=%async_computation.19 | async-start | bytes 4325376 | tf_op jit(solution)/shard_map/reduce_scatter | solution.py:337
  562.8 552.4 %reduce-scatter.7.cloned.1.call-start = ((), (), s32[]{:S(2)}) async-start(), calls=%async_computation.16 | async-start | bytes 8650752 | tf_op jit(solution)/shard_map/reduce_scatter | solution.py:333
  570.0 19.5 collective-permute-start
  593.4 18.8 collective-permute-start
  616.1 19.3 collective-permute-start
  639.3 19.2 collective-permute-start
  662.4 19.2 collective-permute-start
  685.4 19.4 collective-permute-start
  708.7 17.2 collective-permute-start
  750.9 17.2 collective-permute-start
  835.4 17.2 collective-permute-start
  877.6 17.2 collective-permute-start
  934.7 343.6 %reduce-scatter.11.cloned.1.call-start = ((), (), s32[]{:S(2)}) async-start(), calls=%async_computation.18 | async-start | bytes 12976128 | tf_op jit(solution)/shard_map/reduce_scatter | solution.py:336
  941.9 695.8 %reduce-scatter.15.cloned.1.call-start = ((), (), s32[]{:S(2)}) async-start(), calls=%async_computation.20 | async-start | bytes 17301504 | tf_op jit(solution)/shard_map/reduce_scatter | solution.py:338
  951.3 1047.9 %reduce-scatter.17.cloned.1.call-start = ((), (), s32[]{:S(2)}) async-start(), calls=%async_computation.21 | async-start | bytes 17301504 | tf_op jit(solution)/shard_map/reduce_scatter | solution.py:340
  962.3 1398.5 %reduce-scatter.9.cloned.1.call-start = ((), (), s32[]{:S(2)}) async-start(), calls=%async_computation.17 | async-start | bytes 17301504 | tf_op jit(solution)/shard_map/reduce_scatter | solution.py:335
  (61 other events, 1104.3 us)
Sparse Core Ops, SparseCore 0:
  11.0 64.7 all-gather.9
  78.8 75.8 all-gather.11
  157.6 68.0 all-gather.13
  246.6 76.6 all-gather.21
  326.1 56.2 all-gather.15
  385.2 75.5 all-gather.17
  463.8 75.8 all-gather.19
  563.6 150.0 reduce-scatter.12
  934.8 180.3 reduce-scatter.6
  1121.6 156.6 reduce-scatter.10
  1281.3 356.4 reduce-scatter.14
  1640.6 358.5 reduce-scatter.16
  2002.2 358.5 reduce-scatter.8
where the time goes:
time: 2380 us; the launch traced here: 2370 us
  waiting for transfers between devices  1830 us (77%)
  blocking collectives  234 us (10%)
  matrix products  171 us (7%)
  other arithmetic  61.4 us (3%)
  local copies, waits for them, and re-layouts  43 us (2%)
    reduce_scatter x1, waiting for transfers between devices, per_device(): lax.psum_scatter(grad_mod, ('blk', 'uly'), scatter_dimension=0, tiled=True)  362 us
    reduce_scatter x1, waiting for transfers between devices, per_device(): lax.psum_scatter(grad_down, ('blk', 'uly'), scatter_dimension=0, tiled=True)  361 us
    reduce_scatter x1, waiting for transfers between devices, per_device(): lax.psum_scatter(grad_up, ('blk', 'uly'), scatter_dimension=0, tiled=True)  359 us
    ppermute x31, waiting for transfers between devices, passed_along(): lax.ppermute(x, axis, [(i, (i + by) % devices) for i in range(devices)])  229 us
    reduce_scatter x1, waiting for transfers between devices, per_device(): lax.psum_scatter(grad_qkv, ('blk', 'uly'), scatter_dimension=0, tiled=True)  163 us
    unnamed x2, blocking collectives  80.7 us
    all_gather x1, waiting for transfers between devices, per_device(): lax.all_gather(w_mod, ('blk', 'uly'), axis=0, tiled=True)  75.4 us
    all_gather x1, waiting for transfers between devices, per_device(): lax.all_gather(w_up, ('blk', 'uly'), axis=0, tiled=True)  75.2 us
  transfers between devices with their start and end apart: 46, of which 44 were waited for; matrix products, arithmetic and copies ran while one was open for 10% of the time, Pallas kernels for 0%

commit v1 on v0

--- a/solution.py
+++ b/solution.py
@@ -1,8 +1,11 @@
+import functools
 import math
 
 import jax
 import jax.numpy as jnp
 from jax import lax
+from jax.experimental import pallas as pl
+from jax.experimental.pallas import tpu as pltpu
 from jax.sharding import PartitionSpec as P
 
 HEADS = 16
@@ -357,6 +360,1248 @@
     )
 
 
+MESH = pl.DeviceIdType.MESH
+
+
+class Place:
+    def __init__(self, depth):
+        self.depth = depth
+        self.b = lax.axis_index("blk")
+        self.x = lax.axis_index("uly")
+        self.z = self.b // 4
+        self.y = (self.b // 2) % 2
+        self.c = self.b % 2
+        self.to_x = (self.b, 1 - self.x)
+        self.to_y = (self.b + 2 - 4 * self.y, self.x)
+        self.to_core = (self.b + 1 - 2 * self.c, self.x)
+        self.to_up = (self.b + 4, self.x)
+        self.to_down = (self.b - 4, self.x)
+
+    def shard(self, z, y, c, x):
+        return ((z * 2 + y) * 2 + c) * 2 + x
+
+    def greet(self):
+        barrier = pltpu.get_barrier_semaphore()
+        for to in (self.to_x, self.to_y, self.to_core):
+            pl.semaphore_signal(barrier, inc=1, device_id=to, device_id_type=MESH)
+
+        @pl.when(self.z < self.depth - 1)
+        def _():
+            pl.semaphore_signal(barrier, inc=1, device_id=self.to_up, device_id_type=MESH)
+
+        @pl.when(self.z > 0)
+        def _():
+            pl.semaphore_signal(barrier, inc=1, device_id=self.to_down, device_id_type=MESH)
+
+        top = self.depth - 1
+        pl.semaphore_wait(barrier, 3 + (self.z + top - 1) // top + (2 * top - 1 - self.z) // top)
+
+
+def remote(src, dst, send, recv, to):
+    return pltpu.make_async_remote_copy(
+        src_ref=src, dst_ref=dst, send_sem=send, recv_sem=recv, device_id=to, device_id_type=MESH
+    )
+
+
+class Gather:
+    SENDS = 64
+    RECVS = 48
+
+    def __init__(self, place, src, dst, rows, lo, hi, split, plane_first, sends, recvs):
+        self.p, self.src, self.dst, self.rows = place, src, dst, rows
+        self.lo, self.hi, self.split, self.plane_first = lo, hi, split, plane_first
+        self.sends, self.recvs = sends, recvs
+        self.pending = []
+
+    def part(self, z, y, c, x, half=None):
+        base = self.p.shard(z, y, c, x) * self.rows
+        rows = self.rows
+        if half is not None:
+            rows = rows // 2
+            base = base + half * rows
+        return self.dst.at[pl.ds(pl.multiple_of(base, rows), rows), pl.ds(self.lo, self.hi - self.lo)]
+
+    def mine(self):
+        return self.src.at[:, pl.ds(self.lo, self.hi - self.lo)]
+
+    def go(self, when, src, dst, send, recv, to):
+        def start():
+            remote(src, dst, self.sends.at[send], self.recvs.at[recv], to).start()
+
+        def finish():
+            remote(src, dst, self.sends.at[send], self.recvs.at[recv], to).wait_send()
+
+        if when is None:
+            start()
+            self.pending.append(finish)
+        else:
+            pl.when(when)(start)
+            self.pending.append(lambda: pl.when(when)(finish))
+
+    def got(self, dst, recv):
+        remote(dst, dst, self.sends.at[0], self.recvs.at[recv], self.p.to_x).wait_recv()
+
+    def share(self, when, src, z, y, x):
+        slot = z * 4 + y * 2 + x
+        self.go(when, src, self.part(z, y, self.p.c, x), slot, slot, self.p.to_core)
+
+    def steps(self):
+        return self.plane_steps() if self.plane_first else self.line_steps()
+
+    def line_steps(self):
+        p = self.p
+        top = p.depth - 1
+
+        def hand_on(when, src, z):
+            whole = self.part(z, p.y, p.c, p.x)
+            self.go(when, src, whole, 24 + z, 20 + z, p.to_x)
+            self.go(when, src, whole, 28 + z, 24 + z, p.to_y)
+            self.share(when, src, z, p.y, p.x)
+
+        def own():
+            src = self.mine()
+            whole = self.part(p.z, p.y, p.c, p.x)
+            self.go(p.z < top, src, whole, 16 + p.z, 16 + p.z, p.to_up)
+            self.go(p.z > 0, src, whole, 20 + p.z, 16 + p.z, p.to_down)
+            hand_on(None, src, p.z)
+
+        def line(d):
+            for side in (-1, 1):
+                z = p.z + side * d
+                here = (z >= 0) & (z <= top)
+                whole = self.part(z, p.y, p.c, p.x)
+                pl.when(here)(lambda: self.got(whole, 16 + z))
+                if side < 0:
+                    self.go(here & (p.z < top), whole, whole, 16 + z, 16 + z, p.to_up)
+                else:
+                    self.go(here & (p.z > 0), whole, whole, 20 + z, 16 + z, p.to_down)
+                hand_on(here, whole, z)
+
+        def origins(d):
+            return [(None, p.z)] if d == 0 else [
+                ((p.z + s * d >= 0) & (p.z + s * d <= top), p.z + s * d) for s in (-1, 1)
+            ]
+
+        def cond(when, f):
+            f() if when is None else pl.when(when)(f)
+
+        def cross(d):
+            for when, z in origins(d):
+                from_x = self.part(z, p.y, p.c, 1 - p.x)
+                cond(when, lambda: self.got(from_x, 20 + z))
+                self.share(when, from_x, z, p.y, 1 - p.x)
+                if self.split:
+                    part = self.part(z, p.y, p.c, 1 - p.x, 0)
+                else:
+                    part = from_x
+                self.go(when, part, part, 32 + z, 28 + z, p.to_y)
+                from_y = self.part(z, 1 - p.y, p.c, p.x)
+                cond(when, lambda: self.got(from_y, 24 + z))
+                self.share(when, from_y, z, 1 - p.y, p.x)
+                if self.split:
+                    part = self.part(z, 1 - p.y, p.c, p.x, 1)
+                    self.go(when, part, part, 36 + z, 32 + z, p.to_x)
+
+        def corner(d):
+            for when, z in origins(d):
+                whole = self.part(z, 1 - p.y, p.c, 1 - p.x)
+                if self.split:
+                    for half in (0, 1):
+                        part = self.part(z, 1 - p.y, p.c, 1 - p.x, half)
+                        cond(when, lambda: self.got(part, 28 + 4 * half + z))
+                else:
+                    cond(when, lambda: self.got(whole, 28 + z))
+                self.share(when, whole, z, 1 - p.y, 1 - p.x)
+
+        out = [(0, own)]
+        for d in range(p.depth):
+            if d:
+                out.append((d, functools.partial(line, d)))
+            out.append((d + 1, functools.partial(cross, d)))
+            out.append((d + 2, functools.partial(corner, d)))
+        return out
+
+    def plane_steps(self):
+        p = self.p
+        top = p.depth - 1
+
+        def along(when, src, z, y, x, up, down):
+            slot = 20 + z * 4 + y * 2 + x
+            whole = self.part(z, y, p.c, x)
+            if up:
+                w = p.z < top
+                self.go(w if when is None else w & when, src, whole, slot, slot, p.to_up)
+            if down:
+                w = p.z > 0
+                self.go(w if when is None else w & when, src, whole, slot + 16, slot, p.to_down)
+
+        def own():
+            src = self.mine()
+            whole = self.part(p.z, p.y, p.c, p.x)
+            self.go(None, src, whole, 16, 16, p.to_x)
+            self.go(None, src, whole, 17, 17, p.to_y)
+            along(None, src, p.z, p.y, p.x, True, True)
+            self.share(None, src, p.z, p.y, p.x)
+
+        def cross():
+            from_x = self.part(p.z, p.y, p.c, 1 - p.x)
+            self.got(from_x, 16)
+            part = self.part(p.z, p.y, p.c, 1 - p.x, 0) if self.split else from_x
+            self.go(None, part, part, 18, 18, p.to_y)
+            along(None, from_x, p.z, p.y, 1 - p.x, True, True)
+            self.share(None, from_x, p.z, p.y, 1 - p.x)
+            from_y = self.part(p.z, 1 - p.y, p.c, p.x)
+            self.got(from_y, 17)
+            if self.split:
+                part = self.part(p.z, 1 - p.y, p.c, p.x, 1)
+                self.go(None, part, part, 19, 19, p.to_x)
+            along(None, from_y, p.z, 1 - p.y, p.x, True, True)
+            self.share(None, from_y, p.z, 1 - p.y, p.x)
+
+        def corner():
+            whole = self.part(p.z, 1 - p.y, p.c, 1 - p.x)
+            if self.split:
+                for half in (0, 1):
+                    self.got(self.part(p.z, 1 - p.y, p.c, 1 - p.x, half), 18 + half)
+            else:
+                self.got(whole, 18)
+            along(None, whole, p.z, 1 - p.y, 1 - p.x, True, True)
+            self.share(None, whole, p.z, 1 - p.y, 1 - p.x)
+
+        def line(d, k):
+            y = p.y if k in (0, 1) else 1 - p.y
+            x = p.x if k in (0, 2) else 1 - p.x
+            for side in (-1, 1):
+                z = p.z + side * d
+                here = (z >= 0) & (z <= top)
+                whole = self.part(z, y, p.c, x)
+                pl.when(here)(lambda: self.got(whole, 20 + z * 4 + y * 2 + x))
+                along(here, whole, z, y, x, side < 0, side > 0)
+                self.share(here, whole, z, y, x)
+
+        out = [(0, own), (1, cross), (2, corner)]
+        for d in range(1, p.depth):
+            for k in range(4):
+                out.append((d + 0.1 + min(k, 2) * 0.9, functools.partial(line, d, k)))
+        return out
+
+    def finish(self):
+        p = self.p
+        for z in range(p.depth):
+            for y in range(2):
+                for x in range(2):
+                    self.got(self.part(z, y, 1 - p.c, x), z * 4 + y * 2 + x)
+        for wait in self.pending:
+            wait()
+
+
+def gather_sems(n):
+    return [pltpu.SemaphoreType.DMA((n, Gather.SENDS)), pltpu.SemaphoreType.DMA((n, Gather.RECVS))]
+
+
+class Reduce:
+    def __init__(self, place, xt, g, turned, rows, lo, hi, line_first, out, full, outgo, income, sends, recvs):
+        self.p, self.xt, self.g, self.turned, self.rows = place, xt, g, turned, rows
+        self.lo, self.width, self.line_first, self.out = lo, hi - lo, line_first, out
+        self.full, self.outgo, self.income = full, outgo, income
+        self.sends, self.recvs = sends, recvs
+        self.chunk = math.gcd(self.width, 512)
+        self.order = [0, place.depth - 1] + list(range(1, place.depth - 1))
+        self.pending = []
+
+    @staticmethod
+    def scratch(rows, width, depth, line_first):
+        full = (4 if line_first else 3 * depth) * rows
+        outgo = (4 * depth + 3) if line_first else 4 * depth
+        income = (4 * (depth + 1) + 3) if line_first else 4 * depth + 1
+        return [
+            pltpu.VMEM((full, width), jnp.float32),
+            pltpu.VMEM((outgo * rows, width), jnp.bfloat16),
+            pltpu.VMEM((income * rows, width), jnp.bfloat16),
+            pltpu.SemaphoreType.DMA((32,)),
+            pltpu.SemaphoreType.DMA((32,)),
+        ]
+
+    def piece(self, ref, slot, half=None, count=1):
+        rows = self.rows * count
+        base = slot * self.rows
+        if half is not None:
+            rows = rows // 2
+            base = base + half * rows
+        return ref.at[pl.ds(pl.multiple_of(base, 16), rows)]
+
+    def go(self, when, src, dst, send, recv, to):
+        def start():
+            remote(src, dst, self.sends.at[send], self.recvs.at[recv], to).start()
+
+        def finish():
+            remote(src, dst, self.sends.at[send], self.recvs.at[recv], to).wait_send()
+
+        if when is None:
+            start()
+            self.pending.append(finish)
+        else:
+            pl.when(when)(start)
+            self.pending.append(lambda: pl.when(when)(finish))
+
+    def got(self, when, dst, recv):
+        def wait():
+            remote(dst, dst, self.sends.at[0], self.recvs.at[recv], self.p.to_x).wait_recv()
+
+        wait() if when is None else pl.when(when)(wait)
+
+    def columns(self, body):
+        @pl.loop(0, self.width // self.chunk)
+        def _(j):
+            start = pl.multiple_of(j * self.chunk, self.chunk)
+            body(pl.ds(start, self.chunk), pl.ds(pl.multiple_of(self.lo + start, 128), self.chunk))
+
+    def product(self, owners, cols):
+        x = jnp.concatenate(
+            [self.xt[pl.ds(pl.multiple_of(o * self.rows, self.rows), self.rows), :] for o in owners], 0
+        )
+        if self.turned:
+            return lax.dot_general(
+                x, self.g[cols, :], (((1,), (1,)), ((), ())), preferred_element_type=jnp.float32
+            )
+        return jnp.dot(x, self.g[:, cols], preferred_element_type=jnp.float32)
+
+    def steps(self):
+        return self.line_steps() if self.line_first else self.plane_steps()
+
+    def line_slots(self, count, base):
+        p, top = self.p, self.p.depth - 1
+
+        def zero(slot):
+            ref = self.piece(self.income, slot, None, count)
+            ref[...] = jnp.zeros(ref.shape, ref.dtype)
+
+        for z in range(p.depth):
+            pl.when((p.z == 0) if z == top else (p.z == 0) | (p.z == top))(
+                functools.partial(zero, base + count * z)
+            )
+        pl.when(p.z == top)(functools.partial(zero, base + count * p.depth))
+
+    def line_wait(self, z, count, base, number):
+        p, top = self.p, self.p.depth - 1
+        here = ((p.z < z) & (p.z > 0)) | ((p.z > z) & (p.z < top))
+        self.got(here, self.piece(self.income, base + count * z, None, count), number + z)
+
+    def line_go(self, z, src, count, base, number):
+        p = self.p
+        dst = self.piece(self.income, base + count * z, None, count)
+        last = self.piece(self.income, base + count * p.depth, None, count)
+        if z > 0:
+            self.go(p.z < z, src, dst, number + z, number + z, p.to_up)
+        if z < p.depth - 1:
+            self.go(p.z > z + 1, src, dst, number + z, number + z, p.to_down)
+            self.go(p.z == z + 1, src, last, number + z, number + p.depth, p.to_down)
+
+    def line_end(self, count, base, number):
+        p, top = self.p, self.p.depth - 1
+        for z in range(p.depth):
+            if z > 0:
+                self.got(p.z == z, self.piece(self.income, base + count * z, None, count), number + z)
+        self.got(p.z < top, self.piece(self.income, base + count * p.depth, None, count), number + p.depth)
+
+    def plane_steps(self):
+        p, n, r = self.p, self.p.depth, self.rows
+        sides = ((1 - p.x, 1 - p.y), (1 - p.x, p.y), (p.x, 1 - p.y), (p.x, p.y))
+
+        def owners(k):
+            x, y = sides[k]
+            return [p.shard(z, y, p.c, x) for z in range(n)]
+
+        def far():
+            self.line_slots(1, 3 * n)
+
+            def body(here, cols):
+                self.outgo[pl.ds(0, n * r), here] = self.product(owners(0), cols).astype(jnp.bfloat16)
+
+            self.columns(body)
+            for z in self.order:
+                self.go(None, self.piece(self.outgo, z, 0), self.piece(self.income, z, 0), z, z, p.to_y)
+                self.go(None, self.piece(self.outgo, z, 1), self.piece(self.income, z, 1), n + z, n + z, p.to_x)
+
+        def near():
+            def body(here, cols):
+                for k in range(3):
+                    self.full[pl.ds(k * n * r, n * r), here] = self.product(owners(k + 1), cols)
+
+            self.columns(body)
+
+        def cross(z):
+            self.got(None, self.piece(self.income, z, 0), z)
+            self.got(None, self.piece(self.income, z, 1), n + z)
+            h = r // 2
+
+            def body(here, cols):
+                for k in range(2):
+                    base = (k * n + z) * r
+                    to = ((k + 1) * n + z) * r
+                    far_half = pl.ds(z * r + k * h, h)
+                    mine = self.full[pl.ds(base + k * h, h), here]
+                    self.outgo[pl.ds(to + k * h, h), here] = (
+                        mine + self.income[far_half, here].astype(jnp.float32)
+                    ).astype(jnp.bfloat16)
+                    self.outgo[pl.ds(to + (1 - k) * h, h), here] = self.full[
+                        pl.ds(base + (1 - k) * h, h), here
+                    ].astype(jnp.bfloat16)
+
+            self.columns(body)
+            for k, to in ((1, p.to_x), (2, p.to_y)):
+                slot = k * n + z
+                self.go(None, self.piece(self.outgo, slot), self.piece(self.income, slot), (k + 1) * n + z, (k + 1) * n + z, to)
+
+        def line(z):
+            self.got(None, self.piece(self.income, n + z), 2 * n + z)
+            self.got(None, self.piece(self.income, 2 * n + z), 3 * n + z)
+            self.line_wait(z, 1, 3 * n, 4 * n)
+            away = p.z != z
+
+            def body(here, cols):
+                rows = pl.ds((2 * n + z) * r, r)
+                total = (
+                    self.full[rows, here]
+                    + self.income[pl.ds((n + z) * r, r), here].astype(jnp.float32)
+                    + self.income[pl.ds((2 * n + z) * r, r), here].astype(jnp.float32)
+                )
+                self.full[rows, here] = total
+
+            self.columns(body)
+
+            @pl.when(away)
+            def _():
+                def body(here, cols):
+                    self.outgo[pl.ds((3 * n + z) * r, r), here] = (
+                        self.full[pl.ds((2 * n + z) * r, r), here]
+                        + self.income[pl.ds((3 * n + z) * r, r), here].astype(jnp.float32)
+                    ).astype(jnp.bfloat16)
+
+                self.columns(body)
+
+            self.line_go(z, self.piece(self.outgo, 3 * n + z), 1, 3 * n, 4 * n)
+
+        def end():
+            self.line_end(1, 3 * n, 4 * n)
+            own = pl.ds(pl.multiple_of((2 * n + p.z) * r, r), r)
+            below = pl.ds(pl.multiple_of((3 * n + p.z) * r, r), r)
+            above = pl.ds(4 * n * r, r)
+
+            def body(here, cols):
+                self.out[:, cols] = (
+                    self.full[own, here]
+                    + self.income[below, here].astype(jnp.float32)
+                    + self.income[above, here].astype(jnp.float32)
+                )
+
+            self.columns(body)
+
+        steps = [(0.0, far), (0.5, near)]
+        for k, z in enumerate(self.order):
+            steps.append((1 + k, functools.partial(cross, z)))
+            steps.append((2.5 + k, functools.partial(line, z)))
+        steps.append((9.0, end))
+        return steps
+
+    def line_steps(self):
+        p, n, r = self.p, self.p.depth, self.rows
+
+        def first():
+            self.line_slots(4, 0)
+
+        def line(z):
+            places = [p.shard(z, y, p.c, x) for y in range(2) for x in range(2)]
+            self.line_wait(z, 4, 0, 0)
+
+            @pl.when(p.z != z)
+            def _():
+                def body(here, cols):
+                    self.outgo[pl.ds(4 * z * r, 4 * r), here] = (
+                        self.product(places, cols) + self.income[pl.ds(4 * z * r, 4 * r), here].astype(jnp.float32)
+                    ).astype(jnp.bfloat16)
+
+                self.columns(body)
+
+            @pl.when(p.z == z)
+            def _():
+                def body(here, cols):
+                    self.full[:, here] = self.product(places, cols)
+
+                self.columns(body)
+
+            self.line_go(z, self.piece(self.outgo, 4 * z, None, 4), 4, 0, 0)
+
+        def spot(y, x):
+            return pl.multiple_of((y * 2 + x) * r, r)
+
+        sent, come = 4 * n, 4 * (n + 1)
+
+        def meet():
+            self.line_end(4, 0, 0)
+            below = pl.ds(pl.multiple_of(4 * p.z * r, r), 4 * r)
+            above = pl.ds(4 * n * r, 4 * r)
+            far = pl.ds(spot(1 - p.y, 1 - p.x), r)
+
+            def body(here, cols):
+                self.full[:, here] = (
+                    self.full[:, here]
+                    + self.income[below, here].astype(jnp.float32)
+                    + self.income[above, here].astype(jnp.float32)
+                )
+                self.outgo[pl.ds(sent * r, r), here] = self.full[far, here].astype(jnp.bfloat16)
+
+            self.columns(body)
+            self.go(None, self.piece(self.outgo, sent, 0), self.piece(self.income, come, 0), 8, 8, p.to_y)
+            self.go(None, self.piece(self.outgo, sent, 1), self.piece(self.income, come, 1), 9, 9, p.to_x)
+
+        def cross():
+            self.got(None, self.piece(self.income, come, 0), 8)
+            self.got(None, self.piece(self.income, come, 1), 9)
+            h = r // 2
+            spots = (spot(p.y, 1 - p.x), spot(1 - p.y, p.x))
+
+            def body(here, cols):
+                for k in range(2):
+                    to = (sent + 1 + k) * r
+                    with_half = pl.ds(pl.multiple_of(spots[k] + k * h, h), h)
+                    plain = pl.ds(pl.multiple_of(spots[k] + (1 - k) * h, h), h)
+                    self.outgo[pl.ds(to + k * h, h), here] = (
+                        self.full[with_half, here] + self.income[pl.ds(come * r + k * h, h), here].astype(jnp.float32)
+                    ).astype(jnp.bfloat16)
+                    self.outgo[pl.ds(to + (1 - k) * h, h), here] = self.full[plain, here].astype(jnp.bfloat16)
+
+            self.columns(body)
+            for k, to in ((1, p.to_x), (2, p.to_y)):
+                self.go(None, self.piece(self.outgo, sent + k), self.piece(self.income, come + k), 9 + k, 9 + k, to)
+
+        def end():
+            self.got(None, self.piece(self.income, come + 1), 10)
+            self.got(None, self.piece(self.income, come + 2), 11)
+            own = pl.ds(spot(p.y, p.x), r)
+
+            def body(here, cols):
+                self.out[:, cols] = (
+                    self.full[own, here]
+                    + self.income[pl.ds((come + 1) * r, r), here].astype(jnp.float32)
+                    + self.income[pl.ds((come + 2) * r, r), here].astype(jnp.float32)
+                )
+
+            self.columns(body)
+
+        steps = [(-1.0, first)]
+        for k, z in enumerate(self.order):
+            steps.append((0.2 + k, functools.partial(line, z)))
+        steps += [(5.2, meet), (6.2, cross), (8.2, end)]
+        return steps
+
+    def finish(self):
+        for wait in self.pending:
+            wait()
+
+
+VMEM_BYTES = 58 * 2**20
+
+
+def kernel_params(number):
+    return pltpu.CompilerParams(collective_id=number, has_side_effects=True, vmem_limit_bytes=VMEM_BYTES)
+
+
+def in_vmem(count):
+    return [pl.BlockSpec(memory_space=pltpu.VMEM)] * count
+
+
+def in_any(count):
+    return [pl.BlockSpec(memory_space=pl.ANY)] * count
+
+
+def ranges(cols, cut):
+    return [(0, cut, True), (cut, cols, False)] if cut else [(0, cols, False)]
+
+
+def keep_own(p, pairs, sems):
+    copies = []
+    for k, (src, dst, rows) in enumerate(pairs):
+        at = pl.multiple_of(p.shard(p.z, p.y, p.c, p.x) * rows, rows)
+        copies.append(pltpu.make_async_copy(src, dst.at[pl.ds(at, rows)], sems.at[k]))
+    for copy in copies:
+        copy.start()
+    return copies
+
+
+class Exchange:
+    def __init__(self, place, count, src, dst, sends, recvs, own):
+        self.p, self.count, self.src, self.dst = place, count, src, dst
+        self.sends, self.recvs, self.own = sends, recvs, own
+
+    def copy(self, k):
+        to = (self.p.b + k) % self.count
+        return remote(
+            self.src.at[to], self.dst.at[self.p.b], self.sends.at[k], self.recvs.at[k], (to, self.p.x)
+        )
+
+    def mine(self):
+        return pltpu.make_async_copy(self.src.at[self.p.b], self.dst.at[self.p.b], self.own)
+
+    def start(self):
+        self.mine().start()
+        for k in range(1, self.count):
+            self.copy(k).start()
+
+    def arrived(self):
+        self.mine().wait()
+        for k in range(1, self.count):
+            came = (self.p.b + self.count - k) % self.count
+            remote(
+                self.dst.at[came], self.dst.at[came], self.sends.at[k], self.recvs.at[k], self.p.to_x
+            ).wait_recv()
+
+    def finish(self):
+        for k in range(1, self.count):
+            self.copy(k).wait_send()
+
+
+def exchange_sems(count):
+    return [
+        pltpu.SemaphoreType.DMA((count,)),
+        pltpu.SemaphoreType.DMA((count,)),
+        pltpu.SemaphoreType.DMA,
+    ]
+
+
+def greet_plane(p, count):
+    barrier = pltpu.get_barrier_semaphore()
+    for k in range(1, count):
+        pl.semaphore_signal(barrier, inc=1, device_id=((p.b + k) % count, p.x), device_id_type=MESH)
+    pl.semaphore_signal(barrier, inc=1, device_id=p.to_x, device_id_type=MESH)
+    pl.semaphore_wait(barrier, count)
+
+
+def play(events):
+    for event in events:
+        event()
+
+
+def open_kernel(depth, cuts, own_time, other_time, biases, w_mod, w_skip, w_qkv, skip_full, qkv_full, pack_full,
+                times, got_time, pack, time_sems, sends, recvs, own_sems):
+    p = Place(depth)
+    p.greet()
+    ask = remote(other_time, got_time, time_sems.at[0], time_sems.at[1], p.to_x)
+    ask.start()
+    gathers = []
+    for src, dst, rows, cols, cut in (
+        (w_skip, skip_full, w_skip.shape[0], w_skip.shape[1], cuts[0]),
+        (w_qkv, qkv_full, w_qkv.shape[0], w_qkv.shape[1], cuts[1]),
+    ):
+        for lo, hi, first in ranges(cols, cut):
+            k = len(gathers)
+            gathers.append(Gather(p, src, dst, rows, lo, hi, True, first, sends.at[k], recvs.at[k]))
+    k = len(gathers)
+    width = pack.shape[1]
+    packs = Gather(p, pack, pack_full, 8, 0, width, False, False, sends.at[k], recvs.at[k])
+
+    def products():
+        ask.wait_recv()
+        both = own_time[...] + got_time[...]
+        times[...] = both
+        left = both[:, : w_mod.shape[0]].astype(jnp.bfloat16)
+        model = w_skip.shape[1]
+        row = lax.broadcasted_iota(jnp.int32, (8, model), 0) % 4
+        total = jnp.zeros((8, model), jnp.float32)
+        for part in range(4):
+            made = jnp.dot(
+                left, w_mod[:, part * model : (part + 1) * model], preferred_element_type=jnp.float32
+            )
+            total = jnp.where(row == part, made, total)
+        pack[:, :model] = total
+        pack[:, model:] = biases[...]
+
+    events = [(t, k, f) for k, g in enumerate(gathers) for t, f in g.steps()]
+    events.append((0.3, 0, products))
+    events += [(t + 0.5, 9, f) for t, f in packs.steps()]
+    events.sort(key=lambda e: (e[0], e[1]))
+    owns = keep_own(p, ((w_skip, skip_full, w_skip.shape[0]), (w_qkv, qkv_full, w_qkv.shape[0])), own_sems)
+    play([f for _, _, f in events])
+    at = pl.multiple_of(p.shard(p.z, p.y, p.c, p.x) * 8, 8)
+    last = pltpu.make_async_copy(pack, pack_full.at[pl.ds(at, 8)], own_sems.at[2])
+    last.start()
+    for g in gathers + [packs]:
+        g.finish()
+    for copy in owns:
+        copy.wait()
+    last.wait()
+    ask.wait_send()
+
+
+def open_call(depth, devices, own_time, other_time, biases, w_mod, w_skip, w_qkv):
+    model = w_skip.shape[1]
+    cuts = (model // 4, w_qkv.shape[1] // 4)
+    width = model + 128
+    return pl.pallas_call(
+        functools.partial(open_kernel, depth, cuts),
+        name="open",
+        out_shape=[
+            jax.ShapeDtypeStruct((devices * w_skip.shape[0], model), jnp.bfloat16),
+            jax.ShapeDtypeStruct((devices * w_qkv.shape[0], w_qkv.shape[1]), jnp.bfloat16),
+            jax.ShapeDtypeStruct((devices * 8, width), jnp.float32),
+            jax.ShapeDtypeStruct((8, 128), jnp.float32),
+        ],
+        in_specs=in_vmem(4) + in_any(2),
+        out_specs=in_any(3) + in_vmem(1),
+        scratch_shapes=[
+            pltpu.VMEM((8, 128), jnp.float32),
+            pltpu.VMEM((8, width), jnp.float32),
+            pltpu.SemaphoreType.DMA((2,)),
+            *gather_sems(5),
+            pltpu.SemaphoreType.DMA((3,)),
+        ],
+        compiler_params=kernel_params(1),
+    )(own_time, other_time, biases, w_mod, w_skip, w_qkv)
+
+
+def three_terms(v):
+    a = v.astype(jnp.bfloat16).astype(jnp.float32)
+    b = (v - a).astype(jnp.bfloat16).astype(jnp.float32)
+    return a, b, v - a - b
+
+
+def extra_rows(rows, length, width):
+    shape = (length, width)
+    row = lax.broadcasted_iota(jnp.int32, shape, 0)
+    total = jnp.zeros(shape, jnp.float32)
+    for k, values in enumerate(rows):
+        total = jnp.where(row == k, values, total)
+    return total.astype(jnp.bfloat16)
+
+
+def attend(p, lengths, got, qkv, keys, mixed_out, lse, plain, block):
+    count, _, span = got.shape
+    frames = count * span
+    for k in range(count):
+        qkv[:, k * span : (k + 1) * span] = got[k]
+    length = lengths[p.x]
+    position = lax.broadcasted_iota(jnp.int32, (1, frames), 1)
+    hidden_key = jnp.where(position < length, 0.0, -1e30)
+    keys[...] = jnp.concatenate([qkv[HEAD_DIM : 2 * HEAD_DIM, :], extra_rows([hidden_key], HEAD_DIM, frames)], 0).T
+    values = jnp.concatenate([qkv[2 * HEAD_DIM :, :], extra_rows([1.0], 16, frames)], 0)
+    ones = extra_rows([1.0], HEAD_DIM, block)
+    scaling = HEAD_DIM ** (-0.5)
+    parts = block // span
+
+    @pl.loop(0, frames // block)
+    def _(j):
+        here = pl.ds(pl.multiple_of(j * block, block), block)
+        query = jnp.concatenate([qkv[:HEAD_DIM, here] * jnp.bfloat16(scaling), ones], 0)
+        score = jnp.dot(keys[...], query, preferred_element_type=jnp.float32)
+        peak = jnp.max(score, 0, keepdims=True)
+        weights = jnp.exp(score - peak).astype(jnp.bfloat16)
+        out = jnp.dot(values, weights, preferred_element_type=jnp.float32)
+        total = out[HEAD_DIM : HEAD_DIM + 1]
+        out = out[:HEAD_DIM] / total
+        plain[:, here] = out
+        lse[:, here] = peak + jnp.log(total)
+        column = lax.broadcasted_iota(jnp.int32, (HEAD_DIM, block), 1) + j * block
+        kept = jnp.where(column < length, out, 0.0).astype(jnp.bfloat16)
+        for k in range(parts):
+            mixed_out[j * parts + k] = kept[:, k * span : (k + 1) * span]
+
+
+def forward_kernel(depth, cuts, lengths, heads_in, w_out, w_up, w_down, out_full, up_full, down_full, mixed, qkv, lse,
+                   plain, got, keys, mixed_out, s1, r1, o1, s2, r2, o2, sends, recvs, own_sems):
+    p = Place(depth)
+    count = heads_in.shape[0]
+    greet_plane(p, count)
+    there = Exchange(p, count, heads_in, got, s1, r1, o1)
+    back = Exchange(p, count, mixed_out, mixed, s2, r2, o2)
+    gathers, owns = [], []
+    for src, dst, cut in ((w_out, out_full, cuts[0]), (w_up, up_full, cuts[1]), (w_down, down_full, cuts[2])):
+        for lo, hi, first in ranges(src.shape[1], cut):
+            k = len(gathers)
+            gathers.append(Gather(p, src, dst, src.shape[0], lo, hi, True, first, sends.at[k], recvs.at[k]))
+        owns.append((src, dst, src.shape[0]))
+    events = [(t, k, f) for k, g in enumerate(gathers) for t, f in g.steps()]
+
+    def attention():
+        there.arrived()
+        attend(p, lengths, got, qkv, keys, mixed_out, lse, plain, 256)
+        back.start()
+
+    there.start()
+    events.append((1.5, 0, attention))
+    events.sort(key=lambda e: (e[0], e[1]))
+    owns = keep_own(p, owns, own_sems)
+    play([f for _, _, f in events])
+    for g in gathers:
+        g.finish()
+    there.finish()
+    back.arrived()
+    back.finish()
+    for copy in owns:
+        copy.wait()
+
+
+def forward_call(depth, devices, lengths, heads_in, w_out, w_up, w_down):
+    count, depth3, span = heads_in.shape
+    frames = count * span
+    weights = (w_out, w_up, w_down)
+    cuts = tuple(w.shape[1] // 4 for w in weights)
+    return pl.pallas_call(
+        functools.partial(forward_kernel, depth, cuts),
+        name="forward",
+        out_shape=[
+            *[jax.ShapeDtypeStruct((devices * w.shape[0], w.shape[1]), jnp.bfloat16) for w in weights],
+            jax.ShapeDtypeStruct((count, HEAD_DIM, span), jnp.bfloat16),
+            jax.ShapeDtypeStruct((depth3, frames), jnp.bfloat16),
+            jax.ShapeDtypeStruct((1, frames), jnp.float32),
+            jax.ShapeDtypeStruct((HEAD_DIM, frames), jnp.float32),
+        ],
+        in_specs=[pl.BlockSpec(memory_space=pltpu.SMEM)] + in_any(4),
+        out_specs=in_any(4) + in_vmem(3),
+        scratch_shapes=[
+            pltpu.VMEM((count, depth3, span), jnp.bfloat16),
+            pltpu.VMEM((frames, 2 * HEAD_DIM), jnp.bfloat16),
+            pltpu.VMEM((count, HEAD_DIM, span), jnp.bfloat16),
+            *exchange_sems(count),
+            *exchange_sems(count),
+            *gather_sems(6),
+            pltpu.SemaphoreType.DMA((3,)),
+        ],
+        compiler_params=kernel_params(2),
+    )(lengths, heads_in, w_out, w_up, w_down)
+
+
+def attend_back(p, lengths, got, qkv, lse, plain, keys, values, key_grad, value_grad, grads_out, block):
+    count, _, span = got.shape
+    frames = count * span
+    length = lengths[p.x]
+    position = lax.broadcasted_iota(jnp.int32, (1, frames), 1)
+    hidden_key = jnp.where(position < length, 0.0, -1e30)
+    keys[...] = jnp.concatenate(
+        [qkv[HEAD_DIM : 2 * HEAD_DIM, :], extra_rows([hidden_key, 1.0, 1.0, 1.0], HEAD_DIM, frames)], 0
+    ).T
+    values[...] = jnp.concatenate(
+        [qkv[2 * HEAD_DIM :, :], extra_rows([1.0, 1.0, 1.0], HEAD_DIM, frames)], 0
+    ).T
+    key_grad[...] = jnp.zeros_like(key_grad)
+    value_grad[...] = jnp.zeros_like(value_grad)
+    scaling = HEAD_DIM ** (-0.5)
+    parts = block // span
+
+    @pl.loop(0, frames // block)
+    def _(j):
+        here = pl.ds(pl.multiple_of(j * block, block), block)
+        query = qkv[:HEAD_DIM, here] * jnp.bfloat16(scaling)
+        upstream = jnp.concatenate([got[j * parts + k] for k in range(parts)], 1)
+        delta = jnp.sum(upstream.astype(jnp.float32) * plain[:, here], 0, keepdims=True)
+        left = jnp.concatenate(
+            [query, extra_rows([1.0, *[-t for t in three_terms(lse[:, here])]], HEAD_DIM, block)], 0
+        )
+        right = jnp.concatenate([upstream, extra_rows([-t for t in three_terms(delta)], HEAD_DIM, block)], 0)
+        weights = jnp.exp(jnp.dot(keys[...], left, preferred_element_type=jnp.float32))
+        slope = jnp.dot(values[...], right, preferred_element_type=jnp.float32)
+        slope = (weights * slope).astype(jnp.bfloat16)
+        value_grad[...] += lax.dot_general(
+            weights.astype(jnp.bfloat16), upstream, (((1,), (1,)), ((), ())), preferred_element_type=jnp.float32
+        )
+        key_grad[...] += lax.dot_general(
+            slope, query, (((1,), (1,)), ((), ())), preferred_element_type=jnp.float32
+        )
+        query_grad = (
+            jnp.dot(qkv[HEAD_DIM : 2 * HEAD_DIM, :], slope, preferred_element_type=jnp.float32) * scaling
+        ).astype(jnp.bfloat16)
+        for k in range(parts):
+            grads_out[j * parts + k, :HEAD_DIM, :] = query_grad[:, k * span : (k + 1) * span]
+
+    @pl.loop(0, count)
+    def _(k):
+        rows = pl.ds(pl.multiple_of(k * span, span), span)
+        both = jnp.concatenate([key_grad[rows, :], value_grad[rows, :]], 1)
+        grads_out[k, HEAD_DIM:, :] = both.T.astype(jnp.bfloat16)
+
+
+class Shared:
+    def __init__(self, p, src, dst, axis, sems):
+        self.p, self.src, self.dst, self.axis, self.sems = p, src, dst, axis, sems
+
+    def half(self, k):
+        span = self.src.shape[self.axis]
+        if self.axis:
+            return self.dst.at[:, pl.ds(k * span, span)]
+        return self.dst.at[pl.ds(k * span, span)]
+
+    def here(self):
+        return pltpu.make_async_copy(self.src, self.half(0), self.sems.at[0])
+
+    def there(self):
+        return remote(self.src, self.half(1), self.sems.at[1], self.sems.at[2], self.p.to_core)
+
+    def start(self):
+        self.here().start()
+        self.there().start()
+
+    def arrived(self):
+        self.here().wait()
+        self.there().wait_recv()
+
+    def finish(self):
+        self.there().wait_send()
+
+
+def sum_specs(p_depth, shards):
+    scratch = []
+    for rows, cols, cut in shards:
+        for lo, hi, first in ranges(cols, cut):
+            scratch += Reduce.scratch(rows, hi - lo, p_depth, first)
+    return scratch
+
+
+def backward_kernel(depth, cuts, lengths, mixed_grad, qkv, lse, plain, pack, act, cot, normed2, inner_grad, mixed,
+                    branch_grad, got_grads, down_grad, up_grad, out_grad, pack_full, got, keys, values, key_grad,
+                    value_grad, grads_out, x0, g0, x1, g1, x2, g2, share_sems, s1, r1, o1, s2, r2, o2, sends, recvs,
+                    own_sems, *rest):
+    p = Place(depth)
+    count = mixed_grad.shape[0]
+    greet_plane(p, count)
+    there = Exchange(p, count, mixed_grad, got, s1, r1, o1)
+    back = Exchange(p, count, grads_out, got_grads, s2, r2, o2)
+    there.start()
+    shared = []
+    for k, (src, dst, axis) in enumerate(
+        ((act, x0, 1), (cot, g0, 0), (normed2, x1, 1), (inner_grad, g1, 1), (mixed, x2, 1), (branch_grad, g2, 0))
+    ):
+        shared.append(Shared(p, src, dst, axis, share_sems.at[k]))
+        shared[-1].start()
+    packs = Gather(p, pack, pack_full, 8, 0, pack.shape[1], False, False, sends.at[0], recvs.at[0])
+    sums = []
+    rest = list(rest)
+    for x, g, turned, out, cut in (
+        (x0, g0, False, down_grad, cuts[0]),
+        (x1, g1, True, up_grad, cuts[1]),
+        (x2, g2, False, out_grad, cuts[2]),
+    ):
+        for lo, hi, first in ranges(out.shape[1], cut):
+            sums.append(Reduce(p, x, g, turned, out.shape[0], lo, hi, first, out, *rest[:5]))
+            rest = rest[5:]
+
+    def attention():
+        there.arrived()
+        attend_back(p, lengths, got, qkv, lse, plain, keys, values, key_grad, value_grad, grads_out, 256)
+        back.start()
+
+    at = pl.multiple_of(p.shard(p.z, p.y, p.c, p.x) * 8, 8)
+    own = pltpu.make_async_copy(pack, pack_full.at[pl.ds(at, 8)], own_sems.at[0])
+    own.start()
+    for s in shared:
+        s.arrived()
+    events = [(t, k, f) for k, g in enumerate(sums) for t, f in g.steps()]
+    events += [(t + 0.6, 9, f) for t, f in packs.steps()]
+    events.append((0.7, 0, attention))
+    events.sort(key=lambda e: (e[0], e[1]))
+    play([f for _, _, f in events])
+    for g in sums + [packs] + shared:
+        g.finish()
+    there.finish()
+    back.arrived()
+    back.finish()
+    own.wait()
+
+
+def backward_call(depth, devices, lengths, mixed_grad, qkv, lse, plain, pack, act, cot, normed2, inner_grad, mixed,
+                  branch_grad):
+    count, _, span = mixed_grad.shape
+    frames = count * span
+    model, ff = cot.shape[1], act.shape[0]
+    shards = [
+        (ff // devices, model, model // 4),
+        (model // devices, ff, ff // 4),
+        (model // devices, model, model // 4),
+    ]
+    pair = 2 * span
+    return pl.pallas_call(
+        functools.partial(backward_kernel, depth, tuple(s[2] for s in shards)),
+        name="backward",
+        out_shape=[
+            jax.ShapeDtypeStruct((count, 3 * HEAD_DIM, span), jnp.bfloat16),
+            *[jax.ShapeDtypeStruct(s[:2], jnp.float32) for s in shards],
+            jax.ShapeDtypeStruct((devices * 8, pack.shape[1]), jnp.float32),
+        ],
+        in_specs=[pl.BlockSpec(memory_space=pltpu.SMEM)] + in_any(1) + in_vmem(4) + in_any(6),
+        out_specs=in_any(1) + in_vmem(3) + in_any(1),
+        scratch_shapes=[
+            pltpu.VMEM((count, HEAD_DIM, span), jnp.bfloat16),
+            pltpu.VMEM((frames, 2 * HEAD_DIM), jnp.bfloat16),
+            pltpu.VMEM((frames, 2 * HEAD_DIM), jnp.bfloat16),
+            pltpu.VMEM((frames, HEAD_DIM), jnp.float32),
+            pltpu.VMEM((frames, HEAD_DIM), jnp.float32),
+            pltpu.VMEM((count, 3 * HEAD_DIM, span), jnp.bfloat16),
+            pltpu.VMEM((ff, pair), jnp.bfloat16),
+            pltpu.VMEM((pair, model), jnp.bfloat16),
+            pltpu.VMEM((model, pair), jnp.bfloat16),
+            pltpu.VMEM((ff, pair), jnp.bfloat16),
+            pltpu.VMEM((model, pair), jnp.bfloat16),
+            pltpu.VMEM((pair, model), jnp.bfloat16),
+            pltpu.SemaphoreType.DMA((6, 3)),
+            *exchange_sems(count),
+            *exchange_sems(count),
+            *gather_sems(1),
+            pltpu.SemaphoreType.DMA((1,)),
+            *sum_specs(depth, shards),
+        ],
+        compiler_params=kernel_params(3),
+    )(lengths, mixed_grad, qkv, lse, plain, pack, act, cot, normed2, inner_grad, mixed, branch_grad)
+
+
+def close_kernel(depth, cuts, pack, late, w_mod, normed, grad, joined, base_grad, qkv_grad, skip_grad, sums_out,
+                 times_full, pack_full, times, x0, g0, x1, g1, share_sems, sends, recvs, own_sems, *rest):
+    p = Place(depth)
+    p.greet()
+    shared = []
+    for k, (src, dst, axis) in enumerate(((normed, x0, 1), (grad, g0, 1), (joined, x1, 1), (base_grad, g1, 0))):
+        shared.append(Shared(p, src, dst, axis, share_sems.at[k]))
+        shared[-1].start()
+    packs = Gather(p, pack, pack_full, 8, 0, pack.shape[1], False, False, sends.at[0], recvs.at[0])
+    spread = Gather(p, times, times_full, 8, 0, 128, False, False, sends.at[1], recvs.at[1])
+    sums = []
+    rest = list(rest)
+    for x, g, turned, out, cut in ((x0, g0, True, qkv_grad, cuts[0]), (x1, g1, False, skip_grad, cuts[1])):
+        for lo, hi, first in ranges(out.shape[1], cut):
+            sums.append(Reduce(p, x, g, turned, out.shape[0], lo, hi, first, out, *rest[:5]))
+            rest = rest[5:]
+    at = pl.multiple_of(p.shard(p.z, p.y, p.c, p.x) * 8, 8)
+    own = pltpu.make_async_copy(pack, pack_full.at[pl.ds(at, 8)], own_sems.at[0])
+    own.start()
+    model = pack.shape[1]
+
+    def modulations():
+        own.wait()
+        packs.finish()
+        rows = [jnp.zeros((8, model), jnp.float32) for _ in range(2)]
+        for k in range(pack_full.shape[0] // 8):
+            rows[k % 2] = rows[k % 2] + pack_full[pl.ds(k * 8, 8), :]
+        sums_out[0:8, :] = rows[0]
+        sums_out[8:16, :] = rows[1]
+        total = jnp.zeros((8, w_mod.shape[0]), jnp.float32)
+        for part in range(4):
+            values = []
+            for r in range(2):
+                if part < 2:
+                    values.append(rows[r][part : part + 1])
+                else:
+                    values.append(late[2 * r + part - 2 : 2 * r + part - 1, :])
+            terms = [*three_terms(values[0]), *three_terms(values[1])]
+            left = extra_rows(terms, 8, model)
+            total = total + lax.dot_general(
+                left,
+                w_mod[:, part * model : (part + 1) * model],
+                (((1,), (1,)), ((), ())),
+                preferred_element_type=jnp.float32,
+            )
+        first = total[0:1] + total[1:2] + total[2:3]
+        second = total[3:4] + total[4:5] + total[5:6]
+        made = jnp.concatenate([first, second, jnp.zeros((6, w_mod.shape[0]), jnp.float32)], 0)
+        times[...] = jnp.concatenate([made, jnp.zeros((8, 128 - w_mod.shape[0]), jnp.float32)], 1)
+
+    play([f for t, f in sorted(packs.steps(), key=lambda e: e[0])[:1]])
+    for s in shared:
+        s.arrived()
+    events = [(t, k, f) for k, g in enumerate(sums) for t, f in g.steps()]
+    events += [(t + 0.6, 9, f) for t, f in sorted(packs.steps(), key=lambda e: e[0])[1:]]
+    events.append((6.8, 9, modulations))
+    events += [(t + 6.9, 9, f) for t, f in spread.steps()]
+    events.sort(key=lambda e: (e[0], e[1]))
+    play([f for _, _, f in events])
+    last = pltpu.make_async_copy(times, times_full.at[pl.ds(at, 8)], own_sems.at[1])
+    last.start()
+    for g in sums + [spread] + shared:
+        g.finish()
+    last.wait()
+
+
+def close_call(depth, devices, pack, late, w_mod, normed, grad, joined, base_grad):
+    model, span = normed.shape
+    pair = 2 * span
+    shards = [
+        (model // devices, grad.shape[0], grad.shape[0] // 4),
+        (joined.shape[0] // devices, model, model // 4),
+    ]
+    return pl.pallas_call(
+        functools.partial(close_kernel, depth, tuple(s[2] for s in shards)),
+        name="close",
+        out_shape=[
+            *[jax.ShapeDtypeStruct(s[:2], jnp.float32) for s in shards],
+            jax.ShapeDtypeStruct((16, model), jnp.float32),
+            jax.ShapeDtypeStruct((devices * 8, 128), jnp.float32),
+        ],
+        in_specs=in_vmem(3) + in_any(4),
+        out_specs=in_vmem(3) + in_any(1),
+        scratch_shapes=[
+            pltpu.VMEM((devices * 8, model), jnp.float32),
+            pltpu.VMEM((8, 128), jnp.float32),
+            pltpu.VMEM((model, pair), jnp.bfloat16),
+            pltpu.VMEM((grad.shape[0], pair), jnp.bfloat16),
+            pltpu.VMEM((joined.shape[0], pair), jnp.bfloat16),
+            pltpu.VMEM((pair, model), jnp.bfloat16),
+            pltpu.SemaphoreType.DMA((4, 3)),
+            *gather_sems(2),
+            pltpu.SemaphoreType.DMA((2,)),
+            *sum_specs(depth, shards),
+        ],
+        compiler_params=kernel_params(4),
+    )(pack, late, w_mod, normed, grad, joined, base_grad)
+
+
+def first_with_second(left, right, dims):
+    return lax.dot_general(left, right, ((dims[:1], dims[1:]), ((), ())), preferred_element_type=jnp.float32)
+
+
+def turn(values, cosine, sine):
+    half = HEAD_DIM // 2
+    first, second = values[..., :half, :], values[..., half:, :]
+    return jnp.concatenate([first * cosine - second * sine, second * cosine + first * sine], -2)
+
+
+def on_device(hidden, skip_in, time_embed, lengths, cotangent, w_skip, b_skip, w_mod, w_qkv, w_out, w_up, b_up,
+              w_down, b_down):
+    block, row = lax.axis_index("blk"), lax.axis_index("uly")
+    blocks, rows = lax.axis_size("blk"), lax.axis_size("uly")
+    devices, depth = blocks * rows, blocks // 4
+    _, frames, model = hidden.shape
+    position = block * frames + jnp.arange(frames, dtype=jnp.int32)
+    length = lax.dynamic_index_in_dim(lengths, row, 0, keepdims=False)[0]
+    valid = position < length
+    kept = valid.astype(jnp.float32)
+
+    number = block * rows + row
+    share = w_mod.shape[0]
+    time_row = time_embed[0, 0].astype(jnp.float32)
+    mark = (jnp.arange(8) // 4 == row)[:, None]
+
+    def time_part(index):
+        part = lax.dynamic_slice_in_dim(time_row, index * share, share)
+        return jnp.where(mark, jnp.pad(part, (0, 128 - share))[None], 0.0)
+
+    tile = jnp.concatenate(
+        [
+            b_up.astype(jnp.float32)[None],
+            jnp.pad(
+                jnp.concatenate([b_skip, b_down]).astype(jnp.float32), (0, 128 - 2 * b_skip.shape[0])
+            )[None],
+            jnp.zeros((6, 128), jnp.float32),
+        ]
+    )
+    skip_full, qkv_full, pack, times = open_call(
+        depth, devices, time_part(number), time_part(block * rows + 1 - row), tile, w_mod, w_skip, w_qkv
+    )
+    pack = pack.reshape(devices, 8, model + 128)
+    mods = lax.dynamic_slice_in_dim(jnp.sum(pack[:, :, :model], 0), row * 4, 4, 0)
+    bup_full = pack[:, 0, model:].reshape(-1)
+    each = b_skip.shape[0]
+    bskip_full = pack[:, 1, model : model + each].reshape(-1)
+    bdown_full = pack[:, 1, model + each : model + 2 * each].reshape(-1)
+
+    joined = jnp.concatenate([hidden[0], skip_in[0]], 1)
+    base = jnp.dot(joined, skip_full, preferred_element_type=jnp.float32) + bskip_full
+    a_scale, a_shift, f_scale, f_shift = [kept[:, None] * mods[k][None] for k in range(4)]
+    normed_full, norm_back = jax.vjp(modulate, base, a_scale, a_shift)
+    normed = normed_full.astype(jnp.bfloat16)
+    projected = first_with_second(qkv_full, normed, (0, 1)).reshape(3, HEADS, HEAD_DIM, frames)
+    half = HEAD_DIM // 2
+    freq = 10000.0 ** (-jnp.arange(half, dtype=jnp.float32) / half)
+    offsets = jnp.where(valid, position, position - length).astype(jnp.float32)
+    angle = freq[:, None] * offsets[None, :]
+    cosine, sine = jnp.cos(angle), jnp.sin(angle)
+    heads = jnp.concatenate(
+        [turn(projected[0], cosine, sine), turn(projected[1], cosine, sine), projected[2]], 1
+    ).astype(jnp.bfloat16)
+    out_full, up_full, down_full, mixed, qkv, lse, plain = forward_call(
+        depth, devices, lengths[:, 0], heads, w_out, w_up, w_down
+    )
+    mixed = mixed.reshape(model, frames)
+    branch = first_with_second(mixed, out_full, (0, 0))
+    middle = base + branch
+    normed2_full, norm2_back = jax.vjp(modulate, middle, f_scale, f_shift)
+    normed2 = normed2_full.astype(jnp.bfloat16)
+    inner = first_with_second(up_full, normed2, (0, 1)) + bup_full[:, None]
+    act_full, act_back = jax.vjp(gelu_exact, inner)
+    act = act_full.astype(jnp.bfloat16)
+    output = (middle + first_with_second(act, down_full, (0, 0)) + bdown_full).astype(jnp.bfloat16)[None]
+
+    upstream = cotangent[0]
+    upstream_full = upstream.astype(jnp.float32)
+    grad_inner = act_back(first_with_second(down_full, upstream, (1, 1)))[0].astype(jnp.bfloat16)
+    grad_normed2 = first_with_second(grad_inner, up_full, (0, 1))
+    grad_mid_norm, grad_fscale, grad_fshift = norm2_back(grad_normed2)
+    grad_middle = upstream_full + grad_mid_norm
+    grad_branch = grad_middle.astype(jnp.bfloat16)
+    grad_mixed = first_with_second(out_full, grad_branch, (1, 1)).astype(jnp.bfloat16)
+    grad_mixed = grad_mixed * valid.astype(jnp.bfloat16)[None]
+    early = jnp.concatenate(
+        [
+            jnp.sum(grad_fscale * kept[:, None], 0),
+            jnp.sum(grad_fshift * kept[:, None], 0),
+            jnp.sum(grad_inner.astype(jnp.float32), 1),
+            jnp.sum(upstream_full, 0),
+            jnp.zeros((model,), jnp.float32),
+        ]
+    ).reshape(8, model)
+    head_grads, grad_down, grad_up, grad_out, early_full = backward_call(
+        depth, devices, lengths[:, 0], grad_mixed.reshape(HEADS, HEAD_DIM, frames), qkv, lse, plain, early, act,
+        upstream, normed2.T, grad_inner, mixed, grad_branch,
+    )
+    early_full = early_full.reshape(blocks, rows, 8, model)
+    early_row = jnp.sum(early_full[:, :, :2], 0)
+    early_bias = jnp.sum(early_full[:, :, 2:], (0, 1))
+    head_grads = head_grads.astype(jnp.float32)
+    grad_projected = jnp.stack(
+        [
+            turn(head_grads[:, :HEAD_DIM], cosine, -sine),
+            turn(head_grads[:, HEAD_DIM : 2 * HEAD_DIM], cosine, -sine),
+            head_grads[:, 2 * HEAD_DIM :],
+        ]
+    ).astype(jnp.bfloat16).reshape(3 * model, frames)
+    grad_normed = first_with_second(grad_projected, qkv_full, (0, 1))
+    grad_base_norm, grad_ascale, grad_ashift = norm_back(grad_normed)
+    grad_base = (grad_middle + grad_base_norm).astype(jnp.bfloat16)
+    grad_joined = first_with_second(grad_base, skip_full, (1, 1)).astype(jnp.bfloat16)
+    late = jnp.concatenate(
+        [
+            jnp.sum(grad_ascale * kept[:, None], 0),
+            jnp.sum(grad_ashift * kept[:, None], 0),
+            jnp.sum(grad_base.astype(jnp.float32), 0),
+            jnp.zeros((5 * model,), jnp.float32),
+        ]
+    ).reshape(8, model)
+    early_mods = jnp.pad(early_row.reshape(2 * rows, model), ((0, 8 - 2 * rows), (0, 0)))
+    grad_qkv, grad_skip, late_sums, time_parts = close_call(
+        depth, devices, late, early_mods, w_mod, normed.T, grad_projected, joined.T, grad_base
+    )
+    late_sums = late_sums.reshape(2, 8, model)
+    mod_grads = jnp.concatenate([late_sums[:, :2], early_row], 1).reshape(rows, 4 * model)
+    own_times = times[::4, :share]
+    grad_mod = jnp.sum(own_times[:, :, None] * mod_grads[:, None, :], 0)
+    time_parts = time_parts.reshape(devices, 8, 128)[:, :, :share]
+    time_grad = lax.dynamic_index_in_dim(time_parts, row, 1, keepdims=False).reshape(1, 1, model)
+    grad_bskip = lax.dynamic_slice_in_dim(late_sums[0, 2] + late_sums[1, 2], number * each, each)
+    ups = b_up.shape[0]
+    grad_bup = lax.dynamic_slice_in_dim(early_bias[:4].reshape(-1), number * ups, ups)
+    grad_bdown = lax.dynamic_slice_in_dim(early_bias[4], number * each, each)
+    return (
+        output,
+        grad_joined[:, :model][None],
+        grad_joined[:, model:][None],
+        time_grad,
+        grad_skip,
+        grad_bskip,
+        grad_mod,
+        grad_qkv,
+        grad_out,
+        grad_up,
+        grad_bup,
+        grad_down,
+        grad_bdown,
+    )
+
+
 def solution(mesh):
     placed = (
         P("uly", "blk", None),
@@ -374,8 +1619,10 @@
         P(("blk", "uly"), None),
         P(("blk", "uly")),
     )
+    blocks = mesh.shape["blk"]
+    special = mesh.shape["uly"] == 2 and blocks == HEADS and blocks % 4 == 0 and blocks > 4
     return jax.shard_map(
-        per_device,
+        on_device if special else per_device,
         mesh=mesh,
         in_specs=placed,
         out_specs=(

time: 2380 us -> 466 us (0.20)
  waiting for transfers between devices: 1830 us -> 0 us
  Pallas kernels: 0 us -> 379 us
  blocking collectives: 234 us -> 0 us
  matrix products: 171 us -> 45.2 us
  other arithmetic: 61.4 us -> 10.5 us
    reduce_scatter x6 -> x0, waiting for transfers between devices: 1260 us -> none  [the longest x1 362 us: per_device(): lax.psum_scatter(grad_mod, ('blk', 'uly'), scatter_dimension=0, tiled=True)]
    pallas_call x0 -> x4, Pallas kernels: none -> 379 us  [the longest x1 118 us: backward_call(): pl.pallas_call(functools.partial(backward_kernel, depth, tuple((s[2] for...]
    all_gather x7 -> x0, waiting for transfers between devices: 333 us -> none  [the longest x1 75.4 us: per_device(): lax.all_gather(w_mod, ('blk', 'uly'), axis=0, tiled=True)]
    ppermute x31 -> x0, waiting for transfers between devices: 229 us -> none  [passed_along(): lax.ppermute(x, axis, [(i, (i + by) % devices) for i in range(devices)])]
    dot_general x102 -> x10, matrix products: 171 us -> 45.2 us  [the longest x9 42.1 us: first_with_second(): lax.dot_general(left, right, ((dims[:1], dims[1:]), ((), ())), preferred_...]
    unnamed x2 -> x0, blocking collectives: 80.7 us -> none
    all_gather x1 -> x0, blocking collectives: 65.5 us -> none  [per_device(): lax.all_gather(b_up, ('blk', 'uly'), axis=0, tiled=True)]
    psum x1 -> x0, blocking collectives: 59.5 us -> none  [per_device(): slot_total = lax.psum(slot_grad, 'blk')]
  transfers between devices with their start and end apart: 46 -> 0, of which waited for: 44 -> 0; matrix products, arithmetic and copies ran while one was open for 10% -> 0% of each run, Pallas kernels for 0% -> 0%
where the time goes in v1:
time: 466 us; the launch traced here: 458 us
  Pallas kernels  379 us (81%)
  matrix products  45.2 us (10%)
  local copies, waits for them, and re-layouts  22 us (5%)
  other arithmetic  10.5 us (2%)
    pallas_call x1, Pallas kernels, backward_call(): pl.pallas_call(functools.partial(backward_kernel, depth, tuple((s[2] for...  118 us
    pallas_call x1, Pallas kernels, close_call(): pl.pallas_call(functools.partial(close_kernel, depth, tuple((s[2] for s i...  105 us
    pallas_call x1, Pallas kernels, forward_call(): pl.pallas_call(functools.partial(forward_kernel, depth, cuts), name='forw...  98.1 us
    pallas_call x1, Pallas kernels, open_call(): pl.pallas_call(functools.partial(open_kernel, depth, cuts), name='open',...  57 us
    dot_general x9, matrix products, first_with_second(): lax.dot_general(left, right, ((dims[:1], dims[1:]), ((), ())), preferred_...  42.1 us

profile of v1, /device:TPU:0, one launch (start us, length us, event | category | flops | bytes accessed | tf_op | source)
XLA Modules:
  0.0 457.7 jit_solution(2134005341582004544)
XLA Ops:
  3.6 57.0 %open.1 = (bf16[2048,1024]{1,0:T(8,128)(2,1)}, bf16[1024,3072]{1,0:T(8,128)(2,1)}, f32[256,1152]{1,0:T(8,128)}, f32[8,128]{1,0:T(8,128)}) custom-call(f32[8,128]{1,0:T(8,128)} %get-tuple-element.91.own_time, f32[8,128]{1,0:T(8,128)} %get-tuple-element.90.other_time, f32[8,128]{1,0:T(8,128)} %maximum_maximum_fusion.biases, bf16[32,4096]{1,0:T(8,128)(2,1)} %w_mod.3, ...), custom_call_target="tpu_custom_call" | custom-call | tf_op jit(solution)/shard_map/open/pallas_call | solution.py:1040
  60.7 1.1 slice_reduce_fusion.3
  61.8 1.1 copy.35
  63.0 1.1 copy.34
  64.1 3.1 fusion.57
  68.8 4.8 %fusion.18 = f32[3072,128]{1,0:T(8,128)S(1)} fusion(bf16[1024,3072]{1,0:T(8,128)(2,1)} %get-tuple-element.35, f32[128,1024]{1,0:T(8,128)S(1)} %get-tuple-element.93, f32[1024]{0:T(1024)S(1)} %bitcast.126, f32[1024]{0:T(1024)S(1)} %bitcast.118, f32[128]{0:T(128)S(1)} %get-tuple-element.105, f32[128]{0:T(128)S(1)} %fusion.44, f32[128]{0:T(128)S(1)} %broadcast_multiply_fusion.1), kind=kOutput, calls=%fused_computation.62 | convolution fusion | flops 806354944 | bytes 8398336 | tf_op jit(solution)/shard_map/dot_general | solution.py:1454
  74.8 0.9 copy-done.10
  75.7 98.1 %forward.1 = (bf16[1024,1024]{1,0:T(8,128)(2,1)}, bf16[1024,4096]{1,0:T(8,128)(2,1)}, bf16[4096,1024]{1,0:T(8,128)(2,1)}, bf16[16,64,128]{2,1,0:T(8,128)(2,1)}, ...) custom-call(s32[2]{0:T(128)} %bitcast.134, bf16[16,192,128]{2,1,0:T(8,128)(2,1)} %copy-done.10, ...), custom_call_target="tpu_custom_call" | custom-call | tf_op jit(solution)/shard_map/forward/pallas_call | solution.py:1148
  173.8 2.2 fusion.58
  176.3 10.9 %multiply_convert_fusion = (bf16[4096,128]{1,0:T(8,128)(2,1)S(1)}, f32[4096,128]{1,0:T(8,128)}) fusion(f32[4096]{0:T(1024)S(1)} %bitcast.131, bf16[1024,4096]{1,0:T(8,128)(2,1)} %get-tuple-element.38, f32[128,1024]{1,0:T(8,128)S(1)} %get-tuple-element.95, f32[1024]{0:T(1024)S(1)} %bitcast.128, f32[1024]{0:T(1024)S(1)} %bitcast.122, f32[128]{0:T(128)S(1)} %fusion.45, ...), kind=kOutput, calls=%fused_computation.6 | convolution fusion | flops 1109393408 | bytes 12084736 | tf_op jit(solution)/shard_map/dot_general | solution.py:1454
  187.2 5.7 %fusion.9 = bf16[1,128,1024]{2,1,0:T(8,128)(2,1)} fusion(f32[128,1024]{1,0:T(8,128)S(1)} %get-tuple-element.95, bf16[4096,128]{1,0:T(8,128)(2,1)S(1)} %get-tuple-element.96.act, bf16[4096,1024]{1,0:T(8,128)(2,1)} %get-tuple-element.39, f32[1024]{0:T(1024)S(1)} %add.189), kind=kOutput, calls=%fused_computation.27 | convolution fusion | flops 1074135040 | bytes 10227712 | tf_op jit(solution)/shard_map/dot_general | solution.py:1454
  194.1 7.0 %convert_reduce_fusion = (f32[4096]{0:T(1024)S(1)}, bf16[4096,128]{1,0:T(8,128)(2,1)S(1)}) fusion(f32[4096,128]{1,0:T(8,128)S(1)} %copy-done.19, bf16[4096,1024]{1,0:T(8,128)(2,1)S(1)} %copy-done, bf16[1,128,1024]{2,1,0:T(8,128)(2,1)S(1)} %copy-done.6), kind=kOutput, calls=%fused_computation.4 | convolution fusion | flops 1112535040 | bytes 11812864 | tf_op jit(solution)/shard_map/dot_general | solution.py:1454
  201.1 3.1 multiply_reduce_fusion.5
  204.8 1.2 copy-done.8
  205.9 1.4 fusion.8
  209.2 118.1 %backward.1 = (bf16[16,192,128]{2,1,0:T(8,128)(2,1)}, f32[128,1024]{1,0:T(8,128)}, f32[32,4096]{1,0:T(8,128)}, f32[32,1024]{1,0:T(8,128)}, f32[256,1024]{1,0:T(8,128)}) custom-call(s32[2]{0:T(128)} %bitcast.135, bf16[16,64,128]{2,1,0:T(8,128)(2,1)} %bitcast.116, bf16[192,2048]{1,0:T(8,128)(2,1)} %get-tuple-element.40.qkv, f32[1,2048]{1,0:T(1,128)} %get-tuple-element.41.lse, ...), custom_call_target="tpu_custom_call" | custom-call | tf_op jit(solution)/shard_map/backward/pallas_call | solution.py:1320
  327.3 1.0 slice_bitcast_fusion.2
  328.3 1.3 convert_element_type.99
  329.9 5.5 %multiply_reduce_fusion.2 = (f32[1024]{0:T(1024)S(1)}, f32[128]{0:T(128)S(1)}, f32[1024]{0:T(1024)S(1)}, f32[128,1024]{1,0:T(8,128)S(1)}) fusion(f32[128,1024]{1,0:T(8,128)S(1)} %get-tuple-element.93, f32[128]{0:T(128)S(1)} %get-tuple-element.105, f32[128]{0:T(128)S(1)} %fusion.44, f32[128]{0:T(128)S(1)} %broadcast_multiply_fusion.1, ...), kind=kOutput, calls=%fused_computation.46 | convolution fusion | flops 806877056 | bytes 8140800 | tf_op jit(solution)/shard_map/dot_general | solution.py:1454
  336.0 1.5 convolution_convert_fusion
  341.4 105.3 %close.1 = (f32[32,3072]{1,0:T(8,128)}, f32[64,1024]{1,0:T(8,128)}, f32[16,1024]{1,0:T(8,128)}, f32[256,128]{1,0:T(8,128)}) custom-call(f32[8,1024]{1,0:T(8,128)} %reshape.255.pack, f32[8,1024]{1,0:T(8,128)} %pad.19.late, bf16[32,4096]{1,0:T(8,128)(2,1)} %w_mod.3, bf16[1024,128]{1,0:T(8,128)(2,1)} %copy.40.normed, bf16[3072,128]{1,0:T(8,128)(2,1)} %bitcast.98, ...), custom_call_target="tpu_custom_call" | custom-call | tf_op jit(solution)/shard_map/close/pallas_call | solution.py:1427
  446.8 1.1 dynamic-slice_reduce_fusion
  449.9 0.8 slice.156
  451.5 1.0 multiply_reduce_fusion
  (122 shorter events, 22.0 us)
Async XLA Ops:
  64.1 3.1 copy-start.12
  64.1 3.2 copy-start.18
  74.8 0.9 copy-start.10
  187.2 5.8 %copy-start.2 = (bf16[4096,128]{1,0:T(8,128)(2,1)}, bf16[4096,128]{1,0:T(8,128)(2,1)S(1)}, u32[]{:S(2)}) copy-start(bf16[4096,128]{1,0:T(8,128)(2,1)S(1)} %get-tuple-element.96.act) | copy-start | bytes 3145732
  187.2 6.2 %copy-start = (bf16[4096,1024]{1,0:T(8,128)(2,1)S(1)}, bf16[4096,1024]{1,0:T(8,128)(2,1)}, u32[]{:S(2)}) copy-start(bf16[4096,1024]{1,0:T(8,128)(2,1)} %get-tuple-element.39) | copy-start | bytes 25165828
  187.2 6.2 %copy-start.6 = (bf16[1,128,1024]{2,1,0:T(8,128)(2,1)S(1)}, bf16[1,128,1024]{2,1,0:T(8,128)(2,1)}, u32[]{:S(2)}) copy-start(bf16[1,128,1024]{2,1,0:T(8,128)(2,1)} %param.18) | copy-start | bytes 786436
  187.2 6.8 %copy-start.19 = (f32[4096,128]{1,0:T(8,128)S(1)}, f32[4096,128]{1,0:T(8,128)}, u32[]{:S(2)}) copy-start(f32[4096,128]{1,0:T(8,128)} %get-tuple-element.97) | copy-start | bytes 6291460
  187.2 13.8 %slice-start = ((s8[8388608]{0:T(1024)(128)(4,1)}), s8[4194304]{0:T(1024)(128)(4,1)S(1)}, s32[]{:S(2)}) async-start(s8[8388608]{0:T(1024)(128)(4,1)} %bitcast.95), calls=%async_computation | async-start | bytes 8388608
  194.1 7.0 %slice-start.1 = ((s8[8388608]{0:T(1024)(128)(4,1)}), s8[4194304]{0:T(1024)(128)(4,1)S(1)}, s32[]{:S(2)}) async-start(s8[8388608]{0:T(1024)(128)(4,1)} %bitcast.95), calls=%async_computation.1 | async-start | bytes 8388608
  201.1 3.2 copy-start.4
  204.2 1.7 copy-start.8
  204.7 3.6 copy-start.11
  329.9 5.5 %copy-start.3 = (bf16[3,16,64,128]{3,2,1,0:T(8,128)(2,1)}, bf16[3,16,64,128]{3,2,1,0:T(8,128)(2,1)S(1)}, u32[]{:S(2)}) copy-start(bf16[3,16,64,128]{3,2,1,0:T(8,128)(2,1)S(1)} %pad_maximum_fusion) | copy-start | bytes 2359300
  329.9 5.9 %copy-start.7 = (bf16[1,128,1024]{2,1,0:T(8,128)(2,1)S(1)}, bf16[1,128,1024]{2,1,0:T(8,128)(2,1)}, u32[]{:S(2)}) copy-start(bf16[1,128,1024]{2,1,0:T(8,128)(2,1)} %param.18) | copy-start | bytes 786436
  329.9 6.1 %copy-start.1 = (bf16[2048,1024]{1,0:T(8,128)(2,1)S(1)}, bf16[2048,1024]{1,0:T(8,128)(2,1)}, u32[]{:S(2)}) copy-start(bf16[2048,1024]{1,0:T(8,128)(2,1)} %get-tuple-element.33) | copy-start | bytes 12582916
  336.0 1.6 copy-start.5
  336.0 3.0 copy-start.9
  446.8 7.0 %copy-start.16 = (f32[64,1024]{1,0:T(8,128)S(1)}, f32[64,1024]{1,0:T(8,128)}, u32[]{:S(2)}) copy-start(f32[64,1024]{1,0:T(8,128)} %get-tuple-element.123) | copy-start | bytes 786436
  446.8 7.7 %copy-start.15 = (f32[32,3072]{1,0:T(8,128)S(1)}, f32[32,3072]{1,0:T(8,128)}, u32[]{:S(2)}) copy-start(f32[32,3072]{1,0:T(8,128)} %get-tuple-element.126) | copy-start | bytes 1179652
  446.8 8.5 %copy-start.17 = (f32[32,1024]{1,0:T(8,128)S(1)}, f32[32,1024]{1,0:T(8,128)}, u32[]{:S(2)}) copy-start(f32[32,1024]{1,0:T(8,128)} %get-tuple-element.127) | copy-start | bytes 393220
  446.8 9.1 %copy-start.14 = (f32[32,4096]{1,0:T(8,128)S(1)}, f32[32,4096]{1,0:T(8,128)}, u32[]{:S(2)}) copy-start(f32[32,4096]{1,0:T(8,128)} %get-tuple-element.128) | copy-start | bytes 1572868
  451.5 5.2 %copy-start.13 = (f32[128,1024]{1,0:T(8,128)S(1)}, f32[128,1024]{1,0:T(8,128)}, u32[]{:S(2)}) copy-start(f32[128,1024]{1,0:T(8,128)} %get-tuple-element.130) | copy-start | bytes 1572868

commit v2 on v0

--- a/solution.py
+++ b/solution.py
@@ -1,8 +1,11 @@
+import functools
 import math
 
 import jax
 import jax.numpy as jnp
 from jax import lax
+from jax.experimental import pallas as pl
+from jax.experimental.pallas import tpu as pltpu
 from jax.sharding import PartitionSpec as P
 
 HEADS = 16
@@ -357,6 +360,1637 @@
     )
 
 
+MESH = pl.DeviceIdType.MESH
+
+
+class Place:
+    def __init__(self, depth):
+        self.depth = depth
+        self.b = lax.axis_index("blk")
+        self.x = lax.axis_index("uly")
+        self.z = self.b // 4
+        self.y = (self.b // 2) % 2
+        self.c = self.b % 2
+        self.to_x = (self.b, 1 - self.x)
+        self.to_y = (self.b + 2 - 4 * self.y, self.x)
+        self.to_core = (self.b + 1 - 2 * self.c, self.x)
+        self.to_far = (self.b + 3 - 4 * self.y - 2 * self.c, self.x)
+        self.to_up = (self.b + 4, self.x)
+        self.to_down = (self.b - 4, self.x)
+
+    def shard(self, z, y, c, x):
+        return ((z * 2 + y) * 2 + c) * 2 + x
+
+    def greet(self):
+        barrier = pltpu.get_barrier_semaphore()
+        for to in (self.to_x, self.to_y, self.to_core, self.to_far):
+            pl.semaphore_signal(barrier, inc=1, device_id=to, device_id_type=MESH)
+
+        @pl.when(self.z < self.depth - 1)
+        def _():
+            pl.semaphore_signal(barrier, inc=1, device_id=self.to_up, device_id_type=MESH)
+
+        @pl.when(self.z > 0)
+        def _():
+            pl.semaphore_signal(barrier, inc=1, device_id=self.to_down, device_id_type=MESH)
+
+        top = self.depth - 1
+        pl.semaphore_wait(barrier, 4 + (self.z + top - 1) // top + (2 * top - 1 - self.z) // top)
+
+
+def remote(src, dst, send, recv, to):
+    return pltpu.make_async_remote_copy(
+        src_ref=src, dst_ref=dst, send_sem=send, recv_sem=recv, device_id=to, device_id_type=MESH
+    )
+
+
+class Gather:
+    SENDS = 64
+    RECVS = 48
+
+    def __init__(self, place, src, dst, rows, lo, hi, split, plane_first, sends, recvs):
+        self.p, self.src, self.dst, self.rows = place, src, dst, rows
+        self.lo, self.hi, self.split, self.plane_first = lo, hi, split, plane_first
+        self.sends, self.recvs = sends, recvs
+        self.pending = []
+
+    def part(self, z, y, c, x, half=None):
+        base = self.p.shard(z, y, c, x) * self.rows
+        rows = self.rows
+        if half is not None:
+            rows = rows // 2
+            base = base + half * rows
+        return self.dst.at[pl.ds(pl.multiple_of(base, rows), rows), pl.ds(self.lo, self.hi - self.lo)]
+
+    def mine(self):
+        return self.src.at[:, pl.ds(self.lo, self.hi - self.lo)]
+
+    def go(self, when, src, dst, send, recv, to):
+        def start():
+            remote(src, dst, self.sends.at[send], self.recvs.at[recv], to).start()
+
+        def finish():
+            remote(src, dst, self.sends.at[send], self.recvs.at[recv], to).wait_send()
+
+        if when is None:
+            start()
+            self.pending.append(finish)
+        else:
+            pl.when(when)(start)
+            self.pending.append(lambda: pl.when(when)(finish))
+
+    def got(self, dst, recv):
+        remote(dst, dst, self.sends.at[0], self.recvs.at[recv], self.p.to_x).wait_recv()
+
+    def share(self, when, src, z, y, x):
+        slot = z * 4 + y * 2 + x
+        self.go(when, src, self.part(z, y, self.p.c, x), slot, slot, self.p.to_core)
+
+    def steps(self):
+        return self.plane_steps() if self.plane_first else self.line_steps()
+
+    def line_steps(self):
+        p = self.p
+        top = p.depth - 1
+
+        def hand_on(when, src, z):
+            whole = self.part(z, p.y, p.c, p.x)
+            self.go(when, src, whole, 24 + z, 20 + z, p.to_x)
+            self.go(when, src, whole, 28 + z, 24 + z, p.to_y)
+            self.share(when, src, z, p.y, p.x)
+
+        def own():
+            src = self.mine()
+            whole = self.part(p.z, p.y, p.c, p.x)
+            self.go(p.z < top, src, whole, 16 + p.z, 16 + p.z, p.to_up)
+            self.go(p.z > 0, src, whole, 20 + p.z, 16 + p.z, p.to_down)
+            hand_on(None, src, p.z)
+
+        def line(d):
+            for side in (-1, 1):
+                z = p.z + side * d
+                here = (z >= 0) & (z <= top)
+                whole = self.part(z, p.y, p.c, p.x)
+                pl.when(here)(lambda: self.got(whole, 16 + z))
+                if side < 0:
+                    self.go(here & (p.z < top), whole, whole, 16 + z, 16 + z, p.to_up)
+                else:
+                    self.go(here & (p.z > 0), whole, whole, 20 + z, 16 + z, p.to_down)
+                hand_on(here, whole, z)
+
+        def origins(d):
+            return [(None, p.z)] if d == 0 else [
+                ((p.z + s * d >= 0) & (p.z + s * d <= top), p.z + s * d) for s in (-1, 1)
+            ]
+
+        def cond(when, f):
+            f() if when is None else pl.when(when)(f)
+
+        def cross(d):
+            for when, z in origins(d):
+                from_x = self.part(z, p.y, p.c, 1 - p.x)
+                cond(when, lambda: self.got(from_x, 20 + z))
+                self.share(when, from_x, z, p.y, 1 - p.x)
+                if self.split:
+                    part = self.part(z, p.y, p.c, 1 - p.x, 0)
+                else:
+                    part = from_x
+                self.go(when, part, part, 32 + z, 28 + z, p.to_y)
+                from_y = self.part(z, 1 - p.y, p.c, p.x)
+                cond(when, lambda: self.got(from_y, 24 + z))
+                self.share(when, from_y, z, 1 - p.y, p.x)
+                if self.split:
+                    part = self.part(z, 1 - p.y, p.c, p.x, 1)
+                    self.go(when, part, part, 36 + z, 32 + z, p.to_x)
+
+        def corner(d):
+            for when, z in origins(d):
+                whole = self.part(z, 1 - p.y, p.c, 1 - p.x)
+                if self.split:
+                    for half in (0, 1):
+                        part = self.part(z, 1 - p.y, p.c, 1 - p.x, half)
+                        cond(when, lambda: self.got(part, 28 + 4 * half + z))
+                else:
+                    cond(when, lambda: self.got(whole, 28 + z))
+                self.share(when, whole, z, 1 - p.y, 1 - p.x)
+
+        out = [(0, own)]
+        for d in range(p.depth):
+            if d:
+                out.append((d, functools.partial(line, d)))
+            out.append((d + 1, functools.partial(cross, d)))
+            out.append((d + 2, functools.partial(corner, d)))
+        return out
+
+    def plane_steps(self):
+        p = self.p
+        top = p.depth - 1
+
+        def along(when, src, z, y, x, up, down):
+            slot = 20 + z * 4 + y * 2 + x
+            whole = self.part(z, y, p.c, x)
+            if up:
+                w = p.z < top
+                self.go(w if when is None else w & when, src, whole, slot, slot, p.to_up)
+            if down:
+                w = p.z > 0
+                self.go(w if when is None else w & when, src, whole, slot + 16, slot, p.to_down)
+
+        def own():
+            src = self.mine()
+            whole = self.part(p.z, p.y, p.c, p.x)
+            self.go(None, src, whole, 16, 16, p.to_x)
+            self.go(None, src, whole, 17, 17, p.to_y)
+            along(None, src, p.z, p.y, p.x, True, True)
+            self.share(None, src, p.z, p.y, p.x)
+
+        def cross():
+            from_x = self.part(p.z, p.y, p.c, 1 - p.x)
+            self.got(from_x, 16)
+            part = self.part(p.z, p.y, p.c, 1 - p.x, 0) if self.split else from_x
+            self.go(None, part, part, 18, 18, p.to_y)
+            along(None, from_x, p.z, p.y, 1 - p.x, True, True)
+            self.share(None, from_x, p.z, p.y, 1 - p.x)
+            from_y = self.part(p.z, 1 - p.y, p.c, p.x)
+            self.got(from_y, 17)
+            if self.split:
+                part = self.part(p.z, 1 - p.y, p.c, p.x, 1)
+                self.go(None, part, part, 19, 19, p.to_x)
+            along(None, from_y, p.z, 1 - p.y, p.x, True, True)
+            self.share(None, from_y, p.z, 1 - p.y, p.x)
+
+        def corner():
+            whole = self.part(p.z, 1 - p.y, p.c, 1 - p.x)
+            if self.split:
+                for half in (0, 1):
+                    self.got(self.part(p.z, 1 - p.y, p.c, 1 - p.x, half), 18 + half)
+            else:
+                self.got(whole, 18)
+            along(None, whole, p.z, 1 - p.y, 1 - p.x, True, True)
+            self.share(None, whole, p.z, 1 - p.y, 1 - p.x)
+
+        def line(d, k):
+            y = p.y if k in (0, 1) else 1 - p.y
+            x = p.x if k in (0, 2) else 1 - p.x
+            for side in (-1, 1):
+                z = p.z + side * d
+                here = (z >= 0) & (z <= top)
+                whole = self.part(z, y, p.c, x)
+                pl.when(here)(lambda: self.got(whole, 20 + z * 4 + y * 2 + x))
+                along(here, whole, z, y, x, side < 0, side > 0)
+                self.share(here, whole, z, y, x)
+
+        out = [(0, own), (1, cross), (2, corner)]
+        for d in range(1, p.depth):
+            for k in range(4):
+                out.append((d + 0.1 + min(k, 2) * 0.9, functools.partial(line, d, k)))
+        return out
+
+    def shared(self):
+        p = self.p
+        for z in range(p.depth):
+            for y in range(2):
+                for x in range(2):
+                    self.got(self.part(z, y, 1 - p.c, x), z * 4 + y * 2 + x)
+
+    def sent(self):
+        for wait in self.pending:
+            wait()
+
+
+class Quad:
+    def __init__(self, p, src, dst, sems):
+        self.p, self.src, self.dst, self.sems = p, src, dst, sems
+
+    def to_core(self):
+        return remote(self.src, self.dst(1), self.sems(0), self.sems(1), self.p.to_core)
+
+    def to_y(self):
+        return remote(self.src, self.dst(2), self.sems(2), self.sems(3), self.p.to_y)
+
+    def on(self):
+        return remote(self.dst(2), self.dst(3), self.sems(4), self.sems(5), self.p.to_core)
+
+    def start(self):
+        self.to_y().start()
+        self.to_core().start()
+
+    def relay(self):
+        self.to_y().wait_recv()
+        self.on().start()
+
+    def arrived(self):
+        self.to_core().wait_recv()
+        self.on().wait_recv()
+
+    def finish(self):
+        self.to_y().wait_send()
+        self.to_core().wait_send()
+        self.on().wait_send()
+
+
+class QuadRows:
+    def __init__(self, p, src, dst, sems):
+        self.p, self.src, self.dst, self.sems = p, src, dst, sems
+
+    def mine(self, y, c):
+        pair = self.dst.shape[2]
+        return self.src.at[:, pl.ds(pl.multiple_of((y * 2 + c) * pair, pair), pair), :]
+
+    def own(self):
+        return pltpu.make_async_copy(self.mine(self.p.y, self.p.c), self.dst.at[0], self.sems.at[0])
+
+    def copy(self, k):
+        p = self.p
+        y, c, to = (
+            (p.y, 1 - p.c, p.to_core),
+            (1 - p.y, p.c, p.to_y),
+            (1 - p.y, 1 - p.c, p.to_far),
+        )[k - 1]
+        return remote(self.mine(y, c), self.dst.at[k], self.sems.at[2 * k - 1], self.sems.at[2 * k], to)
+
+    def start(self):
+        self.own().start()
+        for k in (2, 3, 1):
+            self.copy(k).start()
+
+    def arrived(self):
+        self.own().wait()
+        for k in (1, 2, 3):
+            self.copy(k).wait_recv()
+
+    def finish(self):
+        for k in (1, 2, 3):
+            self.copy(k).wait_send()
+
+
+class Reduce:
+    CHUNK = 512
+
+    def __init__(self, place, x, take, rows, lo, width, out, full, outgo, income, sends, recvs):
+        self.p, self.x, self.take, self.rows = place, x, take, rows
+        self.lo, self.width, self.out = lo, width, out
+        self.full, self.outgo, self.income = full, outgo, income
+        self.sends, self.recvs = sends, recvs
+
+    @staticmethod
+    def scratch(rows, width, depth):
+        return [
+            pltpu.VMEM((2 * depth * rows, width), jnp.bfloat16),
+            pltpu.VMEM(((2 * depth + 1) * rows, width), jnp.bfloat16),
+            pltpu.SemaphoreType.DMA((4,)),
+            pltpu.SemaphoreType.DMA((4,)),
+        ]
+
+    def part(self, ref, lo, hi):
+        return ref.at[pl.ds(lo * self.rows, (hi - lo) * self.rows)]
+
+    def along_x(self):
+        n = self.p.depth
+        return remote(
+            self.part(self.outgo, 0, n), self.part(self.income, 0, n), self.sends.at[0], self.recvs.at[0], self.p.to_x
+        )
+
+    def up(self, lo):
+        n = self.p.depth
+        return remote(
+            self.part(self.outgo, n + lo, 2 * n),
+            self.part(self.income, n + lo, 2 * n),
+            self.sends.at[1],
+            self.recvs.at[1],
+            self.p.to_up,
+        )
+
+    def down(self, hi):
+        n = self.p.depth
+        return remote(
+            self.part(self.outgo, n, n + hi),
+            self.part(self.income, n, n + hi),
+            self.sends.at[2],
+            self.recvs.at[2],
+            self.p.to_down,
+        )
+
+    def down_last(self, at):
+        n = self.p.depth
+        return remote(
+            self.part(self.outgo, n + at, n + at + 1),
+            self.part(self.income, 2 * n, 2 * n + 1),
+            self.sends.at[3],
+            self.recvs.at[3],
+            self.p.to_down,
+        )
+
+    def columns(self, body):
+        @pl.loop(0, self.width // self.CHUNK)
+        def _(j):
+            body(j, pl.ds(pl.multiple_of(j * self.CHUNK, self.CHUNK), self.CHUNK))
+
+    def product(self, side, j):
+        n, r = self.p.depth, self.rows
+        side = pl.ds(pl.multiple_of(side * r, r), r)
+        x = jnp.concatenate([self.x[k, :, side, :].reshape(n * r, self.x.shape[3]) for k in range(4)], 1)
+        return jnp.dot(x, self.take(self.lo // self.CHUNK + j), preferred_element_type=jnp.float32)
+
+    def begin(self):
+        p, n, r = self.p, self.p.depth, self.rows
+
+        def away(j, here):
+            self.outgo[pl.ds(0, n * r), here] = self.product(1 - p.x, j).astype(jnp.bfloat16)
+
+        self.columns(away)
+        self.along_x().start()
+
+        def near(j, here):
+            self.full[pl.ds(0, n * r), here] = self.product(p.x, j)
+
+        self.columns(near)
+
+        @pl.when(p.z == 0)
+        def _():
+            ref = self.part(self.income, n, n + 1)
+            ref[...] = jnp.zeros(ref.shape, ref.dtype)
+
+        @pl.when(p.z == n - 1)
+        def _():
+            ref = self.part(self.income, 2 * n, 2 * n + 1)
+            ref[...] = jnp.zeros(ref.shape, ref.dtype)
+
+    def total(self, h, lo, hi):
+        n, r = self.p.depth, self.rows
+
+        def body(j, here):
+            rows = pl.ds(lo * r, (hi - lo) * r)
+            line = pl.ds((n + lo) * r, (hi - lo) * r)
+            total = self.full[rows, here] + self.income[rows, here].astype(jnp.float32)
+            if h:
+                total = total + self.income[line, here].astype(jnp.float32)
+            self.outgo[line, here] = total.astype(jnp.bfloat16)
+
+        self.columns(body)
+
+    def hop(self, h):
+        p, n = self.p, self.p.depth
+        if h == 0:
+            self.along_x().wait_recv()
+
+        @pl.when(p.z == h)
+        def _():
+            if h:
+                self.up(h).wait_recv()
+            self.total(h, h + 1, n)
+            self.up(h + 1).start()
+
+        @pl.when(p.z == n - 1 - h)
+        def _():
+            if h:
+                self.down(n - 1 - h).wait_recv()
+            self.total(h, 0, n - 1 - h)
+            if h < n - 2:
+                self.down(n - 2 - h).start()
+            self.down_last(n - 2 - h).start()
+
+    def end(self):
+        p, n, r = self.p, self.p.depth, self.rows
+        pl.when(p.z == n - 1)(lambda: self.up(n - 1).wait_recv())
+        pl.when(p.z < n - 1)(lambda: self.down_last(0).wait_recv())
+        own = pl.ds(pl.multiple_of(p.z * r, r), r)
+        line = pl.ds(pl.multiple_of((n + p.z) * r, r), r)
+
+        def body(j, here):
+            there = pl.ds(pl.multiple_of(self.lo + j * self.CHUNK, self.CHUNK), self.CHUNK)
+            self.out[:, there] = (
+                self.full[own, here]
+                + self.income[own, here].astype(jnp.float32)
+                + self.income[line, here].astype(jnp.float32)
+                + self.income[pl.ds(2 * n * r, r), here].astype(jnp.float32)
+            )
+
+        self.columns(body)
+
+    def finish(self):
+        p, n = self.p, self.p.depth
+        self.along_x().wait_send()
+        for h in range(n - 1):
+            pl.when(p.z == h)(lambda: self.up(h + 1).wait_send())
+
+            @pl.when(p.z == n - 1 - h)
+            def _():
+                if h < n - 2:
+                    self.down(n - 2 - h).wait_send()
+                self.down_last(n - 2 - h).wait_send()
+
+
+VMEM_BYTES = 58 * 2**20
+
+
+def kernel_params(number):
+    return pltpu.CompilerParams(collective_id=number, has_side_effects=True, vmem_limit_bytes=VMEM_BYTES)
+
+
+def in_vmem(count):
+    return [pl.BlockSpec(memory_space=pltpu.VMEM)] * count
+
+
+def in_any(count):
+    return [pl.BlockSpec(memory_space=pl.ANY)] * count
+
+
+def ranges(cols, cut):
+    return [(0, cut, True), (cut, cols, False)] if cut else [(0, cols, False)]
+
+
+def keep_own(p, pairs, sems):
+    copies = []
+    for k, (src, dst, rows) in enumerate(pairs):
+        at = pl.multiple_of(p.shard(p.z, p.y, p.c, p.x) * rows, rows)
+        copies.append(pltpu.make_async_copy(src, dst.at[pl.ds(at, rows)], sems.at[k]))
+    for copy in copies:
+        copy.start()
+    return copies
+
+
+class Exchange:
+    def __init__(self, place, count, src, dst, sends, recvs, own):
+        self.p, self.count, self.src, self.dst = place, count, src, dst
+        self.sends, self.recvs, self.own = sends, recvs, own
+
+    def copy(self, k):
+        to = (self.p.b + k) % self.count
+        return remote(
+            self.src.at[to], self.dst.at[self.p.b], self.sends.at[k], self.recvs.at[k], (to, self.p.x)
+        )
+
+    def mine(self):
+        return pltpu.make_async_copy(self.src.at[self.p.b], self.dst.at[self.p.b], self.own)
+
+    def start(self):
+        self.mine().start()
+        for k in range(1, self.count):
+            self.copy(k).start()
+
+    def arrived(self):
+        self.mine().wait()
+        for k in range(1, self.count):
+            came = (self.p.b + self.count - k) % self.count
+            remote(
+                self.dst.at[came], self.dst.at[came], self.sends.at[k], self.recvs.at[k], self.p.to_x
+            ).wait_recv()
+
+    def finish(self):
+        for k in range(1, self.count):
+            self.copy(k).wait_send()
+
+
+def exchange_sems(count):
+    return [
+        pltpu.SemaphoreType.DMA((count,)),
+        pltpu.SemaphoreType.DMA((count,)),
+        pltpu.SemaphoreType.DMA,
+    ]
+
+
+def greet_plane(p, count):
+    barrier = pltpu.get_barrier_semaphore()
+    for k in range(1, count):
+        pl.semaphore_signal(barrier, inc=1, device_id=((p.b + k) % count, p.x), device_id_type=MESH)
+    pl.semaphore_signal(barrier, inc=1, device_id=p.to_x, device_id_type=MESH)
+    pl.semaphore_wait(barrier, count)
+
+
+def play(events):
+    for event in events:
+        event()
+
+
+def three_terms(v):
+    a = v.astype(jnp.bfloat16).astype(jnp.float32)
+    b = (v - a).astype(jnp.bfloat16).astype(jnp.float32)
+    return a, b, v - a - b
+
+
+def extra_rows(rows, length, width):
+    shape = (length, width)
+    row = lax.broadcasted_iota(jnp.int32, shape, 0)
+    total = jnp.zeros(shape, jnp.float32)
+    for k, values in enumerate(rows):
+        total = jnp.where(row == k, values, total)
+    return total.astype(jnp.bfloat16)
+
+
+def attend_open(p, lengths, got, qkv, keys, values):
+    count, _, span = got.shape
+    frames = count * span
+    for k in range(count):
+        qkv[:, k * span : (k + 1) * span] = got[k]
+    position = lax.broadcasted_iota(jnp.int32, (1, frames), 1)
+    hidden_key = jnp.where(position < lengths[p.x], 0.0, -1e30)
+    keys[...] = jnp.concatenate([qkv[HEAD_DIM : 2 * HEAD_DIM, :], extra_rows([hidden_key], HEAD_DIM, frames)], 0).T
+    values[...] = jnp.concatenate([qkv[2 * HEAD_DIM :, :], extra_rows([1.0], 16, frames)], 0)
+
+
+def attend(p, lengths, got, qkv, keys, values, mixed_out, lse, plain, block, lo, hi):
+    span = got.shape[2]
+    length = lengths[p.x]
+    ones = extra_rows([1.0], HEAD_DIM, block)
+    scaling = HEAD_DIM ** (-0.5)
+    parts = block // span
+
+    @pl.loop(lo, hi)
+    def _(j):
+        here = pl.ds(pl.multiple_of(j * block, block), block)
+        query = jnp.concatenate([qkv[:HEAD_DIM, here] * jnp.bfloat16(scaling), ones], 0)
+        score = jnp.dot(keys[...], query, preferred_element_type=jnp.float32)
+        peak = jnp.max(score, 0, keepdims=True)
+        weights = jnp.exp(score - peak).astype(jnp.bfloat16)
+        out = jnp.dot(values[...], weights, preferred_element_type=jnp.float32)
+        total = out[HEAD_DIM : HEAD_DIM + 1]
+        out = out[:HEAD_DIM] / total
+        plain[:, here] = out
+        lse[:, here] = peak + jnp.log(total)
+        column = lax.broadcasted_iota(jnp.int32, (HEAD_DIM, block), 1) + j * block
+        kept = jnp.where(column < length, out, 0.0).astype(jnp.bfloat16)
+        for k in range(parts):
+            mixed_out[j * parts + k] = kept[:, k * span : (k + 1) * span]
+
+
+def attend_back_open(p, lengths, qkv, keys, values, sums):
+    frames = qkv.shape[1]
+    length = lengths[p.x]
+    position = lax.broadcasted_iota(jnp.int32, (1, frames), 1)
+    hidden_key = jnp.where(position < length, 0.0, -1e30)
+    keys[...] = jnp.concatenate(
+        [qkv[HEAD_DIM : 2 * HEAD_DIM, :], extra_rows([hidden_key, 1.0, 1.0, 1.0], HEAD_DIM, frames)], 0
+    ).T
+    values[...] = jnp.concatenate(
+        [qkv[2 * HEAD_DIM :, :], extra_rows([1.0, 1.0, 1.0], HEAD_DIM, frames)], 0
+    ).T
+    sums[...] = jnp.zeros_like(sums)
+
+
+def attend_back(got, qkv, lse, plain, keys, values, sums, grads_out, block, lo, hi):
+    span = got.shape[2]
+    scaling = HEAD_DIM ** (-0.5)
+    parts = block // span
+
+    @pl.loop(lo, hi)
+    def _(j):
+        here = pl.ds(pl.multiple_of(j * block, block), block)
+        query = qkv[:HEAD_DIM, here] * jnp.bfloat16(scaling)
+        upstream = jnp.concatenate([got[j * parts + k] for k in range(parts)], 1)
+        delta = jnp.sum(upstream.astype(jnp.float32) * plain[:, here], 0, keepdims=True)
+        left = jnp.concatenate(
+            [query, extra_rows([1.0, *[-t for t in three_terms(lse[:, here])]], HEAD_DIM, block)], 0
+        )
+        right = jnp.concatenate([upstream, extra_rows([-t for t in three_terms(delta)], HEAD_DIM, block)], 0)
+        weights = jnp.exp(jnp.dot(keys[...], left, preferred_element_type=jnp.float32))
+        slope = jnp.dot(values[...], right, preferred_element_type=jnp.float32)
+        slope = (weights * slope).astype(jnp.bfloat16)
+        sums[:, HEAD_DIM:] += lax.dot_general(
+            weights.astype(jnp.bfloat16), upstream, (((1,), (1,)), ((), ())), preferred_element_type=jnp.float32
+        )
+        sums[:, :HEAD_DIM] += lax.dot_general(
+            slope, query, (((1,), (1,)), ((), ())), preferred_element_type=jnp.float32
+        )
+        query_grad = (
+            jnp.dot(qkv[HEAD_DIM : 2 * HEAD_DIM, :], slope, preferred_element_type=jnp.float32) * scaling
+        ).astype(jnp.bfloat16)
+        for k in range(parts):
+            grads_out[j * parts + k, :HEAD_DIM, :] = query_grad[:, k * span : (k + 1) * span]
+
+
+def attend_back_close(sums, grads_out):
+    count, _, span = grads_out.shape
+
+    @pl.loop(0, count)
+    def _(k):
+        rows = pl.ds(pl.multiple_of(k * span, span), span)
+        grads_out[k, HEAD_DIM:, :] = sums[rows, :].T.astype(jnp.bfloat16)
+
+
+def others(p, count, k):
+    number = (p.b * 2 + p.x + k) % (2 * count)
+    return (number // 2, number % 2)
+
+
+def nt(left, right):
+    return lax.dot_general(left, right, (((1,), (1,)), ((), ())), preferred_element_type=jnp.float32)
+
+
+def mean(v):
+    return jnp.mean(v, -1, keepdims=True)
+
+
+def normal(v):
+    center = v - mean(v)
+    rstd = lax.rsqrt(mean(center * center) + epsilon)
+    return center * rstd, rstd
+
+
+def normal_back(grad, hat, rstd, scale):
+    gx = grad * (1.0 + scale)
+    return rstd * (gx - mean(gx) - hat * mean(gx * hat))
+
+
+def fold(v):
+    width = v.shape[1] // 8
+    return jnp.concatenate([v[:, k * width : (k + 1) * width] for k in range(8)], 0)
+
+
+class Tiles:
+    def __init__(self, p, src, dst, sends, recvs, each):
+        self.p, self.src, self.dst, self.sends, self.recvs, self.each = p, src, dst, sends, recvs, each
+        self.count = 4 * p.depth
+
+    def number(self, k=0):
+        return (self.p.b * 2 + self.p.x + k) % (2 * self.count)
+
+    def copy(self, k):
+        src = self.src.at[self.number(k)] if self.each else self.src
+        return remote(src, self.dst.at[self.number()], self.sends.at[k], self.recvs.at[k], others(self.p, self.count, k))
+
+    def start(self):
+        for k in range(1, 2 * self.count):
+            self.copy(k).start()
+        if self.each:
+            self.dst[self.number()] = self.src[self.number()]
+        else:
+            self.dst[self.number()] = self.src[...]
+
+    def arrived(self):
+        for k in range(1, 2 * self.count):
+            came = self.dst.at[self.number(2 * self.count - k)]
+            remote(came, came, self.sends.at[k], self.recvs.at[k], self.p.to_x).wait_recv()
+
+    def finish(self):
+        for k in range(1, 2 * self.count):
+            self.copy(k).wait_send()
+
+
+BACK_IN = [
+    "lengths", "base", "mods", "b_up", "b_down", "cosine",
+    "sine", "w_mod", "times", "qkv", "lse", "plain",
+    "cot", "mixed", "joined", "normed", "w_out", "w_up",
+    "w_down", "w_qkv", "w_skip",
+]
+BACK_OUT = [
+    "output", "joined_grad", "skip_grad", "qkv_grad", "out_grad", "up_grad",
+    "down_grad", "mod_grad", "sums_out", "times_full",
+]
+BACK_SCRATCH = [
+    "wide", "weights", "middle", "total", "back", "normed2",
+    "normed2_rows", "act_rows", "gcot", "gup", "gbranch", "xact",
+    "xmix", "xn2", "xnormed", "xjoined", "mixed_grad", "got",
+    "keys", "values", "kv_sums", "grads_out", "got_grads", "pack",
+    "pack_full", "tiles", "tiles_full", "time_tile", "weight_sems", "row_sems", "act_sems",
+    "cot_sems", "up_sems", "branch_sems", "late_sems", "s1", "r1",
+    "o1", "s2", "r2", "o2", "s3", "r3",
+    "s4", "r4", "s5", "r5", "own_sems",
+]
+
+
+def back_kernel(depth, shards, *refs):
+    names = BACK_IN + BACK_OUT + BACK_SCRATCH
+    r = Refs(names, refs)
+    rest = list(refs[len(names) :])
+    p = Place(depth)
+    count = 4 * depth
+    devices = 2 * count
+    frames, model = r.base.shape
+    ff = r.w_up.shape[1]
+    half = model // 2
+    chunk = 512
+    chunks = ff // chunk
+    bf = jnp.bfloat16
+
+    barrier = pltpu.get_barrier_semaphore()
+    for k in range(1, devices):
+        pl.semaphore_signal(barrier, inc=1, device_id=others(p, count, k), device_id_type=MESH)
+
+    def fetch_out(k):
+        return pltpu.make_async_copy(r.w_out.at[:, pl.ds(k * chunk, chunk)], r.weights.at[k], r.weight_sems.at[k])
+
+    def fetch_up(k):
+        slot = 2 + k % 2
+        at = pl.multiple_of(k * chunk, chunk)
+        return pltpu.make_async_copy(r.w_up.at[:, pl.ds(at, chunk)], r.weights.at[slot], r.weight_sems.at[slot])
+
+    def fetch_down(k, side):
+        slot = 4 + k % 2
+        at = pl.multiple_of(k * chunk, chunk)
+        return pltpu.make_async_copy(
+            r.w_down.at[pl.ds(at, chunk), pl.ds(side * half, half)],
+            r.weights.at[slot, pl.ds(side * chunk, chunk)],
+            r.weight_sems.at[slot + 2 * side],
+        )
+
+    def fetch_qkv(k):
+        return pltpu.make_async_copy(r.w_qkv.at[:, pl.ds(k * chunk, chunk)], r.weights.at[k], r.weight_sems.at[k])
+
+    def fetch_skip(k):
+        return pltpu.make_async_copy(
+            r.w_skip.at[pl.ds((k // 2) * model, model), pl.ds((k % 2) * chunk, chunk)],
+            r.weights.at[k],
+            r.weight_sems.at[k],
+        )
+
+    for k in range(2):
+        fetch_out(k).start()
+        fetch_up(k).start()
+        fetch_down(k, 0).start()
+        fetch_down(k, 1).start()
+    own_cot = pltpu.make_async_copy(r.cot, r.gcot.at[0], r.own_sems.at[0])
+    own_cot.start()
+    pl.semaphore_wait(barrier, devices - 1)
+
+    share_cot = Quad(p, r.cot, lambda k: r.gcot.at[k], lambda k: r.cot_sems.at[k])
+    share_mixed = QuadRows(p, r.mixed, r.xmix, r.row_sems.at[0])
+    share_n2 = QuadRows(p, r.normed2_rows, r.xn2, r.row_sems.at[1])
+    share_normed = QuadRows(p, r.normed, r.xnormed, r.row_sems.at[3])
+    share_joined = QuadRows(p, r.joined, r.xjoined, r.row_sems.at[4])
+
+    def share_act(c, what):
+        pair = chunk // 2
+        z = c // 2
+
+        def half(core):
+            return r.act_rows.at[c, pl.ds(pl.multiple_of(core * pair, pair), pair)]
+
+        def copy(core, k, to):
+            return remote(half(core), r.xact.at[k, z], r.act_sems.at[z, 2 * k - 1], r.act_sems.at[z, 2 * k], to)
+
+        own = pltpu.make_async_copy(half(p.c), r.xact.at[0, z], r.act_sems.at[z, 0])
+        mine = p.y == c % 2
+        if what == "start":
+
+            @pl.when(mine)
+            def _():
+                own.start()
+                copy(1 - p.c, 1, p.to_core).start()
+
+            @pl.when(p.y != c % 2)
+            def _():
+                copy(p.c, 2, p.to_y).start()
+                copy(1 - p.c, 3, p.to_far).start()
+
+        elif what == "arrived":
+
+            @pl.when(mine)
+            def _():
+                own.wait()
+                copy(1 - p.c, 1, p.to_core).wait_recv()
+                copy(p.c, 2, p.to_y).wait_recv()
+                copy(1 - p.c, 3, p.to_far).wait_recv()
+
+        else:
+            pl.when(mine)(lambda: copy(1 - p.c, 1, p.to_core).wait_send())
+
+            @pl.when(p.y != c % 2)
+            def _():
+                copy(p.c, 2, p.to_y).wait_send()
+                copy(1 - p.c, 3, p.to_far).wait_send()
+
+    share_branch = Quad(p, r.gbranch.at[0], lambda k: r.gbranch.at[k], lambda k: r.branch_sems.at[k])
+
+    def share_up(c):
+        return Quad(p, r.gup.at[0, c], lambda k: r.gup.at[k, c], lambda k: r.up_sems.at[c, k])
+
+    def share_late(c):
+        return Quad(p, r.gup.at[0, c], lambda k: r.gup.at[k, c], lambda k: r.late_sems.at[c, k])
+
+    share_cot.start()
+    share_mixed.start()
+
+    length = r.lengths[p.x]
+    position = p.b * frames
+    kept = (position + lax.broadcasted_iota(jnp.int32, (frames, 1), 0) < length).astype(jnp.float32)
+    kept_row = (position + lax.broadcasted_iota(jnp.int32, (1, frames), 1) < length).astype(jnp.float32)
+    a_scale = kept * r.mods[0:1, :]
+    f_scale = kept * r.mods[2:3, :]
+    f_shift = kept * r.mods[3:4, :]
+    mixed = r.mixed[...].reshape(model, frames).T
+    for k in range(2):
+        fetch_out(k).wait()
+        cols = pl.ds(k * chunk, chunk)
+        r.middle[:, cols] = r.base[:, cols] + jnp.dot(mixed, r.weights[k], preferred_element_type=jnp.float32)
+    hat, rstd = normal(r.middle[...])
+    normed2 = (hat * (1.0 + f_scale) + f_shift).astype(bf)
+    r.normed2[...] = normed2
+    r.normed2_rows[...] = normed2.T.reshape(r.normed2_rows.shape)
+    share_n2.start()
+    r.total[...] = jnp.zeros_like(r.total)
+    r.back[...] = jnp.zeros_like(r.back)
+    own_cot.wait()
+
+    @pl.loop(0, chunks)
+    def _(c):
+        fetch_up(c).wait()
+        fetch_down(c, 0).wait()
+        fetch_down(c, 1).wait()
+        up, down = r.weights.at[2 + c % 2], r.weights.at[4 + c % 2]
+        here = pl.ds(pl.multiple_of(c * chunk, chunk), chunk)
+        inner = jnp.dot(r.normed2[...], up[...], preferred_element_type=jnp.float32) + r.b_up[:, here]
+        cdf = 0.5 * (1.0 + lax.erf(inner * (0.5**0.5)))
+        act = (inner * cdf).astype(bf)
+        slope = cdf + inner * (jnp.exp(-0.5 * inner * inner) * (1.0 / math.sqrt(2.0 * math.pi)))
+        act_grad = nt(r.gcot[0, :, :half], down[:chunk, :]) + nt(r.gcot[0, :, half:], down[chunk:, :])
+        inner_grad = (act_grad * slope).astype(bf)
+        r.gup[0, c] = inner_grad
+        rows = chunk // 4
+        r.act_rows[c] = act.T
+        share_act(c, "start")
+        r.total[:, :half] += jnp.dot(act, down[:chunk, :], preferred_element_type=jnp.float32)
+        r.total[:, half:] += jnp.dot(act, down[chunk:, :], preferred_element_type=jnp.float32)
+        r.back[...] += nt(inner_grad, up[...])
+        bias = jnp.sum(inner_grad.astype(jnp.float32), 0, keepdims=True)
+        for k in range(4):
+            r.tiles[c * 4 + k, 0:1, :] = bias[:, k * rows : (k + 1) * rows]
+
+        @pl.when(c + 2 < chunks)
+        def _():
+            fetch_up(c + 2).start()
+            fetch_down(c + 2, 0).start()
+            fetch_down(c + 2, 1).start()
+
+    middle = r.middle[...]
+    r.output[...] = (middle + r.total[...] + r.b_down[...]).astype(bf)
+    hat, rstd = normal(middle)
+    grad = r.back[...]
+    cot = r.gcot[0].astype(jnp.float32)
+    middle_grad = cot + normal_back(grad, hat, rstd, f_scale)
+    r.middle[...] = middle_grad
+    branch_grad = middle_grad.astype(bf)
+    r.gbranch[0] = branch_grad
+    there = Exchange(p, count, r.mixed_grad, r.got, r.s1, r.r1, r.o1)
+    back = Exchange(p, count, r.grads_out, r.got_grads, r.s2, r.r2, r.o2)
+    mixed_grad = nt(r.weights[0], branch_grad[:, :half]) + nt(r.weights[1], branch_grad[:, half:])
+    r.mixed_grad[...] = (mixed_grad.astype(bf) * kept_row.astype(bf)).reshape(r.mixed_grad.shape)
+    there.start()
+    for c in range(6):
+        share_up(c).start()
+    for k in range(6):
+        fetch_qkv(k).start()
+    f_scale_grad = jnp.sum(kept * grad * hat, 0, keepdims=True)
+    f_shift_grad = jnp.sum(kept * grad, 0, keepdims=True)
+    r.pack[:, 256:384] = fold(f_scale_grad)
+    r.pack[:, 384:512] = fold(f_shift_grad)
+
+    def columns_of(ref):
+        def take(j):
+            here = pl.ds(pl.multiple_of(j * chunk, chunk), chunk)
+            return jnp.concatenate([ref[k, :, here] for k in range(4)], 0)
+
+        return take
+
+    def blocks_of(first):
+        return lambda j: jnp.concatenate([r.gup[k, first + j] for k in range(4)], 0)
+
+    sums = {}
+    given = (
+        ("up", r.xn2, blocks_of(0), r.up_grad),
+        ("down", r.xact, columns_of(r.gcot), r.down_grad),
+        ("out", r.xmix, columns_of(r.gbranch), r.out_grad),
+        ("qkv", r.xnormed, blocks_of(0), r.qkv_grad),
+        ("skip", r.xjoined, blocks_of(chunks), r.skip_grad),
+    )
+    full = {}
+    for (name, x, take, out), (rows, cols, parts) in zip(given, shards):
+        width = cols // parts
+        sums[name] = []
+        for k in range(parts):
+            if name in ("up", "down", "out"):
+                full[name, k] = rest.pop(0)
+            mine = full[{"qkv": "up", "skip": "down"}.get(name, name), k]
+            sums[name].append(Reduce(p, x, take, rows, k * width, width, out, mine, *rest[:4]))
+            rest = rest[4:]
+    up, down, out, qkv, skip = (sums[name] for name in ("up", "down", "out", "qkv", "skip"))
+
+    def ready(shares):
+        for share in shares:
+            if isinstance(share, Quad):
+                share.relay()
+        for share in shares:
+            share.arrived()
+
+    blocks = 2048 // 256
+    attend_back_open(p, r.lengths, r.qkv, r.keys, r.values, r.kv_sums)
+    for c in range(chunks):
+        share_act(c, "arrived")
+    ready([share_cot])
+    down[0].begin()
+    down[1].begin()
+    there.arrived()
+    attend = functools.partial(
+        attend_back, r.got, r.qkv, r.lse, r.plain, r.keys, r.values, r.kv_sums, r.grads_out, 256
+    )
+    attend(0, blocks // 2)
+    ready([share_n2, share_up(0), share_up(1)])
+    up[0].begin()
+    down[0].hop(0)
+    attend(blocks // 2, blocks)
+    attend_back_close(r.kv_sums, r.grads_out)
+    ready([share_up(2), share_up(3)])
+    up[1].begin()
+    ready([share_up(4), share_up(5)])
+    up[2].begin()
+    for c in range(6):
+        share_up(c).finish()
+    back.start()
+    share_up(6).start()
+    share_up(7).start()
+    share_branch.start()
+    share_normed.start()
+    share_joined.start()
+    down[0].hop(1)
+    down[1].hop(0)
+    up[0].hop(0)
+    down[0].hop(2)
+    down[1].hop(1)
+    up[1].hop(0)
+    ready([share_up(6), share_up(7)])
+    up[3].begin()
+    up[0].hop(1)
+    down[0].end()
+    down[1].hop(2)
+
+    back.arrived()
+
+    def unturned(at):
+        h = r.got_grads[:, at : at + HEAD_DIM, :].astype(jnp.float32)
+        first, second = h[:, : HEAD_DIM // 2, :], h[:, HEAD_DIM // 2 :, :]
+        cosine, sine = r.cosine[...][None], r.sine[...][None]
+        h = jnp.concatenate([first * cosine + second * sine, second * cosine - first * sine], 1)
+        return h.astype(bf)
+
+    for part in range(3):
+        if part < 2:
+            h = unturned(part * HEAD_DIM)
+        else:
+            h = r.got_grads[:, 2 * HEAD_DIM :, :]
+        h = h.reshape(model, frames).T
+        for k in range(2):
+            r.gup[0, 2 * part + k] = h[:, k * chunk : (k + 1) * chunk]
+            share_late(2 * part + k).start()
+    for k in range(6):
+        fetch_qkv(k).wait()
+        made = nt(r.gup[0, k], r.weights[k])
+        if k == 0:
+            r.back[...] = made
+        else:
+            r.back[...] += made
+    for k in range(4):
+        fetch_skip(k).start()
+    hat, rstd = normal(r.base[...])
+    grad = r.back[...]
+    base_grad = (r.middle[...] + normal_back(grad, hat, rstd, a_scale)).astype(bf)
+    for k in range(2):
+        r.gup[0, chunks + k] = base_grad[:, k * chunk : (k + 1) * chunk]
+        share_late(chunks + k).start()
+    r.pack[:, 0:128] = fold(jnp.sum(kept * grad * hat, 0, keepdims=True))
+    r.pack[:, 128:256] = fold(jnp.sum(kept * grad, 0, keepdims=True))
+    bias_down = jnp.sum(cot, 0, keepdims=True)
+    bias_skip = jnp.sum(base_grad.astype(jnp.float32), 0, keepdims=True)
+    each = model // devices
+    for k in range(devices):
+        r.tiles[k, 1:2, :each] = bias_down[:, k * each : (k + 1) * each]
+        r.tiles[k, 1:2, each : 2 * each] = bias_skip[:, k * each : (k + 1) * each]
+    packs = Tiles(p, r.pack, r.pack_full, r.s3, r.r3, False)
+    tiles = Tiles(p, r.tiles, r.tiles_full, r.s4, r.r4, True)
+    times = Tiles(p, r.time_tile, r.times_full, r.s5, r.r5, False)
+    packs.start()
+    tiles.start()
+    for i in range(2):
+        total = None
+        for j in range(2):
+            fetch_skip(2 * i + j).wait()
+            made = nt(r.gup[0, chunks + j], r.weights[2 * i + j])
+            total = made if total is None else total + made
+        r.joined_grad[i] = total.astype(bf)
+
+    ready([share_mixed, share_branch])
+    out[0].begin()
+    down[1].end()
+    up[0].hop(2)
+    up[1].hop(1)
+    up[2].hop(0)
+    ready([share_normed, share_late(0), share_late(1)])
+    up[0].end()
+    up[1].hop(2)
+    up[2].hop(1)
+    up[3].hop(0)
+    qkv[0].begin()
+    up[1].end()
+    up[2].hop(2)
+    up[3].hop(1)
+    out[0].hop(0)
+    ready([share_late(2), share_late(3)])
+    qkv[1].begin()
+    up[2].end()
+    up[3].hop(2)
+    out[0].hop(1)
+    qkv[0].hop(0)
+    ready([share_late(4), share_late(5)])
+    qkv[2].begin()
+    up[3].end()
+    out[0].hop(2)
+    qkv[0].hop(1)
+    qkv[1].hop(0)
+    ready([share_joined, share_late(chunks), share_late(chunks + 1)])
+    skip[0].begin()
+    skip[1].begin()
+    out[0].end()
+    qkv[0].hop(2)
+    qkv[1].hop(1)
+    qkv[2].hop(0)
+
+    packs.arrived()
+    rows = [jnp.zeros(r.pack.shape, jnp.float32) for _ in range(2)]
+    for k in range(devices):
+        rows[k % 2] = rows[k % 2] + r.pack_full[k]
+    total = jnp.zeros((8, r.w_mod.shape[0]), jnp.float32)
+    columns = r.times[...].T
+    share = r.w_mod.shape[0]
+    width = model // 8
+    for part in range(4):
+        for k in range(8):
+            values = [rows[s][k : k + 1, part * width : (part + 1) * width] for s in range(2)]
+            here = pl.ds(part * model + k * width, width)
+            left = extra_rows([*three_terms(values[0]), *three_terms(values[1])], 8, width)
+            total = total + nt(left, r.w_mod[:, here])
+            r.mod_grad[:, here] = columns[:share, 0:1] * values[0] + columns[:share, 4:5] * values[1]
+    first = total[0:1] + total[1:2] + total[2:3]
+    second = total[3:4] + total[4:5] + total[5:6]
+    made = jnp.concatenate([first, second, jnp.zeros((6, share), jnp.float32)], 0)
+    r.time_tile[...] = jnp.concatenate([made, jnp.zeros((8, 128 - share), jnp.float32)], 1)
+    times.start()
+    qkv[0].end()
+    qkv[1].hop(2)
+    qkv[2].hop(1)
+    skip[0].hop(0)
+    skip[1].hop(0)
+    tiles.arrived()
+    total = r.tiles_full[0]
+    for k in range(1, devices):
+        total = total + r.tiles_full[k]
+    r.sums_out[...] = total
+    qkv[1].end()
+    qkv[2].hop(2)
+    skip[0].hop(1)
+    skip[1].hop(1)
+    qkv[2].end()
+    skip[0].hop(2)
+    skip[1].hop(2)
+    skip[0].end()
+    skip[1].end()
+    times.arrived()
+    for group in sums.values():
+        for one in group:
+            one.finish()
+    for share in (share_cot, share_mixed, share_n2, share_normed, share_joined, share_branch):
+        share.finish()
+    for c in range(chunks):
+        share_act(c, "sent")
+    for c in (6, 7):
+        share_up(c).finish()
+    for c in [*range(6), chunks, chunks + 1]:
+        share_late(c).finish()
+    for one in (there, back, packs, tiles, times):
+        one.finish()
+
+
+def in_slices(x, depth):
+    return x.reshape(depth, x.shape[0] // depth, x.shape[1])
+
+
+def back_call(depth, devices, args):
+    base, qkv = args["base"], args["qkv"]
+    frames, model = base.shape
+    count = devices // 2
+    ff = args["w_up"].shape[1]
+    bf, f32 = jnp.bfloat16, jnp.float32
+    share = args["w_mod"].shape[0]
+    shards = [
+        (model // devices, ff, 4),
+        (ff // devices, model, 2),
+        (model // devices, model, 1),
+        (model // devices, 3 * model, 3),
+        (2 * model // devices, model, 2),
+    ]
+    sum_scratch = []
+    for which, (rows, cols, parts) in enumerate(shards):
+        for _ in range(parts):
+            if which < 3:
+                sum_scratch.append(pltpu.VMEM((depth * rows, cols // parts), f32))
+            sum_scratch += Reduce.scratch(rows, cols // parts, depth)
+    chunks = ff // 512
+    dma = pltpu.SemaphoreType.DMA
+
+    def rows(n):
+        return pltpu.VMEM((4, depth, n // (4 * depth), frames), bf)
+
+    scratch = dict(
+        wide=pltpu.VMEM((8, 128), f32),
+        weights=pltpu.VMEM((6, model, 512), bf),
+        middle=pltpu.VMEM((frames, model), f32),
+        total=pltpu.VMEM((frames, model), f32),
+        back=pltpu.VMEM((frames, model), f32),
+        normed2=pltpu.VMEM((frames, model), bf),
+        normed2_rows=pltpu.VMEM((depth, model // depth, frames), bf),
+        act_rows=pltpu.VMEM((chunks, 512, frames), bf),
+        gcot=pltpu.VMEM((4, frames, model), bf),
+        gup=pltpu.VMEM((4, chunks + 2, frames, 512), bf),
+        gbranch=pltpu.VMEM((4, frames, model), bf),
+        xact=rows(ff),
+        xmix=rows(model),
+        xn2=rows(model),
+        xnormed=rows(model),
+        xjoined=rows(2 * model),
+        mixed_grad=pltpu.VMEM((count, HEAD_DIM, frames), bf),
+        got=pltpu.VMEM((count, HEAD_DIM, frames), bf),
+        keys=pltpu.VMEM((qkv.shape[1], 2 * HEAD_DIM), bf),
+        values=pltpu.VMEM((qkv.shape[1], 2 * HEAD_DIM), bf),
+        kv_sums=pltpu.VMEM((qkv.shape[1], 2 * HEAD_DIM), f32),
+        grads_out=pltpu.VMEM((count, 3 * HEAD_DIM, frames), bf),
+        got_grads=pltpu.VMEM((count, 3 * HEAD_DIM, frames), bf),
+        pack=pltpu.VMEM((8, 512), f32),
+        pack_full=pltpu.VMEM((devices, 8, 512), f32),
+        tiles=pltpu.VMEM((devices, 8, 128), f32),
+        tiles_full=pltpu.VMEM((devices, 8, 128), f32),
+        time_tile=pltpu.VMEM((8, 128), f32),
+        weight_sems=dma((8,)),
+        row_sems=dma((5, 7)),
+        act_sems=dma((depth, 7)),
+        cot_sems=dma((6,)),
+        up_sems=dma((chunks, 6)),
+        branch_sems=dma((6,)),
+        late_sems=dma((chunks + 2, 6)),
+        s1=dma((count,)),
+        r1=dma((count,)),
+        o1=dma,
+        s2=dma((count,)),
+        r2=dma((count,)),
+        o2=dma,
+        s3=dma((devices,)),
+        r3=dma((devices,)),
+        s4=dma((devices,)),
+        r4=dma((devices,)),
+        s5=dma((devices,)),
+        r5=dma((devices,)),
+        own_sems=dma((1,)),
+    )
+    shape = jax.ShapeDtypeStruct
+    outs = dict(
+        output=shape((frames, model), bf),
+        joined_grad=shape((2, frames, model), bf),
+        skip_grad=shape((2 * model // devices, model), f32),
+        qkv_grad=shape((model // devices, 3 * model), f32),
+        out_grad=shape((model // devices, model), f32),
+        up_grad=shape((model // devices, ff), f32),
+        down_grad=shape((ff // devices, model), f32),
+        mod_grad=shape((share, 4 * model), f32),
+        sums_out=shape((8, 128), f32),
+        times_full=shape((devices, 8, 128), f32),
+    )
+    made = pl.pallas_call(
+        functools.partial(back_kernel, depth, shards),
+        name="back",
+        out_shape=[outs[name] for name in BACK_OUT],
+        in_specs=[pl.BlockSpec(memory_space=pltpu.SMEM)] + in_vmem(11) + in_any(1) + in_vmem(1) + in_any(7),
+        out_specs=in_vmem(len(BACK_OUT)),
+        scratch_shapes=[scratch[name] for name in BACK_SCRATCH] + sum_scratch,
+        compiler_params=kernel_params(3),
+    )(*[args[name] for name in BACK_IN])
+    return dict(zip(BACK_OUT, made))
+
+
+FRONT_IN = (
+    ["lengths", "time_row", "b_skip", "b_up_part", "b_down_part", "w_mod", "cosine", "sine", "hidden", "skip_in"]
+    + ["w_skip", "w_qkv", "w_out", "w_up", "w_down"]
+)
+FRONT_OUT = (
+    ["skip_full", "qkv_full", "out_full", "up_full", "down_full", "mixed"]
+    + ["times", "mods", "b_up", "b_down", "base", "normed", "joined", "qkv", "lse", "plain"]
+)
+FRONT_SCRATCH = (
+    ["own_time", "other_time", "got_time", "pack", "pack_full", "skip_here", "qkv_here", "heads_in", "got", "keys", "values", "mixed_out"]
+    + ["time_sems", "load_sems", "own_sems", "sends", "recvs", "s1", "r1", "o1", "s2", "r2", "o2"]
+)
+
+
+class Refs:
+    def __init__(self, names, refs):
+        for name, ref in zip(names, refs):
+            setattr(self, name, ref)
+
+
+def front_kernel(depth, cuts, *refs):
+    r = Refs(FRONT_IN + FRONT_OUT + FRONT_SCRATCH, refs)
+    p = Place(depth)
+    count = 4 * depth
+    devices = 2 * count
+    frames, model = r.hidden.shape
+    bf = jnp.bfloat16
+    share = r.w_mod.shape[0]
+    tile = pl.ds(pl.multiple_of((p.b // 2) * 128, 128), 128)
+    part = r.time_row[:, tile].astype(jnp.float32)
+    mark = lax.broadcasted_iota(jnp.int32, (8, 128), 0) // 4 == p.x
+    for ref, x in ((r.own_time, p.x), (r.other_time, 1 - p.x)):
+        slot = p.c * 2 + x
+        picked = part[:, 0:share]
+        for k in range(1, 4):
+            picked = jnp.where(slot == k, part[:, k * share : (k + 1) * share], picked)
+        picked = jnp.concatenate([picked, jnp.zeros((1, 128 - share), jnp.float32)], 1)
+        ref[...] = jnp.where(mark, picked, 0.0)
+    greet_plane(p, count)
+    ask = remote(r.other_time, r.got_time, r.time_sems.at[0], r.time_sems.at[1], p.to_x)
+    ask.start()
+
+    groups = {}
+    number = 0
+    owns = []
+    for name, src, dst in (
+        ("skip", r.w_skip, r.skip_full),
+        ("qkv", r.w_qkv, r.qkv_full),
+        ("out", r.w_out, r.out_full),
+        ("up", r.w_up, r.up_full),
+        ("down", r.w_down, r.down_full),
+    ):
+        groups[name] = []
+        for lo, hi, first in ranges(src.shape[1], src.shape[1] // cuts[name] if cuts[name] else 0):
+            groups[name].append(
+                Gather(p, src, dst, src.shape[0], lo, hi, True, first, r.sends.at[number], r.recvs.at[number])
+            )
+            number += 1
+        owns.append((src, dst, src.shape[0]))
+    packs = Gather(
+        p, r.pack, r.pack_full, 8, 0, r.pack.shape[1], False, False, r.sends.at[number], r.recvs.at[number]
+    )
+    number += 1
+    there = Exchange(p, count, r.heads_in, r.got, r.s1, r.r1, r.o1)
+    back = Exchange(p, count, r.mixed_out, r.mixed, r.s2, r.r2, r.o2)
+
+    def products():
+        ask.wait_recv()
+        both = r.own_time[...] + r.got_time[...]
+        r.times[...] = both
+        left = both[:, : r.w_mod.shape[0]].astype(bf)
+        row = lax.broadcasted_iota(jnp.int32, (8, model), 0) % 4
+        total = jnp.zeros((8, model), jnp.float32)
+        for part in range(4):
+            made = jnp.dot(
+                left, r.w_mod[:, part * model : (part + 1) * model], preferred_element_type=jnp.float32
+            )
+            total = jnp.where(row == part, made, total)
+        r.pack[:, :model] = total
+        each = r.b_skip.shape[1]
+        r.pack[:, model:] = jnp.zeros((8, 128), jnp.float32)
+        r.pack[0:1, model:] = r.b_up_part[...].astype(jnp.float32)
+        r.pack[1:2, model : model + each] = r.b_skip[...].astype(jnp.float32)
+        r.pack[1:2, model + each : model + 2 * each] = r.b_down_part[...].astype(jnp.float32)
+
+    def turned_inputs():
+        half = depth // 2
+        rows = 2 * model // depth
+        for k, ref in enumerate((r.hidden, r.skip_in)):
+            r.joined[k * half : (k + 1) * half] = ref[...].T.reshape(half, rows, frames)
+
+    def load_skip():
+        return pltpu.make_async_copy(r.skip_full, r.skip_here, r.load_sems.at[0])
+
+    def load_qkv():
+        return pltpu.make_async_copy(r.qkv_full, r.qkv_here, r.load_sems.at[1])
+
+    own_copies = []
+
+    def complete(name):
+        for g in groups[name]:
+            g.shared()
+
+    def begin_loads():
+        own_copies[0].wait()
+        complete("skip")
+        load_skip().start()
+        own_copies[1].wait()
+        complete("qkv")
+        load_qkv().start()
+
+    def first_norm():
+        at = pl.multiple_of(p.shard(p.z, p.y, p.c, p.x) * 8, 8)
+        r.pack_full[pl.ds(at, 8), :] = r.pack[...]
+        packs.shared()
+        total = r.pack_full[0:8, :model]
+        for k in range(1, devices):
+            total = total + r.pack_full[k * 8 : (k + 1) * 8, :model]
+        mods = jnp.where(p.x == 0, total[0:4], total[4:8])
+        r.mods[0:4, :] = mods
+        r.mods[4:8, :] = mods
+        each = model // devices
+        tiles = [r.pack_full[k * 8 : k * 8 + 2, model:] for k in range(devices)]
+        for k in range(devices):
+            r.b_up[:, k * 128 : (k + 1) * 128] = tiles[k][0:1]
+        b_skip = jnp.concatenate([t[1:2, :each] for t in tiles], 1)
+        r.b_down[...] = jnp.concatenate([t[1:2, each : 2 * each] for t in tiles], 1)
+        length = r.lengths[p.x]
+        kept = (p.b * frames + lax.broadcasted_iota(jnp.int32, (frames, 1), 0) < length).astype(jnp.float32)
+        load_skip().wait()
+        base = jnp.dot(r.hidden[...], r.skip_here[:model, :], preferred_element_type=jnp.float32)
+        base = base + jnp.dot(r.skip_in[...], r.skip_here[model:, :], preferred_element_type=jnp.float32) + b_skip
+        r.base[...] = base
+        hat, _ = normal(base)
+        normed = (hat * (1.0 + kept * mods[0:1]) + kept * mods[1:2]).astype(bf)
+        r.normed[...] = normed.T.reshape(r.normed.shape)
+        load_qkv().wait()
+        cosine, sine = r.cosine[...][None], r.sine[...][None]
+        for part in range(3):
+            made = jnp.dot(
+                normed, r.qkv_here[:, part * model : (part + 1) * model], preferred_element_type=jnp.float32
+            )
+            made = made.T.reshape(HEADS, HEAD_DIM, frames)
+            if part < 2:
+                made = turn(made, cosine, sine)
+            r.heads_in[:, part * HEAD_DIM : (part + 1) * HEAD_DIM, :] = made.astype(bf)
+        there.start()
+
+    def attention(lo, hi):
+        attend(p, r.lengths, r.got, r.qkv, r.keys, r.values, r.mixed_out, r.lse, r.plain, 256, lo, hi)
+
+    blocks = 2048 // 256
+
+    def first_half():
+        there.arrived()
+        attend_open(p, r.lengths, r.got, r.qkv, r.keys, r.values)
+        attention(0, blocks // 2)
+
+    def second_half():
+        attention(blocks // 2, blocks)
+        back.start()
+
+    events = []
+    for k, name in enumerate(("skip", "qkv")):
+        events += [(t, k, f) for g in groups[name] for t, f in g.steps()]
+    events.append((0.3, 0, products))
+    events.append((0.35, 0, turned_inputs))
+    events += [(t + 0.5, 9, f) for t, f in packs.steps()]
+    for k, name in enumerate(("out", "up", "down")):
+        for g in groups[name]:
+            events += [((4.05 if t == 0 else 4.7 + t), k + 2, f) for t, f in g.steps()]
+    events.append((5.6, 0, begin_loads))
+    events.append((5.65, 0, first_norm))
+    events.append((6.9, 0, first_half))
+    events.append((7.9, 0, second_half))
+    events.sort(key=lambda e: (e[0], e[1]))
+    own_copies += keep_own(p, owns, r.own_sems)
+    play([f for _, _, f in events])
+    for name in ("out", "up", "down"):
+        complete(name)
+    for group in groups.values():
+        for g in group:
+            g.sent()
+    packs.sent()
+    there.finish()
+    back.arrived()
+    back.finish()
+    for copy in own_copies[2:]:
+        copy.wait()
+    ask.wait_send()
+
+
+def front_call(depth, devices, args):
+    cuts = dict(skip=4, qkv=4, out=8, up=8, down=8)
+    frames, model = args["hidden"].shape
+    bf, f32 = jnp.bfloat16, jnp.float32
+    count = devices // 2
+    total = count * frames
+    shape = jax.ShapeDtypeStruct
+
+    def whole(name):
+        rows, cols = args[name].shape
+        return shape((devices * rows, cols), bf)
+
+    outs = dict(
+        skip_full=whole("w_skip"),
+        qkv_full=whole("w_qkv"),
+        out_full=whole("w_out"),
+        up_full=whole("w_up"),
+        down_full=whole("w_down"),
+        mixed=shape((count, HEAD_DIM, frames), bf),
+        times=shape((8, 128), f32),
+        mods=shape((8, model), f32),
+        b_up=shape((1, 4 * model), f32),
+        b_down=shape((1, model), f32),
+        base=shape((frames, model), f32),
+        normed=shape((depth, model // depth, frames), bf),
+        joined=shape((depth, 2 * model // depth, frames), bf),
+        qkv=shape((3 * HEAD_DIM, total), bf),
+        lse=shape((1, total), f32),
+        plain=shape((HEAD_DIM, total), f32),
+    )
+    dma = pltpu.SemaphoreType.DMA
+    gathers = 11
+    scratch = dict(
+        own_time=pltpu.VMEM((8, 128), f32),
+        other_time=pltpu.VMEM((8, 128), f32),
+        got_time=pltpu.VMEM((8, 128), f32),
+        pack=pltpu.VMEM((8, model + 128), f32),
+        pack_full=pltpu.VMEM((devices * 8, model + 128), f32),
+        skip_here=pltpu.VMEM((2 * model, model), bf),
+        qkv_here=pltpu.VMEM((model, 3 * model), bf),
+        heads_in=pltpu.VMEM((count, 3 * HEAD_DIM, frames), bf),
+        got=pltpu.VMEM((count, 3 * HEAD_DIM, frames), bf),
+        keys=pltpu.VMEM((total, 2 * HEAD_DIM), bf),
+        values=pltpu.VMEM((HEAD_DIM + 16, total), bf),
+        mixed_out=pltpu.VMEM((count, HEAD_DIM, frames), bf),
+        time_sems=dma((2,)),
+        load_sems=dma((2,)),
+        own_sems=dma((5,)),
+        sends=dma((gathers, Gather.SENDS)),
+        recvs=dma((gathers, Gather.RECVS)),
+        s1=dma((count,)),
+        r1=dma((count,)),
+        o1=dma,
+        s2=dma((count,)),
+        r2=dma((count,)),
+        o2=dma,
+    )
+    made = pl.pallas_call(
+        functools.partial(front_kernel, depth, cuts),
+        name="front",
+        out_shape=[outs[name] for name in FRONT_OUT],
+        in_specs=[pl.BlockSpec(memory_space=pltpu.SMEM)] + in_vmem(14),
+        out_specs=in_any(6) + in_vmem(10),
+        scratch_shapes=[scratch[name] for name in FRONT_SCRATCH],
+        compiler_params=kernel_params(1),
+    )(*[args[name] for name in FRONT_IN])
+    return dict(zip(FRONT_OUT, made))
+
+
+def write_kernel(count, times, sums, joined, *refs):
+    ins, outs = refs[:count], refs[count:]
+    for src, dst in zip(ins, outs):
+        dst[...] = src[...]
+    hidden_grad, skip_grad, time_grad, b_up, b_skip, b_down = outs[count:]
+    hidden_grad[...] = joined[0]
+    skip_grad[...] = joined[1]
+    each = b_skip.shape[1]
+    part = jnp.where(lax.axis_index("uly") == 0, times[:, 0, :each], times[:, 1, :each])
+    time_grad[...] = jnp.concatenate([part[k : k + 1] for k in range(times.shape[0])], 1)
+    b_up[...] = sums[0:1, :]
+    b_down[...] = sums[1:2, :each]
+    b_skip[...] = sums[1:2, each : 2 * each]
+
+
+def write_call(made, names, each):
+    shape = jax.ShapeDtypeStruct
+    joined = made["joined_grad"]
+    frames, model = joined.shape[1:]
+    plain = [shape(made[name].shape, made[name].dtype) for name in names]
+    return pl.pallas_call(
+        functools.partial(write_kernel, len(names)),
+        name="write",
+        out_shape=plain
+        + [shape((frames, model), joined.dtype)] * 2
+        + [shape((1, model), jnp.float32), shape((1, 128), jnp.float32)]
+        + [shape((1, each), jnp.float32)] * 2,
+        in_specs=in_vmem(3 + len(names)),
+        out_specs=in_vmem(6 + len(names)),
+        compiler_params=pltpu.CompilerParams(vmem_limit_bytes=VMEM_BYTES),
+    )(made["times_full"], made["sums_out"], joined, *[made[name] for name in names])
+
+
+def first_with_second(left, right, dims):
+    return lax.dot_general(left, right, ((dims[:1], dims[1:]), ((), ())), preferred_element_type=jnp.float32)
+
+
+def turn(values, cosine, sine):
+    half = HEAD_DIM // 2
+    first, second = values[..., :half, :], values[..., half:, :]
+    return jnp.concatenate([first * cosine - second * sine, second * cosine + first * sine], -2)
+
+
+def on_device(hidden, skip_in, time_embed, lengths, cotangent, w_skip, b_skip, w_mod, w_qkv, w_out, w_up, b_up,
+              w_down, b_down):
+    block, row = lax.axis_index("blk"), lax.axis_index("uly")
+    blocks, rows = lax.axis_size("blk"), lax.axis_size("uly")
+    devices, depth = blocks * rows, blocks // 4
+    _, frames, model = hidden.shape
+    position = block * frames + jnp.arange(frames, dtype=jnp.int32)
+    length = lax.dynamic_index_in_dim(lengths, row, 0, keepdims=False)[0]
+    valid = position < length
+    half = HEAD_DIM // 2
+    freq = 10000.0 ** (-jnp.arange(half, dtype=jnp.float32) / half)
+    offsets = jnp.where(valid, position, position - length).astype(jnp.float32)
+    angle = freq[:, None] * offsets[None, :]
+    cosine, sine = jnp.cos(angle), jnp.sin(angle)
+    front = front_call(
+        depth,
+        devices,
+        dict(
+            lengths=lengths[:, 0],
+            time_row=time_embed[0],
+            b_skip=b_skip[None],
+            b_up_part=b_up[None],
+            b_down_part=b_down[None],
+            w_mod=w_mod,
+            cosine=cosine,
+            sine=sine,
+            hidden=hidden[0],
+            skip_in=skip_in[0],
+            w_skip=w_skip,
+            w_qkv=w_qkv,
+            w_out=w_out,
+            w_up=w_up,
+            w_down=w_down,
+        ),
+    )
+    made = back_call(
+        depth,
+        devices,
+        dict(
+            lengths=lengths[:, 0],
+            base=front["base"],
+            mods=front["mods"],
+            b_up=front["b_up"],
+            b_down=front["b_down"],
+            cosine=cosine,
+            sine=sine,
+            w_mod=w_mod,
+            times=front["times"],
+            qkv=front["qkv"],
+            lse=front["lse"],
+            plain=front["plain"],
+            cot=cotangent[0],
+            mixed=front["mixed"].reshape(depth, model // depth, frames),
+            joined=front["joined"],
+            normed=front["normed"],
+            w_out=front["out_full"],
+            w_up=front["up_full"],
+            w_down=front["down_full"],
+            w_qkv=front["qkv_full"],
+            w_skip=front["skip_full"],
+        ),
+    )
+    names = ["output", "skip_grad", "mod_grad", "qkv_grad", "out_grad", "up_grad", "down_grad"]
+    output, skip_grad, mod_grad, qkv_grad, out_grad, up_grad, down_grad, *small = write_call(
+        made, names, b_skip.shape[0]
+    )
+    hidden_grad, skip_in_grad, time_grad, b_up_grad, b_skip_grad, b_down_grad = small
+    return (
+        output[None],
+        hidden_grad[None],
+        skip_in_grad[None],
+        time_grad[None],
+        skip_grad,
+        b_skip_grad[0],
+        mod_grad,
+        qkv_grad,
+        out_grad,
+        up_grad,
+        b_up_grad[0],
+        down_grad,
+        b_down_grad[0],
+    )
+
+
 def solution(mesh):
     placed = (
         P("uly", "blk", None),
@@ -374,8 +2008,10 @@
         P(("blk", "uly"), None),
         P(("blk", "uly")),
     )
+    blocks = mesh.shape["blk"]
+    special = mesh.shape["uly"] == 2 and blocks == HEADS and blocks % 4 == 0 and blocks > 4
     return jax.shard_map(
-        per_device,
+        on_device if special else per_device,
         mesh=mesh,
         in_specs=placed,
         out_specs=(

time: 2380 us -> 317 us (0.13)
  waiting for transfers between devices: 1830 us -> 0 us
  Pallas kernels: 0 us -> 313 us
  blocking collectives: 234 us -> 0 us
  matrix products: 171 us -> 0 us
  other arithmetic: 61.4 us -> 1.42 us
  local copies, waits for them, and re-layouts: 43 us -> 1.24 us
    reduce_scatter x6 -> x0, waiting for transfers between devices: 1260 us -> none  [the longest x1 362 us: per_device(): lax.psum_scatter(grad_mod, ('blk', 'uly'), scatter_dimension=0, tiled=True)]
    all_gather x7 -> x0, waiting for transfers between devices: 333 us -> none  [the longest x1 75.4 us: per_device(): lax.all_gather(w_mod, ('blk', 'uly'), axis=0, tiled=True)]
    pallas_call x0 -> x3, Pallas kernels: none -> 313 us  [the longest x1 158 us: back_call(): pl.pallas_call(functools.partial(back_kernel, depth, shards), name='back'...]
    ppermute x31 -> x0, waiting for transfers between devices: 229 us -> none  [passed_along(): lax.ppermute(x, axis, [(i, (i + by) % devices) for i in range(devices)])]
    dot_general x102 -> x0, matrix products: 171 us -> none  [the longest x16 34.1 us: contribution(): jnp.einsum('rhqk,rkhd->rqhd', grad_score, key_part, preferred_element_typ...]
    unnamed x2 -> x0, blocking collectives: 80.7 us -> none
    all_gather x1 -> x0, blocking collectives: 65.5 us -> none  [per_device(): lax.all_gather(b_up, ('blk', 'uly'), axis=0, tiled=True)]
    psum x1 -> x0, blocking collectives: 59.5 us -> none  [per_device(): slot_total = lax.psum(slot_grad, 'blk')]
  transfers between devices with their start and end apart: 46 -> 0, of which waited for: 44 -> 0; matrix products, arithmetic and copies ran while one was open for 10% -> 0% of each run, Pallas kernels for 0% -> 0%
where the time goes in v2:
time: 317 us; the launch traced here: 316 us
  Pallas kernels  313 us (99%)
    pallas_call x1, Pallas kernels, back_call(): pl.pallas_call(functools.partial(back_kernel, depth, shards), name='back'...  158 us
    pallas_call x1, Pallas kernels, front_call(): pl.pallas_call(functools.partial(front_kernel, depth, cuts), name='front'...  151 us

profile of v2, /device:TPU:0, one launch (start us, length us, event | category | flops | bytes accessed | tf_op | source)
XLA Modules:
  0.0 316.4 jit_solution(17331953019833379335)
XLA Ops:
  0.7 1.2 constant_dynamic-slice_fusion
  1.9 0.6 fusion
  2.6 0.8 multiply_sine_fusion
  3.3 151.3 %front.1 = (bf16[2048,1024]{1,0:T(8,128)(2,1)}, bf16[1024,3072]{1,0:T(8,128)(2,1)}, bf16[1024,1024]{1,0:T(8,128)(2,1)}, bf16[1024,4096]{1,0:T(8,128)(2,1)}, bf16...) custom-call(s32[2]{0:T(128)} %bitcast.22, ...), custom_call_target="tpu_custom_call" | custom-call | tf_op jit(solution)/shard_map/front/pallas_call | solution.py:1855
  154.6 158.0 %back.1 = (bf16[128,1024]{1,0:T(8,128)(2,1)}, bf16[2,128,1024]{2,1,0:T(8,128)(2,1)}, f32[64,1024]{1,0:T(8,128)}, f32[32,3072]{1,0:T(8,128)}, f32[32,1024]{1,0:T(...) custom-call(s32[2]{0:T(128)} %bitcast.23, ...), custom_call_target="tpu_custom_call" | custom-call | tf_op jit(solution)/shard_map/back/pallas_call | solution.py:1594
  312.6 3.6 %write.1 = (bf16[128,1024]{1,0:T(8,128)(2,1)}, f32[64,1024]{1,0:T(8,128)}, f32[32,4096]{1,0:T(8,128)}, f32[32,3072]{1,0:T(8,128)}, f32[32,1024]{1,0:T(8,128)}, /...) custom-call(f32[32,8,128]{2,1,0:T(8,128)} %get-tuple-element.68.time, ...), custom_call_target="tpu_custom_call" | custom-call | tf_op jit(solution)/shard_map/write/pallas_call | solution.py:1887
  (1 shorter events, 0.0 us)

commit v3 on v2

--- a/solution.py
+++ b/solution.py
@@ -375,6 +375,8 @@
         self.to_y = (self.b + 2 - 4 * self.y, self.x)
         self.to_core = (self.b + 1 - 2 * self.c, self.x)
         self.to_far = (self.b + 3 - 4 * self.y - 2 * self.c, self.x)
+        self.to_across = (self.b + 2 - 4 * self.y, 1 - self.x)
+        self.to_far_x = (self.b + 1 - 2 * self.c, 1 - self.x)
         self.to_up = (self.b + 4, self.x)
         self.to_down = (self.b - 4, self.x)
 
@@ -598,25 +600,115 @@
             wait()
 
 
+class LineGather:
+    def __init__(self, place, src, piece, sends, recvs):
+        self.p, self.src, self.piece, self.sends, self.recvs = place, src, piece, sends, recvs
+        self.pending = []
+
+    def go(self, when, src, dst, send, recv, to):
+        def start():
+            remote(src, dst, self.sends.at[send], self.recvs.at[recv], to).start()
+
+        def finish():
+            remote(src, dst, self.sends.at[send], self.recvs.at[recv], to).wait_send()
+
+        if when is None:
+            start()
+            self.pending.append(finish)
+        else:
+            pl.when(when)(start)
+            self.pending.append(lambda: pl.when(when)(finish))
+
+    def got(self, dst, recv):
+        remote(dst, dst, self.sends.at[0], self.recvs.at[recv], self.p.to_x).wait_recv()
+
+    def own(self):
+        p, n = self.p, self.p.depth
+        dst = self.piece(p.z, p.c)
+        self.go(p.z < n - 1, self.src, dst, p.z, p.z, p.to_up)
+        self.go(p.z > 0, self.src, dst, n + p.z, p.z, p.to_down)
+        self.go(None, self.src, dst, 2 * n + p.z, n + p.z, p.to_core)
+
+    def line(self, d):
+        p, n = self.p, self.p.depth
+        for side in (-1, 1):
+            z = p.z + side * d
+            here = (z >= 0) & (z <= n - 1)
+            dst = self.piece(z, p.c)
+            pl.when(here)(lambda: self.got(dst, z))
+            if side < 0:
+                self.go(here & (p.z < n - 1), dst, dst, z, z, p.to_up)
+            else:
+                self.go(here & (p.z > 0), dst, dst, n + z, z, p.to_down)
+            self.go(here, dst, dst, 2 * n + z, n + z, p.to_core)
+
+    def shared(self):
+        n = self.p.depth
+        for z in range(n):
+            self.got(self.piece(z, 1 - self.p.c), n + z)
+
+    def sent(self):
+        for wait in self.pending:
+            wait()
+
+
+class Plane:
+    def __init__(self, place, src, dst, sends, recvs):
+        self.p, self.src, self.dst, self.sends, self.recvs = place, src, dst, sends, recvs
+
+    def to(self, q):
+        p = self.p
+        return (p.b + (2 - 4 * p.y) * (q // 2), p.x + (1 - 2 * p.x) * (q % 2))
+
+    def copy(self, q):
+        return remote(self.src(q), self.dst(q), self.sends.at[q], self.recvs.at[q], self.to(q))
+
+    def start(self):
+        for q in (3, 1, 2):
+            self.copy(q).start()
+
+    def arrived(self):
+        for q in (1, 2, 3):
+            self.copy(q).wait_recv()
+
+    def finish(self):
+        for q in (1, 2, 3):
+            self.copy(q).wait_send()
+
+
+class Rounds:
+    def __init__(self, place, sends, recvs):
+        self.p, self.sends, self.recvs = place, sends, recvs
+
+    def one(self, k, src, dst, to):
+        return remote(src, dst, self.sends.at[k], self.recvs.at[k], to)
+
+    def line(self, k, d):
+        p = self.p
+        z = (p.z + d) % p.depth
+        return (p.b + 4 * (z - p.z), p.x)
+
+
 class Quad:
-    def __init__(self, p, src, dst, sems):
+    def __init__(self, p, axis, src, dst, sems):
         self.p, self.src, self.dst, self.sems = p, src, dst, sems
+        self.to_pair = p.to_y if axis == 0 else p.to_x
 
     def to_core(self):
         return remote(self.src, self.dst(1), self.sems(0), self.sems(1), self.p.to_core)
 
-    def to_y(self):
-        return remote(self.src, self.dst(2), self.sems(2), self.sems(3), self.p.to_y)
+    def to_next(self):
+        return remote(self.src, self.dst(2), self.sems(2), self.sems(3), self.to_pair)
 
     def on(self):
         return remote(self.dst(2), self.dst(3), self.sems(4), self.sems(5), self.p.to_core)
 
     def start(self):
-        self.to_y().start()
+        self.to_next().start()
         self.to_core().start()
 
     def relay(self):
-        self.to_y().wait_recv()
+        self.to_next().wait_recv()
         self.on().start()
 
     def arrived(self):
@@ -624,30 +716,29 @@
         self.on().wait_recv()
 
     def finish(self):
-        self.to_y().wait_send()
+        self.to_next().wait_send()
         self.to_core().wait_send()
         self.on().wait_send()
 
 
 class QuadRows:
-    def __init__(self, p, src, dst, sems):
-        self.p, self.src, self.dst, self.sems = p, src, dst, sems
-
-    def mine(self, y, c):
-        pair = self.dst.shape[2]
-        return self.src.at[:, pl.ds(pl.multiple_of((y * 2 + c) * pair, pair), pair), :]
+    def __init__(self, p, axis, src, dst, sems):
+        self.p, self.axis, self.src, self.dst, self.sems = p, axis, src, dst, sems
+
+    def mine(self, side, c):
+        return self.src.at[:, side, c] if self.axis == 0 else self.src.at[:, :, c, side]
 
     def own(self):
-        return pltpu.make_async_copy(self.mine(self.p.y, self.p.c), self.dst.at[0], self.sems.at[0])
+        p = self.p
+        side = p.y if self.axis == 0 else p.x
+        return pltpu.make_async_copy(self.mine(side, p.c), self.dst.at[0], self.sems.at[0])
 
     def copy(self, k):
         p = self.p
-        y, c, to = (
-            (p.y, 1 - p.c, p.to_core),
-            (1 - p.y, p.c, p.to_y),
-            (1 - p.y, 1 - p.c, p.to_far),
-        )[k - 1]
-        return remote(self.mine(y, c), self.dst.at[k], self.sems.at[2 * k - 1], self.sems.at[2 * k], to)
+        side = p.y if self.axis == 0 else p.x
+        pair, far = (p.to_y, p.to_far) if self.axis == 0 else (p.to_x, p.to_far_x)
+        side, c, to = ((side, 1 - p.c, p.to_core), (1 - side, p.c, pair), (1 - side, 1 - p.c, far))[k - 1]
+        return remote(self.mine(side, c), self.dst.at[k], self.sems.at[2 * k - 1], self.sems.at[2 * k], to)
 
     def start(self):
         self.own().start()
@@ -667,11 +758,15 @@
 class Reduce:
     CHUNK = 512
 
-    def __init__(self, place, x, take, rows, lo, width, out, full, outgo, income, sends, recvs):
+    def __init__(self, place, axis, x, take, rows, lo, width, out, full, outgo, income, sends, recvs):
         self.p, self.x, self.take, self.rows = place, x, take, rows
+        self.side = place.x if axis == 0 else place.y
+        self.to_other = place.to_x if axis == 0 else place.to_y
         self.lo, self.width, self.out = lo, width, out
         self.full, self.outgo, self.income = full, outgo, income
         self.sends, self.recvs = sends, recvs
+        self.first = place.depth
+        self.chunk = min(self.CHUNK, width)
 
     @staticmethod
     def scratch(rows, width, depth):
@@ -685,84 +780,90 @@
     def part(self, ref, lo, hi):
         return ref.at[pl.ds(lo * self.rows, (hi - lo) * self.rows)]
 
-    def along_x(self):
+    def across(self):
         n = self.p.depth
         return remote(
-            self.part(self.outgo, 0, n), self.part(self.income, 0, n), self.sends.at[0], self.recvs.at[0], self.p.to_x
+            self.part(self.outgo, 0, n), self.part(self.income, 0, n), self.sends.at[0], self.recvs.at[0], self.to_other
         )
 
     def up(self, lo):
-        n = self.p.depth
+        f, n = self.first, self.p.depth
         return remote(
-            self.part(self.outgo, n + lo, 2 * n),
-            self.part(self.income, n + lo, 2 * n),
+            self.part(self.outgo, f + lo, f + n),
+            self.part(self.income, f + lo, f + n),
             self.sends.at[1],
             self.recvs.at[1],
             self.p.to_up,
         )
 
     def down(self, hi):
-        n = self.p.depth
+        f = self.first
         return remote(
-            self.part(self.outgo, n, n + hi),
-            self.part(self.income, n, n + hi),
+            self.part(self.outgo, f, f + hi),
+            self.part(self.income, f, f + hi),
             self.sends.at[2],
             self.recvs.at[2],
             self.p.to_down,
         )
 
     def down_last(self, at):
-        n = self.p.depth
+        f, n = self.first, self.p.depth
         return remote(
-            self.part(self.outgo, n + at, n + at + 1),
-            self.part(self.income, 2 * n, 2 * n + 1),
+            self.part(self.outgo, f + at, f + at + 1),
+            self.part(self.income, f + n, f + n + 1),
             self.sends.at[3],
             self.recvs.at[3],
             self.p.to_down,
         )
 
     def columns(self, body):
-        @pl.loop(0, self.width // self.CHUNK)
+        @pl.loop(0, self.width // self.chunk)
         def _(j):
-            body(j, pl.ds(pl.multiple_of(j * self.CHUNK, self.CHUNK), self.CHUNK))
+            body(j, pl.ds(pl.multiple_of(j * self.chunk, self.chunk), self.chunk))
 
     def product(self, side, j):
         n, r = self.p.depth, self.rows
-        side = pl.ds(pl.multiple_of(side * r, r), r)
-        x = jnp.concatenate([self.x[k, :, side, :].reshape(n * r, self.x.shape[3]) for k in range(4)], 1)
-        return jnp.dot(x, self.take(self.lo // self.CHUNK + j), preferred_element_type=jnp.float32)
+        x = jnp.concatenate([self.x[k, :, side].reshape(n * r, self.x.shape[4]) for k in range(4)], 1)
+        return jnp.dot(x, self.take(self.lo // self.chunk + j), preferred_element_type=jnp.float32)
 
     def begin(self):
         p, n, r = self.p, self.p.depth, self.rows
 
         def away(j, here):
-            self.outgo[pl.ds(0, n * r), here] = self.product(1 - p.x, j).astype(jnp.bfloat16)
+            self.outgo[pl.ds(0, n * r), here] = self.product(1 - self.side, j).astype(jnp.bfloat16)
 
         self.columns(away)
-        self.along_x().start()
+        self.across().start()
 
         def near(j, here):
-            self.full[pl.ds(0, n * r), here] = self.product(p.x, j)
+            self.full[pl.ds(0, n * r), here] = self.product(self.side, j)
 
         self.columns(near)
+
+        self.zeros()
+
+    def zeros(self):
+        p, f, n = self.p, self.first, self.p.depth
 
         @pl.when(p.z == 0)
         def _():
-            ref = self.part(self.income, n, n + 1)
+            ref = self.part(self.income, f, f + 1)
             ref[...] = jnp.zeros(ref.shape, ref.dtype)
 
         @pl.when(p.z == n - 1)
         def _():
-            ref = self.part(self.income, 2 * n, 2 * n + 1)
+            ref = self.part(self.income, f + n, f + n + 1)
             ref[...] = jnp.zeros(ref.shape, ref.dtype)
 
     def total(self, h, lo, hi):
-        n, r = self.p.depth, self.rows
+        f, r = self.first, self.rows
 
         def body(j, here):
             rows = pl.ds(lo * r, (hi - lo) * r)
-            line = pl.ds((n + lo) * r, (hi - lo) * r)
-            total = self.full[rows, here] + self.income[rows, here].astype(jnp.float32)
+            line = pl.ds((f + lo) * r, (hi - lo) * r)
+            total = self.full[rows, here]
+            if f:
+                total = total + self.income[rows, here].astype(jnp.float32)
             if h:
                 total = total + self.income[line, here].astype(jnp.float32)
             self.outgo[line, here] = total.astype(jnp.bfloat16)
@@ -771,8 +872,8 @@
 
     def hop(self, h):
         p, n = self.p, self.p.depth
-        if h == 0:
-            self.along_x().wait_recv()
+        if h == 0 and self.first:
+            self.across().wait_recv()
 
         @pl.when(p.z == h)
         def _():
@@ -790,15 +891,19 @@
                 self.down(n - 2 - h).start()
             self.down_last(n - 2 - h).start()
 
+    def last_waits(self):
+        p, n = self.p, self.p.depth
+        pl.when(p.z == n - 1)(lambda: self.up(n - 1).wait_recv())
+        pl.when(p.z < n - 1)(lambda: self.down_last(0).wait_recv())
+
     def end(self):
         p, n, r = self.p, self.p.depth, self.rows
-        pl.when(p.z == n - 1)(lambda: self.up(n - 1).wait_recv())
-        pl.when(p.z < n - 1)(lambda: self.down_last(0).wait_recv())
+        self.last_waits()
         own = pl.ds(pl.multiple_of(p.z * r, r), r)
         line = pl.ds(pl.multiple_of((n + p.z) * r, r), r)
 
         def body(j, here):
-            there = pl.ds(pl.multiple_of(self.lo + j * self.CHUNK, self.CHUNK), self.CHUNK)
+            there = pl.ds(pl.multiple_of(self.lo + j * self.chunk, self.chunk), self.chunk)
             self.out[:, there] = (
                 self.full[own, here]
                 + self.income[own, here].astype(jnp.float32)
@@ -810,7 +915,8 @@
 
     def finish(self):
         p, n = self.p, self.p.depth
-        self.along_x().wait_send()
+        if self.first:
+            self.across().wait_send()
         for h in range(n - 1):
             pl.when(p.z == h)(lambda: self.up(h + 1).wait_send())
 
@@ -821,7 +927,47 @@
                 self.down_last(n - 2 - h).wait_send()
 
 
-VMEM_BYTES = 58 * 2**20
+class LineReduce(Reduce):
+    def __init__(self, place, product, rows, width, full, outgo, income, sends, recvs):
+        self.p, self.make, self.rows, self.width = place, product, rows, width
+        self.full, self.outgo, self.income = full, outgo, income
+        self.sends, self.recvs = sends, recvs
+        self.first = 0
+        self.chunk = min(self.CHUNK, width)
+
+    @staticmethod
+    def scratch(rows, width, depth):
+        return [
+            pltpu.VMEM((depth * rows, width), jnp.bfloat16),
+            pltpu.VMEM(((depth + 1) * rows, width), jnp.bfloat16),
+            pltpu.SemaphoreType.DMA((4,)),
+            pltpu.SemaphoreType.DMA((4,)),
+        ]
+
+    def begin(self):
+        def near(j, here):
+            self.full[:, here] = self.make(j)
+
+        self.columns(near)
+        self.zeros()
+
+    def end(self, write):
+        self.last_waits()
+        n, r = self.p.depth, self.rows
+        own = pl.ds(pl.multiple_of(self.p.z * r, r), r)
+
+        def body(j, here):
+            write(
+                here,
+                self.full[own, here]
+                + self.income[own, here].astype(jnp.float32)
+                + self.income[pl.ds(n * r, r), here].astype(jnp.float32),
+            )
+
+        self.columns(body)
+
+
+VMEM_BYTES = 62 * 2**20
 
 
 def kernel_params(number):
@@ -890,12 +1036,14 @@
     ]
 
 
-def greet_plane(p, count):
+def greet_plane(p, count, more):
     barrier = pltpu.get_barrier_semaphore()
+    for to in more:
+        pl.semaphore_signal(barrier, inc=1, device_id=to, device_id_type=MESH)
     for k in range(1, count):
         pl.semaphore_signal(barrier, inc=1, device_id=((p.b + k) % count, p.x), device_id_type=MESH)
     pl.semaphore_signal(barrier, inc=1, device_id=p.to_x, device_id_type=MESH)
-    pl.semaphore_wait(barrier, count)
+    pl.semaphore_wait(barrier, count + len(more))
 
 
 def play(events):
@@ -1037,169 +1185,68 @@
     return jnp.concatenate([v[:, k * width : (k + 1) * width] for k in range(8)], 0)
 
 
-class Tiles:
-    def __init__(self, p, src, dst, sends, recvs, each):
-        self.p, self.src, self.dst, self.sends, self.recvs, self.each = p, src, dst, sends, recvs, each
-        self.count = 4 * p.depth
-
-    def number(self, k=0):
-        return (self.p.b * 2 + self.p.x + k) % (2 * self.count)
-
-    def copy(self, k):
-        src = self.src.at[self.number(k)] if self.each else self.src
-        return remote(src, self.dst.at[self.number()], self.sends.at[k], self.recvs.at[k], others(self.p, self.count, k))
-
-    def start(self):
-        for k in range(1, 2 * self.count):
-            self.copy(k).start()
-        if self.each:
-            self.dst[self.number()] = self.src[self.number()]
-        else:
-            self.dst[self.number()] = self.src[...]
-
-    def arrived(self):
-        for k in range(1, 2 * self.count):
-            came = self.dst.at[self.number(2 * self.count - k)]
-            remote(came, came, self.sends.at[k], self.recvs.at[k], self.p.to_x).wait_recv()
-
-    def finish(self):
-        for k in range(1, 2 * self.count):
-            self.copy(k).wait_send()
-
-
-BACK_IN = [
-    "lengths", "base", "mods", "b_up", "b_down", "cosine",
-    "sine", "w_mod", "times", "qkv", "lse", "plain",
-    "cot", "mixed", "joined", "normed", "w_out", "w_up",
-    "w_down", "w_qkv", "w_skip",
-]
-BACK_OUT = [
-    "output", "joined_grad", "skip_grad", "qkv_grad", "out_grad", "up_grad",
-    "down_grad", "mod_grad", "sums_out", "times_full",
-]
-BACK_SCRATCH = [
-    "wide", "weights", "middle", "total", "back", "normed2",
-    "normed2_rows", "act_rows", "gcot", "gup", "gbranch", "xact",
-    "xmix", "xn2", "xnormed", "xjoined", "mixed_grad", "got",
-    "keys", "values", "kv_sums", "grads_out", "got_grads", "pack",
-    "pack_full", "tiles", "tiles_full", "time_tile", "weight_sems", "row_sems", "act_sems",
-    "cot_sems", "up_sems", "branch_sems", "late_sems", "s1", "r1",
-    "o1", "s2", "r2", "o2", "s3", "r3",
-    "s4", "r4", "s5", "r5", "own_sems",
-]
-
-
-def back_kernel(depth, shards, *refs):
-    names = BACK_IN + BACK_OUT + BACK_SCRATCH
+class Refs:
+    def __init__(self, names, refs):
+        for name, ref in zip(names, refs):
+            setattr(self, name, ref)
+
+
+def back_kernel(depth, shards, names, *refs):
     r = Refs(names, refs)
     rest = list(refs[len(names) :])
     p = Place(depth)
     count = 4 * depth
     devices = 2 * count
     frames, model = r.base.shape
-    ff = r.w_up.shape[1]
     half = model // 2
     chunk = 512
-    chunks = ff // chunk
     bf = jnp.bfloat16
+    units = r.w_up.shape[1]
 
     barrier = pltpu.get_barrier_semaphore()
     for k in range(1, devices):
         pl.semaphore_signal(barrier, inc=1, device_id=others(p, count, k), device_id_type=MESH)
 
-    def fetch_out(k):
-        return pltpu.make_async_copy(r.w_out.at[:, pl.ds(k * chunk, chunk)], r.weights.at[k], r.weight_sems.at[k])
-
-    def fetch_up(k):
-        slot = 2 + k % 2
-        at = pl.multiple_of(k * chunk, chunk)
-        return pltpu.make_async_copy(r.w_up.at[:, pl.ds(at, chunk)], r.weights.at[slot], r.weight_sems.at[slot])
-
-    def fetch_down(k, side):
-        slot = 4 + k % 2
-        at = pl.multiple_of(k * chunk, chunk)
-        return pltpu.make_async_copy(
-            r.w_down.at[pl.ds(at, chunk), pl.ds(side * half, half)],
-            r.weights.at[slot, pl.ds(side * chunk, chunk)],
-            r.weight_sems.at[slot + 2 * side],
-        )
-
-    def fetch_qkv(k):
-        return pltpu.make_async_copy(r.w_qkv.at[:, pl.ds(k * chunk, chunk)], r.weights.at[k], r.weight_sems.at[k])
-
-    def fetch_skip(k):
-        return pltpu.make_async_copy(
-            r.w_skip.at[pl.ds((k // 2) * model, model), pl.ds((k % 2) * chunk, chunk)],
-            r.weights.at[k],
-            r.weight_sems.at[k],
-        )
-
-    for k in range(2):
-        fetch_out(k).start()
-        fetch_up(k).start()
-        fetch_down(k, 0).start()
-        fetch_down(k, 1).start()
-    own_cot = pltpu.make_async_copy(r.cot, r.gcot.at[0], r.own_sems.at[0])
-    own_cot.start()
+    def fetch(src, slot):
+        return pltpu.make_async_copy(src, r.weights.at[slot], r.weight_sems.at[slot])
+
+    def columns(ref, k):
+        return ref.at[:, pl.ds(k * chunk, chunk)]
+
+    def fetch_first(slot):
+        return fetch(columns((r.w_out, r.w_up, r.w_down)[slot // 2], slot % 2), slot)
+
+    def fetch_qkv(slot):
+        return fetch(columns(r.w_qkv, slot), slot)
+
+    def fetch_skip(slot):
+        return fetch(r.w_skip.at[pl.ds((slot // 2) * model, model), pl.ds((slot % 2) * chunk, chunk)], slot)
+
+    for slot in range(6):
+        fetch_first(slot).start()
     pl.semaphore_wait(barrier, devices - 1)
 
-    share_cot = Quad(p, r.cot, lambda k: r.gcot.at[k], lambda k: r.cot_sems.at[k])
-    share_mixed = QuadRows(p, r.mixed, r.xmix, r.row_sems.at[0])
-    share_n2 = QuadRows(p, r.normed2_rows, r.xn2, r.row_sems.at[1])
-    share_normed = QuadRows(p, r.normed, r.xnormed, r.row_sems.at[3])
-    share_joined = QuadRows(p, r.joined, r.xjoined, r.row_sems.at[4])
-
-    def share_act(c, what):
-        pair = chunk // 2
-        z = c // 2
-
-        def half(core):
-            return r.act_rows.at[c, pl.ds(pl.multiple_of(core * pair, pair), pair)]
-
-        def copy(core, k, to):
-            return remote(half(core), r.xact.at[k, z], r.act_sems.at[z, 2 * k - 1], r.act_sems.at[z, 2 * k], to)
-
-        own = pltpu.make_async_copy(half(p.c), r.xact.at[0, z], r.act_sems.at[z, 0])
-        mine = p.y == c % 2
-        if what == "start":
-
-            @pl.when(mine)
-            def _():
-                own.start()
-                copy(1 - p.c, 1, p.to_core).start()
-
-            @pl.when(p.y != c % 2)
-            def _():
-                copy(p.c, 2, p.to_y).start()
-                copy(1 - p.c, 3, p.to_far).start()
-
-        elif what == "arrived":
-
-            @pl.when(mine)
-            def _():
-                own.wait()
-                copy(1 - p.c, 1, p.to_core).wait_recv()
-                copy(p.c, 2, p.to_y).wait_recv()
-                copy(1 - p.c, 3, p.to_far).wait_recv()
-
-        else:
-            pl.when(mine)(lambda: copy(1 - p.c, 1, p.to_core).wait_send())
-
-            @pl.when(p.y != c % 2)
-            def _():
-                copy(p.c, 2, p.to_y).wait_send()
-                copy(1 - p.c, 3, p.to_far).wait_send()
-
-    share_branch = Quad(p, r.gbranch.at[0], lambda k: r.gbranch.at[k], lambda k: r.branch_sems.at[k])
-
-    def share_up(c):
-        return Quad(p, r.gup.at[0, c], lambda k: r.gup.at[k, c], lambda k: r.up_sems.at[c, k])
+    def to_sibling(src, dst, k):
+        return remote(src, dst, r.pair_sems.at[0, k], r.pair_sems.at[1, k], p.to_core)
+
+    pair_cot = to_sibling(r.cot_all, r.cot_sib, 0)
+    pair_n2 = to_sibling(r.n2_all, r.n2_sib, 1)
+    pair_act = to_sibling(r.act.at[1 - p.c], r.act_sib, 2)
+    pair_gin = to_sibling(r.gin.at[1 - p.c], r.gin_sib, 3)
+    plane_n2 = Plane(p, lambda q: r.n2_all.at[0], lambda q: r.n2_all.at[q], r.n2_sems.at[0], r.n2_sems.at[1])
+    plane_back = Plane(
+        p, lambda q: r.part_back.at[q - 1], lambda q: r.got_back.at[q - 1], r.back_sems.at[0], r.back_sems.at[1]
+    )
+    plane_total = Plane(
+        p, lambda q: r.part_total.at[q - 1], lambda q: r.got_total.at[q - 1], r.total_sems.at[0], r.total_sems.at[1]
+    )
+    share_mixed = QuadRows(p, 0, r.mixed, r.xmix, r.row_sems.at[0])
+    share_branch = Quad(p, 0, r.gbranch.at[0], lambda k: r.gbranch.at[k], lambda k: r.branch_sems.at[k])
 
     def share_late(c):
-        return Quad(p, r.gup.at[0, c], lambda k: r.gup.at[k, c], lambda k: r.late_sems.at[c, k])
-
-    share_cot.start()
-    share_mixed.start()
+        return Quad(p, c // 6, r.glate.at[0, c], lambda k: r.glate.at[k, c], lambda k: r.late_sems.at[c, k])
+
+    pair_cot.start()
 
     length = r.lengths[p.x]
     position = p.b * frames
@@ -1210,55 +1257,74 @@
     f_shift = kept * r.mods[3:4, :]
     mixed = r.mixed[...].reshape(model, frames).T
     for k in range(2):
-        fetch_out(k).wait()
+        fetch_first(k).wait()
         cols = pl.ds(k * chunk, chunk)
         r.middle[:, cols] = r.base[:, cols] + jnp.dot(mixed, r.weights[k], preferred_element_type=jnp.float32)
     hat, rstd = normal(r.middle[...])
-    normed2 = (hat * (1.0 + f_scale) + f_shift).astype(bf)
-    r.normed2[...] = normed2
-    r.normed2_rows[...] = normed2.T.reshape(r.normed2_rows.shape)
-    share_n2.start()
-    r.total[...] = jnp.zeros_like(r.total)
-    r.back[...] = jnp.zeros_like(r.back)
-    own_cot.wait()
-
-    @pl.loop(0, chunks)
-    def _(c):
-        fetch_up(c).wait()
-        fetch_down(c, 0).wait()
-        fetch_down(c, 1).wait()
-        up, down = r.weights.at[2 + c % 2], r.weights.at[4 + c % 2]
-        here = pl.ds(pl.multiple_of(c * chunk, chunk), chunk)
-        inner = jnp.dot(r.normed2[...], up[...], preferred_element_type=jnp.float32) + r.b_up[:, here]
-        cdf = 0.5 * (1.0 + lax.erf(inner * (0.5**0.5)))
-        act = (inner * cdf).astype(bf)
-        slope = cdf + inner * (jnp.exp(-0.5 * inner * inner) * (1.0 / math.sqrt(2.0 * math.pi)))
-        act_grad = nt(r.gcot[0, :, :half], down[:chunk, :]) + nt(r.gcot[0, :, half:], down[chunk:, :])
-        inner_grad = (act_grad * slope).astype(bf)
-        r.gup[0, c] = inner_grad
-        rows = chunk // 4
-        r.act_rows[c] = act.T
-        share_act(c, "start")
-        r.total[:, :half] += jnp.dot(act, down[:chunk, :], preferred_element_type=jnp.float32)
-        r.total[:, half:] += jnp.dot(act, down[chunk:, :], preferred_element_type=jnp.float32)
-        r.back[...] += nt(inner_grad, up[...])
-        bias = jnp.sum(inner_grad.astype(jnp.float32), 0, keepdims=True)
-        for k in range(4):
-            r.tiles[c * 4 + k, 0:1, :] = bias[:, k * rows : (k + 1) * rows]
-
-        @pl.when(c + 2 < chunks)
+    r.n2_all[0] = (hat * (1.0 + f_scale) + f_shift).astype(bf)
+    plane_n2.start()
+    r.bias[...] = jnp.zeros_like(r.bias)
+    for slot in range(2, 6):
+        fetch_first(slot).wait()
+
+    @pl.loop(0, 4)
+    def _(q):
+        pl.when(q > 0)(lambda: plane_n2.copy(q).wait_recv())
+        acts, grads = [], []
+        for u in range(2):
+            cols = pl.ds(u * chunk, chunk)
+            inner = jnp.dot(r.n2_all[q], r.weights[2 + u], preferred_element_type=jnp.float32) + r.b_up[:, cols]
+            cdf = 0.5 * (1.0 + lax.erf(inner * (0.5**0.5)))
+            act = (inner * cdf).astype(bf)
+            slope = cdf + inner * (jnp.exp(-0.5 * inner * inner) * (1.0 / math.sqrt(2.0 * math.pi)))
+            act_grad = nt(r.cot_all[q, :, :half], r.weights[4, cols, :]) + nt(
+                r.cot_all[q, :, half:], r.weights[5, cols, :]
+            )
+            grad = (act_grad * slope).astype(bf)
+            r.bias[:, cols] += jnp.sum(grad.astype(jnp.float32), 0, keepdims=True)
+            for k in range(4):
+                here = slice(k * 128, (k + 1) * 128)
+                at = (2 * u + k // 2) * 128
+                r.act[k % 2, q, :, at : at + 128] = act[:, here]
+                r.gin[k % 2, q, :, at : at + 128] = grad[:, here]
+            acts.append(act)
+            grads.append(grad)
+        back = nt(grads[0], r.weights[2]) + nt(grads[1], r.weights[3])
+
+        @pl.when(q == 0)
         def _():
-            fetch_up(c + 2).start()
-            fetch_down(c + 2, 0).start()
-            fetch_down(c + 2, 1).start()
-
+            r.back[...] = back
+
+        @pl.when(q > 0)
+        def _():
+            r.part_back[q - 1] = back.astype(bf)
+            plane_back.copy(q).start()
+
+        for k in range(2):
+            cols = slice(k * half, (k + 1) * half)
+            total = jnp.dot(acts[0], r.weights[4 + k, :chunk, :], preferred_element_type=jnp.float32)
+            total = total + jnp.dot(acts[1], r.weights[4 + k, chunk:, :], preferred_element_type=jnp.float32)
+
+            @pl.when(q == 0)
+            def _():
+                r.total[:, cols] = total
+
+            @pl.when(q > 0)
+            def _():
+                r.part_total[q - 1, :, cols] = total.astype(bf)
+
+    pair_n2.start()
+    pair_act.start()
+    pair_gin.start()
+    plane_back.arrived()
     middle = r.middle[...]
-    r.output[...] = (middle + r.total[...] + r.b_down[...]).astype(bf)
     hat, rstd = normal(middle)
     grad = r.back[...]
-    cot = r.gcot[0].astype(jnp.float32)
+    for k in range(3):
+        grad = grad + r.got_back[k].astype(jnp.float32)
+    cot = r.cot_all[0].astype(jnp.float32)
     middle_grad = cot + normal_back(grad, hat, rstd, f_scale)
-    r.middle[...] = middle_grad
+    r.back[...] = middle_grad
     branch_grad = middle_grad.astype(bf)
     r.gbranch[0] = branch_grad
     there = Exchange(p, count, r.mixed_grad, r.got, r.s1, r.r1, r.o1)
@@ -1266,44 +1332,95 @@
     mixed_grad = nt(r.weights[0], branch_grad[:, :half]) + nt(r.weights[1], branch_grad[:, half:])
     r.mixed_grad[...] = (mixed_grad.astype(bf) * kept_row.astype(bf)).reshape(r.mixed_grad.shape)
     there.start()
-    for c in range(6):
-        share_up(c).start()
-    for k in range(6):
-        fetch_qkv(k).start()
-    f_scale_grad = jnp.sum(kept * grad * hat, 0, keepdims=True)
-    f_shift_grad = jnp.sum(kept * grad, 0, keepdims=True)
-    r.pack[:, 256:384] = fold(f_scale_grad)
-    r.pack[:, 384:512] = fold(f_shift_grad)
-
-    def columns_of(ref):
-        def take(j):
-            here = pl.ds(pl.multiple_of(j * chunk, chunk), chunk)
-            return jnp.concatenate([ref[k, :, here] for k in range(4)], 0)
-
-        return take
+    plane_total.start()
+    share_mixed.start()
+    share_branch.start()
+    for slot in range(6):
+        fetch_qkv(slot).start()
+    r.vectors[2:3, :] = jnp.sum(kept * grad * hat, 0, keepdims=True)
+    r.vectors[3:4, :] = jnp.sum(kept * grad, 0, keepdims=True)
 
     def blocks_of(first):
-        return lambda j: jnp.concatenate([r.gup[k, first + j] for k in range(4)], 0)
-
-    sums = {}
-    given = (
-        ("up", r.xn2, blocks_of(0), r.up_grad),
-        ("down", r.xact, columns_of(r.gcot), r.down_grad),
-        ("out", r.xmix, columns_of(r.gbranch), r.out_grad),
-        ("qkv", r.xnormed, blocks_of(0), r.qkv_grad),
-        ("skip", r.xjoined, blocks_of(chunks), r.skip_grad),
-    )
-    full = {}
-    for (name, x, take, out), (rows, cols, parts) in zip(given, shards):
+        return lambda j: jnp.concatenate([r.glate[k, first + j] for k in range(4)], 0)
+
+    def branch_columns(j):
+        here = pl.ds(pl.multiple_of(j * chunk, chunk), chunk)
+        return jnp.concatenate([r.gbranch[k, :, here] for k in range(4)], 0)
+
+    def tn(left, right):
+        return lax.dot_general(left, right, (((0,), (0,)), ((), ())), preferred_element_type=jnp.float32)
+
+    def flat(v):
+        return v.reshape(4 * frames, v.shape[2])
+
+    def down_part(k):
+        cols = slice(k * half, (k + 1) * half)
+
+        def make(j):
+            mine = tn(flat(r.act[p.c]), flat(r.cot_all[:, :, cols]))
+            return mine + tn(flat(r.act_sib[...]), flat(r.cot_sib[:, :, cols]))
+
+        return make
+
+    def up_part(k):
+        cols = slice(k * 256, (k + 1) * 256)
+
+        def make(j):
+            mine = tn(flat(r.n2_all[...]), flat(r.gin[p.c, :, :, cols]))
+            return mine + tn(flat(r.n2_sib[...]), flat(r.gin_sib[:, :, cols]))
+
+        return make
+
+    down, up, out, qkv, skip = [], [], [], [], []
+    group = model // depth
+    for k in range(2):
+        down.append(LineReduce(p, down_part(k), units // (2 * depth), half, *rest[:5]))
+        rest = rest[5:]
+    for k in range(2):
+        up.append(LineReduce(p, up_part(k), group, 256, *rest[:5]))
+        rest = rest[5:]
+    for sums, axis, x, take, res, (rows, cols, parts) in (
+        (out, 0, r.xmix, branch_columns, r.out_grad, shards[0]),
+        (qkv, 0, r.xnormed, blocks_of(0), r.qkv_grad, shards[1]),
+        (skip, 1, r.xjoined, blocks_of(6), r.skip_grad, shards[2]),
+    ):
         width = cols // parts
-        sums[name] = []
         for k in range(parts):
-            if name in ("up", "down", "out"):
-                full[name, k] = rest.pop(0)
-            mine = full[{"qkv": "up", "skip": "down"}.get(name, name), k]
-            sums[name].append(Reduce(p, x, take, rows, k * width, width, out, mine, *rest[:4]))
-            rest = rest[4:]
-    up, down, out, qkv, skip = (sums[name] for name in ("up", "down", "out", "qkv", "skip"))
+            sums.append(Reduce(p, axis, x, take, rows, k * width, width, res, *rest[:5]))
+            rest = rest[5:]
+
+    def end_down(k):
+        def write(here, total):
+            r.down_grad[:, pl.ds(pl.multiple_of(k * half + here.start, 128), here.size)] = total
+
+        down[k].end(write)
+
+    def end_up(k):
+        def write(here, total):
+            r.up_out[:, :, k * 256 : (k + 1) * 256] = total.astype(bf).reshape(8, group // 8, 256)
+
+        up[k].end(write)
+
+    own_slot = p.y * 4 + p.c * 2 + p.x
+
+    def up_copy(k):
+        to = (own_slot + k) % 8
+        device = (p.z * 4 + to // 2, to % 2)
+        return remote(r.up_out.at[to], r.up_got.at[own_slot], r.up_sems.at[0, k], r.up_sems.at[1, k], device)
+
+    def up_spread():
+        for k in range(1, 8):
+            up_copy(k).start()
+        r.up_got[own_slot] = r.up_out[own_slot]
+
+    def up_arrived():
+        for k in range(1, 8):
+            came = r.up_got.at[(own_slot + 8 - k) % 8]
+            remote(came, came, r.up_sems.at[0, k], r.up_sems.at[1, k], p.to_x).wait_recv()
+        for t in range(8):
+            for z in range(depth):
+                at = (z * 8 + t) * 128
+                r.up_grad[:, at : at + 128] = r.up_got[t, :, z * 128 : (z + 1) * 128].astype(jnp.float32)
 
     def ready(shares):
         for share in shares:
@@ -1312,46 +1429,44 @@
         for share in shares:
             share.arrived()
 
-    blocks = 2048 // 256
+    blocks = r.qkv.shape[1] // 256
     attend_back_open(p, r.lengths, r.qkv, r.keys, r.values, r.kv_sums)
-    for c in range(chunks):
-        share_act(c, "arrived")
-    ready([share_cot])
+    pair_cot.wait_recv()
+    pair_act.wait_recv()
     down[0].begin()
+    down[0].hop(0)
     down[1].begin()
     there.arrived()
     attend = functools.partial(
         attend_back, r.got, r.qkv, r.lse, r.plain, r.keys, r.values, r.kv_sums, r.grads_out, 256
     )
     attend(0, blocks // 2)
-    ready([share_n2, share_up(0), share_up(1)])
-    up[0].begin()
-    down[0].hop(0)
+    down[0].hop(1)
+    down[1].hop(0)
     attend(blocks // 2, blocks)
     attend_back_close(r.kv_sums, r.grads_out)
-    ready([share_up(2), share_up(3)])
-    up[1].begin()
-    ready([share_up(4), share_up(5)])
-    up[2].begin()
-    for c in range(6):
-        share_up(c).finish()
     back.start()
-    share_up(6).start()
-    share_up(7).start()
-    share_branch.start()
-    share_normed.start()
-    share_joined.start()
-    down[0].hop(1)
-    down[1].hop(0)
-    up[0].hop(0)
+    plane_total.arrived()
+    total = r.middle[...] + r.total[...] + r.b_down[...]
+    for k in range(3):
+        total = total + r.got_total[k].astype(jnp.float32)
+    r.output[...] = total.astype(bf)
     down[0].hop(2)
     down[1].hop(1)
+    pair_n2.wait_recv()
+    pair_gin.wait_recv()
+    up[0].begin()
+    up[0].hop(0)
+    end_down(0)
+    down[1].hop(2)
+    up[1].begin()
+    up[0].hop(1)
     up[1].hop(0)
-    ready([share_up(6), share_up(7)])
-    up[3].begin()
-    up[0].hop(1)
-    down[0].end()
-    down[1].hop(2)
+    ready([share_mixed, share_branch])
+    out[0].begin()
+    end_down(1)
+    up[0].hop(2)
+    up[1].hop(1)
 
     back.arrived()
 
@@ -1369,214 +1484,262 @@
             h = r.got_grads[:, 2 * HEAD_DIM :, :]
         h = h.reshape(model, frames).T
         for k in range(2):
-            r.gup[0, 2 * part + k] = h[:, k * chunk : (k + 1) * chunk]
+            r.glate[0, 2 * part + k] = h[:, k * chunk : (k + 1) * chunk]
             share_late(2 * part + k).start()
     for k in range(6):
         fetch_qkv(k).wait()
-        made = nt(r.gup[0, k], r.weights[k])
+        made = nt(r.glate[0, k], r.weights[k])
         if k == 0:
-            r.back[...] = made
+            r.total[...] = made
         else:
-            r.back[...] += made
+            r.total[...] += made
     for k in range(4):
         fetch_skip(k).start()
     hat, rstd = normal(r.base[...])
-    grad = r.back[...]
-    base_grad = (r.middle[...] + normal_back(grad, hat, rstd, a_scale)).astype(bf)
+    grad = r.total[...]
+    base_grad = (r.back[...] + normal_back(grad, hat, rstd, a_scale)).astype(bf)
     for k in range(2):
-        r.gup[0, chunks + k] = base_grad[:, k * chunk : (k + 1) * chunk]
-        share_late(chunks + k).start()
-    r.pack[:, 0:128] = fold(jnp.sum(kept * grad * hat, 0, keepdims=True))
-    r.pack[:, 128:256] = fold(jnp.sum(kept * grad, 0, keepdims=True))
-    bias_down = jnp.sum(cot, 0, keepdims=True)
-    bias_skip = jnp.sum(base_grad.astype(jnp.float32), 0, keepdims=True)
-    each = model // devices
-    for k in range(devices):
-        r.tiles[k, 1:2, :each] = bias_down[:, k * each : (k + 1) * each]
-        r.tiles[k, 1:2, each : 2 * each] = bias_skip[:, k * each : (k + 1) * each]
-    packs = Tiles(p, r.pack, r.pack_full, r.s3, r.r3, False)
-    tiles = Tiles(p, r.tiles, r.tiles_full, r.s4, r.r4, True)
-    times = Tiles(p, r.time_tile, r.times_full, r.s5, r.r5, False)
-    packs.start()
-    tiles.start()
+        r.glate[0, 6 + k] = base_grad[:, k * chunk : (k + 1) * chunk]
+        share_late(6 + k).start()
+    r.vectors[0:1, :] = jnp.sum(kept * grad * hat, 0, keepdims=True)
+    r.vectors[1:2, :] = jnp.sum(kept * grad, 0, keepdims=True)
+
+    r.vectors[4:5, :] = jnp.sum(cot, 0, keepdims=True)
+    r.vectors[5:6, :] = jnp.sum(base_grad.astype(jnp.float32), 0, keepdims=True)
+    r.vectors[6:7, :] = r.bias[...]
+    r.vectors[7:8, :] = jnp.zeros((1, model), jnp.float32)
+    small = Rounds(p, r.small_sems.at[0], r.small_sems.at[1])
+
+    def small_core():
+        return small.one(0, r.vectors, r.small_got.at[0], p.to_core)
+
+    def small_line(d):
+        return small.one(d, r.line_out, r.small_got.at[d], small.line(0, d))
+
+    def small_y():
+        return small.one(4, r.y_out, r.small_got.at[4], p.to_y)
+
+    def small_x():
+        return small.one(5, r.x_out, r.small_got.at[5], p.to_x)
+
+    def after_core():
+        small_core().wait_recv()
+        r.line_out[...] = r.vectors[...] + r.small_got[0]
+        for d in range(1, depth):
+            small_line(d).start()
+
+    def after_line():
+        total = r.line_out[...]
+        for d in range(1, depth):
+            small_line(d).wait_recv()
+            total = total + r.small_got[d]
+        r.y_out[...] = total
+        small_y().start()
+
+    def after_y():
+        small_y().wait_recv()
+        r.x_out[...] = r.y_out[...] + r.small_got[4]
+        small_x().start()
+
+    small_core().start()
+
+    def times_block(size):
+        number = p.b * 2 + p.x
+        return r.times_full.at[pl.ds(number // size * size, size)]
+
+    def times_copy(k, size, to):
+        return small.one(6 + k, times_block(size), times_block(size), to)
+
+    def times_step(k):
+        return times_copy(k, 1 << k, (p.to_x, p.to_core, p.to_y)[k])
+
+    def times_line(d):
+        return times_copy(2 + d, 8, small.line(0, d))
+
     for i in range(2):
         total = None
         for j in range(2):
             fetch_skip(2 * i + j).wait()
-            made = nt(r.gup[0, chunks + j], r.weights[2 * i + j])
+            made = nt(r.glate[0, 6 + j], r.weights[2 * i + j])
             total = made if total is None else total + made
         r.joined_grad[i] = total.astype(bf)
 
-    ready([share_mixed, share_branch])
-    out[0].begin()
-    down[1].end()
-    up[0].hop(2)
-    up[1].hop(1)
-    up[2].hop(0)
-    ready([share_normed, share_late(0), share_late(1)])
-    up[0].end()
+    after_core()
+    end_up(0)
     up[1].hop(2)
-    up[2].hop(1)
-    up[3].hop(0)
+    out[0].hop(0)
+    ready([share_late(0), share_late(1)])
     qkv[0].begin()
-    up[1].end()
-    up[2].hop(2)
-    up[3].hop(1)
-    out[0].hop(0)
+    end_up(1)
+    up_spread()
+    after_line()
+    out[0].hop(1)
+    ready([share_late(6), share_late(7)])
+    skip[0].begin()
+    after_y()
     ready([share_late(2), share_late(3)])
     qkv[1].begin()
-    up[2].end()
-    up[3].hop(2)
-    out[0].hop(1)
     qkv[0].hop(0)
+    skip[1].begin()
+    out[0].hop(2)
+    up_arrived()
+
+    small_x().wait_recv()
+    mine, other = r.x_out[...], r.small_got[5]
+    first, second = jnp.where(p.x == 0, mine, other), jnp.where(p.x == 0, other, mine)
+    total = jnp.zeros((8, r.w_mod.shape[0]), jnp.float32)
+    turned = r.times[...].T
+    share = r.w_mod.shape[0]
+    for part in range(4):
+        values = [first[part : part + 1, :], second[part : part + 1, :]]
+        here = pl.ds(part * model, model)
+        left = extra_rows([*three_terms(values[0]), *three_terms(values[1])], 8, model)
+        total = total + nt(left, r.w_mod[:, here])
+        r.mod_grad[:, here] = turned[:share, 0:1] * values[0] + turned[:share, 4:5] * values[1]
+    made = jnp.concatenate(
+        [total[0:1] + total[1:2] + total[2:3], total[3:4] + total[4:5] + total[5:6], jnp.zeros((6, share), jnp.float32)]
+    )
+    number = p.b * 2 + p.x
+    r.times_full[number] = jnp.concatenate([made, jnp.zeros((8, 128 - share), jnp.float32)], 1)
+    times_step(0).start()
+    r.sums_out[...] = jnp.zeros_like(r.sums_out)
+    at = pl.multiple_of((p.z * 2 + p.c) * 128, 128)
+    r.sums_out[0:1, :] = r.y_out[6:7, pl.ds(at, 128)]
+    at = pl.multiple_of(number // 4 * 128, 128)
+    near = r.x_out[4:6, pl.ds(at, 128)] + r.small_got[5, 4:6, pl.ds(at, 128)]
+    each = model // devices
+    own = near[:, :each]
+    for k in range(1, 4):
+        own = jnp.where(number % 4 == k, near[:, k * each : (k + 1) * each], own)
+    r.sums_out[1:2, :each] = own[0:1]
+    r.sums_out[1:2, each : 2 * each] = own[1:2]
+
     ready([share_late(4), share_late(5)])
     qkv[2].begin()
-    up[3].end()
-    out[0].hop(2)
     qkv[0].hop(1)
     qkv[1].hop(0)
-    ready([share_joined, share_late(chunks), share_late(chunks + 1)])
-    skip[0].begin()
-    skip[1].begin()
+    skip[0].hop(0)
     out[0].end()
+    times_step(0).wait_recv()
+    times_step(1).start()
     qkv[0].hop(2)
     qkv[1].hop(1)
     qkv[2].hop(0)
-
-    packs.arrived()
-    rows = [jnp.zeros(r.pack.shape, jnp.float32) for _ in range(2)]
-    for k in range(devices):
-        rows[k % 2] = rows[k % 2] + r.pack_full[k]
-    total = jnp.zeros((8, r.w_mod.shape[0]), jnp.float32)
-    columns = r.times[...].T
-    share = r.w_mod.shape[0]
-    width = model // 8
-    for part in range(4):
-        for k in range(8):
-            values = [rows[s][k : k + 1, part * width : (part + 1) * width] for s in range(2)]
-            here = pl.ds(part * model + k * width, width)
-            left = extra_rows([*three_terms(values[0]), *three_terms(values[1])], 8, width)
-            total = total + nt(left, r.w_mod[:, here])
-            r.mod_grad[:, here] = columns[:share, 0:1] * values[0] + columns[:share, 4:5] * values[1]
-    first = total[0:1] + total[1:2] + total[2:3]
-    second = total[3:4] + total[4:5] + total[5:6]
-    made = jnp.concatenate([first, second, jnp.zeros((6, share), jnp.float32)], 0)
-    r.time_tile[...] = jnp.concatenate([made, jnp.zeros((8, 128 - share), jnp.float32)], 1)
-    times.start()
+    skip[0].hop(1)
+    skip[1].hop(0)
+    times_step(1).wait_recv()
+    times_step(2).start()
     qkv[0].end()
     qkv[1].hop(2)
     qkv[2].hop(1)
-    skip[0].hop(0)
-    skip[1].hop(0)
-    tiles.arrived()
-    total = r.tiles_full[0]
-    for k in range(1, devices):
-        total = total + r.tiles_full[k]
-    r.sums_out[...] = total
+    skip[0].hop(2)
+    skip[1].hop(1)
+    times_step(2).wait_recv()
+    for d in range(1, depth):
+        times_line(d).start()
     qkv[1].end()
     qkv[2].hop(2)
-    skip[0].hop(1)
-    skip[1].hop(1)
+    skip[0].end()
+    skip[1].hop(2)
     qkv[2].end()
-    skip[0].hop(2)
-    skip[1].hop(2)
-    skip[0].end()
     skip[1].end()
-    times.arrived()
-    for group in sums.values():
-        for one in group:
-            one.finish()
-    for share in (share_cot, share_mixed, share_n2, share_normed, share_joined, share_branch):
-        share.finish()
-    for c in range(chunks):
-        share_act(c, "sent")
-    for c in (6, 7):
-        share_up(c).finish()
-    for c in [*range(6), chunks, chunks + 1]:
+    for d in range(1, depth):
+        times_line(d).wait_recv()
+    for one in [*down, *up, *out, *qkv, *skip, share_mixed, share_branch, plane_n2, plane_back, plane_total]:
+        one.finish()
+    for c in range(8):
         share_late(c).finish()
-    for one in (there, back, packs, tiles, times):
+    for k in range(1, 8):
+        up_copy(k).wait_send()
+    for one in (pair_cot, pair_n2, pair_act, pair_gin):
+        one.wait_send()
+    for one in (there, back):
         one.finish()
-
-
-def in_slices(x, depth):
-    return x.reshape(depth, x.shape[0] // depth, x.shape[1])
+    for d in range(1, depth):
+        small_line(d).wait_send()
+        times_line(d).wait_send()
+    for k in range(3):
+        times_step(k).wait_send()
+    for one in (small_core(), small_y(), small_x()):
+        one.wait_send()
 
 
 def back_call(depth, devices, args):
     base, qkv = args["base"], args["qkv"]
     frames, model = base.shape
     count = devices // 2
-    ff = args["w_up"].shape[1]
+    units = args["w_up"].shape[1]
+    ff = units * 4
     bf, f32 = jnp.bfloat16, jnp.float32
     share = args["w_mod"].shape[0]
+    dma = pltpu.SemaphoreType.DMA
+    sum_scratch = []
+    for rows, width in [(units // (2 * depth), model // 2)] * 2 + [(model // depth, 256)] * 2:
+        sum_scratch.append(pltpu.VMEM((depth * rows, width), f32))
+        sum_scratch += LineReduce.scratch(rows, width, depth)
     shards = [
-        (model // devices, ff, 4),
-        (ff // devices, model, 2),
         (model // devices, model, 1),
         (model // devices, 3 * model, 3),
         (2 * model // devices, model, 2),
     ]
-    sum_scratch = []
-    for which, (rows, cols, parts) in enumerate(shards):
+    for rows, cols, parts in shards:
         for _ in range(parts):
-            if which < 3:
-                sum_scratch.append(pltpu.VMEM((depth * rows, cols // parts), f32))
+            sum_scratch.append(pltpu.VMEM((depth * rows, cols // parts), f32))
             sum_scratch += Reduce.scratch(rows, cols // parts, depth)
-    chunks = ff // 512
-    dma = pltpu.SemaphoreType.DMA
-
-    def rows(n):
-        return pltpu.VMEM((4, depth, n // (4 * depth), frames), bf)
+
+    def tall(n, *shape, kind=bf):
+        return pltpu.VMEM((n, *shape), kind)
 
     scratch = dict(
-        wide=pltpu.VMEM((8, 128), f32),
-        weights=pltpu.VMEM((6, model, 512), bf),
-        middle=pltpu.VMEM((frames, model), f32),
-        total=pltpu.VMEM((frames, model), f32),
-        back=pltpu.VMEM((frames, model), f32),
-        normed2=pltpu.VMEM((frames, model), bf),
-        normed2_rows=pltpu.VMEM((depth, model // depth, frames), bf),
-        act_rows=pltpu.VMEM((chunks, 512, frames), bf),
-        gcot=pltpu.VMEM((4, frames, model), bf),
-        gup=pltpu.VMEM((4, chunks + 2, frames, 512), bf),
-        gbranch=pltpu.VMEM((4, frames, model), bf),
-        xact=rows(ff),
-        xmix=rows(model),
-        xn2=rows(model),
-        xnormed=rows(model),
-        xjoined=rows(2 * model),
-        mixed_grad=pltpu.VMEM((count, HEAD_DIM, frames), bf),
-        got=pltpu.VMEM((count, HEAD_DIM, frames), bf),
-        keys=pltpu.VMEM((qkv.shape[1], 2 * HEAD_DIM), bf),
-        values=pltpu.VMEM((qkv.shape[1], 2 * HEAD_DIM), bf),
-        kv_sums=pltpu.VMEM((qkv.shape[1], 2 * HEAD_DIM), f32),
-        grads_out=pltpu.VMEM((count, 3 * HEAD_DIM, frames), bf),
-        got_grads=pltpu.VMEM((count, 3 * HEAD_DIM, frames), bf),
-        pack=pltpu.VMEM((8, 512), f32),
-        pack_full=pltpu.VMEM((devices, 8, 512), f32),
-        tiles=pltpu.VMEM((devices, 8, 128), f32),
-        tiles_full=pltpu.VMEM((devices, 8, 128), f32),
-        time_tile=pltpu.VMEM((8, 128), f32),
-        weight_sems=dma((8,)),
-        row_sems=dma((5, 7)),
-        act_sems=dma((depth, 7)),
-        cot_sems=dma((6,)),
-        up_sems=dma((chunks, 6)),
+        weights=tall(6, model, 512),
+        middle=tall(frames, model, kind=f32),
+        total=tall(frames, model, kind=f32),
+        back=tall(frames, model, kind=f32),
+        bias=tall(1, units, kind=f32),
+        vectors=tall(8, model, kind=f32),
+        n2_all=tall(4, frames, model),
+        n2_sib=tall(4, frames, model),
+        cot_sib=tall(4, frames, model),
+        act=tall(2, 4, frames, units // 2),
+        gin=tall(2, 4, frames, units // 2),
+        act_sib=tall(4, frames, units // 2),
+        gin_sib=tall(4, frames, units // 2),
+        part_back=tall(3, frames, model),
+        got_back=tall(3, frames, model),
+        part_total=tall(3, frames, model),
+        got_total=tall(3, frames, model),
+        up_out=tall(8, model // devices, units // 2),
+        up_got=tall(8, model // devices, units // 2),
+        gbranch=tall(4, frames, model),
+        glate=tall(4, 8, frames, 512),
+        xmix=tall(4, depth, 2, model // devices, frames),
+        mixed_grad=tall(count, HEAD_DIM, frames),
+        got=tall(count, HEAD_DIM, frames),
+        keys=tall(qkv.shape[1], 2 * HEAD_DIM),
+        values=tall(qkv.shape[1], 2 * HEAD_DIM),
+        kv_sums=tall(qkv.shape[1], 2 * HEAD_DIM, kind=f32),
+        grads_out=tall(count, 3 * HEAD_DIM, frames),
+        got_grads=tall(count, 3 * HEAD_DIM, frames),
+        small_got=tall(6, 8, model, kind=f32),
+        line_out=tall(8, model, kind=f32),
+        y_out=tall(8, model, kind=f32),
+        x_out=tall(8, model, kind=f32),
+        weight_sems=dma((6,)),
+        pair_sems=dma((2, 4)),
+        n2_sems=dma((2, 4)),
+        back_sems=dma((2, 4)),
+        total_sems=dma((2, 4)),
+        up_sems=dma((2, 8)),
+        row_sems=dma((1, 7)),
         branch_sems=dma((6,)),
-        late_sems=dma((chunks + 2, 6)),
+        late_sems=dma((8, 6)),
         s1=dma((count,)),
         r1=dma((count,)),
         o1=dma,
         s2=dma((count,)),
         r2=dma((count,)),
         o2=dma,
-        s3=dma((devices,)),
-        r3=dma((devices,)),
-        s4=dma((devices,)),
-        r4=dma((devices,)),
-        s5=dma((devices,)),
-        r5=dma((devices,)),
-        own_sems=dma((1,)),
+        small_sems=dma((2, 12)),
     )
     shape = jax.ShapeDtypeStruct
     outs = dict(
@@ -1591,40 +1754,26 @@
         sums_out=shape((8, 128), f32),
         times_full=shape((devices, 8, 128), f32),
     )
+    names = [*args, *outs, *scratch]
+    vmem = pl.BlockSpec(memory_space=pltpu.VMEM)
+    specs = dict.fromkeys(args, vmem)
+    specs["lengths"] = pl.BlockSpec(memory_space=pltpu.SMEM)
+    for name in ("w_out", "w_up", "w_down", "w_qkv", "w_skip"):
+        specs[name] = pl.BlockSpec(memory_space=pl.ANY)
     made = pl.pallas_call(
-        functools.partial(back_kernel, depth, shards),
+        functools.partial(back_kernel, depth, shards, names),
         name="back",
-        out_shape=[outs[name] for name in BACK_OUT],
-        in_specs=[pl.BlockSpec(memory_space=pltpu.SMEM)] + in_vmem(11) + in_any(1) + in_vmem(1) + in_any(7),
-        out_specs=in_vmem(len(BACK_OUT)),
-        scratch_shapes=[scratch[name] for name in BACK_SCRATCH] + sum_scratch,
+        out_shape=list(outs.values()),
+        in_specs=list(specs.values()),
+        out_specs=[vmem] * len(outs),
+        scratch_shapes=list(scratch.values()) + sum_scratch,
         compiler_params=kernel_params(3),
-    )(*[args[name] for name in BACK_IN])
-    return dict(zip(BACK_OUT, made))
-
-
-FRONT_IN = (
-    ["lengths", "time_row", "b_skip", "b_up_part", "b_down_part", "w_mod", "cosine", "sine", "hidden", "skip_in"]
-    + ["w_skip", "w_qkv", "w_out", "w_up", "w_down"]
-)
-FRONT_OUT = (
-    ["skip_full", "qkv_full", "out_full", "up_full", "down_full", "mixed"]
-    + ["times", "mods", "b_up", "b_down", "base", "normed", "joined", "qkv", "lse", "plain"]
-)
-FRONT_SCRATCH = (
-    ["own_time", "other_time", "got_time", "pack", "pack_full", "skip_here", "qkv_here", "heads_in", "got", "keys", "values", "mixed_out"]
-    + ["time_sems", "load_sems", "own_sems", "sends", "recvs", "s1", "r1", "o1", "s2", "r2", "o2"]
-)
-
-
-class Refs:
-    def __init__(self, names, refs):
-        for name, ref in zip(names, refs):
-            setattr(self, name, ref)
-
-
-def front_kernel(depth, cuts, *refs):
-    r = Refs(FRONT_IN + FRONT_OUT + FRONT_SCRATCH, refs)
+    )(*args.values())
+    return dict(zip(outs, made))
+
+
+def front_kernel(depth, cuts, names, *refs):
+    r = Refs(names, refs)
     p = Place(depth)
     count = 4 * depth
     devices = 2 * count
@@ -1641,7 +1790,7 @@
             picked = jnp.where(slot == k, part[:, k * share : (k + 1) * share], picked)
         picked = jnp.concatenate([picked, jnp.zeros((1, 128 - share), jnp.float32)], 1)
         ref[...] = jnp.where(mark, picked, 0.0)
-    greet_plane(p, count)
+    greet_plane(p, count, (p.to_across, p.to_far_x))
     ask = remote(r.other_time, r.got_time, r.time_sems.at[0], r.time_sems.at[1], p.to_x)
     ask.start()
 
@@ -1652,8 +1801,6 @@
         ("skip", r.w_skip, r.skip_full),
         ("qkv", r.w_qkv, r.qkv_full),
         ("out", r.w_out, r.out_full),
-        ("up", r.w_up, r.up_full),
-        ("down", r.w_down, r.down_full),
     ):
         groups[name] = []
         for lo, hi, first in ranges(src.shape[1], src.shape[1] // cuts[name] if cuts[name] else 0):
@@ -1666,6 +1813,42 @@
         p, r.pack, r.pack_full, 8, 0, r.pack.shape[1], False, False, r.sends.at[number], r.recvs.at[number]
     )
     number += 1
+    units = 2 * depth * 128
+
+    def spread_up():
+        for q in range(4):
+            y, x = (p.y + q // 2) % 2, (p.x + q % 2) % 2
+            for z in range(depth):
+                for c in range(2):
+                    cols = pl.ds(pl.multiple_of(p.shard(z, y, c, x) * 128, 128), 128)
+                    r.up_out[q, :, (z * 2 + c) * 128 : (z * 2 + c + 1) * 128] = r.w_up[:, cols]
+        r.up_mid[p.y, pl.ds(pl.multiple_of(p.x * rows_up, rows_up), rows_up), :] = r.up_out[0]
+        plane_up.start()
+
+    rows_up = r.w_up.shape[0]
+    plane_up = Plane(
+        p,
+        lambda q: r.up_out.at[q],
+        lambda q: r.up_mid.at[p.y, pl.ds(pl.multiple_of(p.x * rows_up, rows_up), rows_up)],
+        r.up_sems.at[0],
+        r.up_sems.at[1],
+    )
+    plane_cot = Plane(p, lambda q: r.cot, lambda q: r.cot_all.at[q], r.cot_sems.at[0], r.cot_sems.at[1])
+    line_up = LineGather(p, r.up_mid, lambda z, c: r.up_here.at[z, :, c], r.line_sems.at[0], r.line_sems.at[1])
+    line_down = LineGather(p, r.w_down, lambda z, c: r.down_here.at[z, c], r.line_sems.at[2], r.line_sems.at[3])
+    lines = (line_up, line_down)
+    own_up = pltpu.make_async_copy(r.up_mid, r.up_here.at[p.z, :, p.c], r.own_sems.at[3])
+    own_down = pltpu.make_async_copy(r.w_down, r.down_here.at[p.z, p.c], r.own_sems.at[4])
+    own_cot = pltpu.make_async_copy(r.cot, r.cot_all.at[0], r.own_sems.at[5])
+    share_joined = QuadRows(p, 1, r.joined, r.xjoined, r.row_sems.at[0])
+    share_normed = QuadRows(p, 0, r.normed, r.xnormed, r.row_sems.at[1])
+
+    def lines_own():
+        plane_up.arrived()
+        own_up.start()
+        for line in lines:
+            line.own()
+
     there = Exchange(p, count, r.heads_in, r.got, r.s1, r.r1, r.o1)
     back = Exchange(p, count, r.mixed_out, r.mixed, r.s2, r.r2, r.o2)
 
@@ -1690,9 +1873,8 @@
 
     def turned_inputs():
         half = depth // 2
-        rows = 2 * model // depth
         for k, ref in enumerate((r.hidden, r.skip_in)):
-            r.joined[k * half : (k + 1) * half] = ref[...].T.reshape(half, rows, frames)
+            r.joined[k * half : (k + 1) * half] = ref[...].T.reshape(half, *r.joined.shape[1:])
 
     def load_skip():
         return pltpu.make_async_copy(r.skip_full, r.skip_here, r.load_sems.at[0])
@@ -1706,15 +1888,10 @@
         for g in groups[name]:
             g.shared()
 
-    def begin_loads():
+    def first_norm():
         own_copies[0].wait()
         complete("skip")
         load_skip().start()
-        own_copies[1].wait()
-        complete("qkv")
-        load_qkv().start()
-
-    def first_norm():
         at = pl.multiple_of(p.shard(p.z, p.y, p.c, p.x) * 8, 8)
         r.pack_full[pl.ds(at, 8), :] = r.pack[...]
         packs.shared()
@@ -1726,8 +1903,11 @@
         r.mods[4:8, :] = mods
         each = model // devices
         tiles = [r.pack_full[k * 8 : k * 8 + 2, model:] for k in range(devices)]
-        for k in range(devices):
-            r.b_up[:, k * 128 : (k + 1) * 128] = tiles[k][0:1]
+        for z in range(depth):
+            for c in range(2):
+                at = pl.multiple_of(p.shard(z, p.y, c, p.x) * 8, 8)
+                here = (z * 2 + c) * 128
+                r.b_up[:, here : here + 128] = r.pack_full[pl.ds(at, 8), model:][0:1]
         b_skip = jnp.concatenate([t[1:2, :each] for t in tiles], 1)
         r.b_down[...] = jnp.concatenate([t[1:2, each : 2 * each] for t in tiles], 1)
         length = r.lengths[p.x]
@@ -1739,6 +1919,14 @@
         hat, _ = normal(base)
         normed = (hat * (1.0 + kept * mods[0:1]) + kept * mods[1:2]).astype(bf)
         r.normed[...] = normed.T.reshape(r.normed.shape)
+        r.normed_here[...] = normed
+
+    def projections():
+        own_copies[1].wait()
+        complete("qkv")
+        load_qkv().start()
+        share_normed.start()
+        normed = r.normed_here[...]
         load_qkv().wait()
         cosine, sine = r.cosine[...][None], r.sine[...][None]
         for part in range(3):
@@ -1767,66 +1955,96 @@
 
     events = []
     for k, name in enumerate(("skip", "qkv")):
-        events += [(t, k, f) for g in groups[name] for t, f in g.steps()]
+        events += [(t + 1.5 * k, k, f) for g in groups[name] for t, f in g.steps()]
     events.append((0.3, 0, products))
     events.append((0.35, 0, turned_inputs))
+    events.append((0.36, 0, spread_up))
     events += [(t + 0.5, 9, f) for t, f in packs.steps()]
-    for k, name in enumerate(("out", "up", "down")):
-        for g in groups[name]:
-            events += [((4.05 if t == 0 else 4.7 + t), k + 2, f) for t, f in g.steps()]
-    events.append((5.6, 0, begin_loads))
-    events.append((5.65, 0, first_norm))
-    events.append((6.9, 0, first_half))
-    events.append((7.9, 0, second_half))
+    events.append((3.2, 5, lines_own))
+    for g in groups["out"]:
+        events += [((5.56 if t == 0 else 6.2 + t), 2, f) for t, f in g.steps()]
+    for k, line in enumerate(lines):
+        events.append((5.55, 5 + k, functools.partial(line.line, 1)))
+        events.append((8.72, 5 + k, functools.partial(line.line, 2)))
+        events.append((9.6, 5 + k, functools.partial(line.line, 3)))
+    events.append((5.6, 0, first_norm))
+    events.append((5.65, 0, plane_cot.start))
+    events.append((5.66, 0, share_joined.start))
+    events.append((7.1, 0, projections))
+    events.append((8.4, 0, first_half))
+    events.append((9.4, 0, second_half))
     events.sort(key=lambda e: (e[0], e[1]))
+    own_down.start()
+    own_cot.start()
     own_copies += keep_own(p, owns, r.own_sems)
     play([f for _, _, f in events])
-    for name in ("out", "up", "down"):
-        complete(name)
+    complete("out")
+    for line in lines:
+        line.shared()
+        line.sent()
     for group in groups.values():
         for g in group:
             g.sent()
     packs.sent()
-    there.finish()
+    for one in (plane_up, there):
+        one.finish()
+    plane_cot.arrived()
+    plane_cot.finish()
+    for share in (share_joined, share_normed):
+        share.arrived()
+        share.finish()
     back.arrived()
     back.finish()
-    for copy in own_copies[2:]:
+    for copy in (own_copies[2], own_up, own_down, own_cot):
         copy.wait()
     ask.wait_send()
 
 
 def front_call(depth, devices, args):
-    cuts = dict(skip=4, qkv=4, out=8, up=8, down=8)
+    cuts = dict(skip=8, qkv=8, out=0)
     frames, model = args["hidden"].shape
     bf, f32 = jnp.bfloat16, jnp.float32
     count = devices // 2
     total = count * frames
     shape = jax.ShapeDtypeStruct
+    vmem = pl.BlockSpec(memory_space=pltpu.VMEM)
+    away = pl.BlockSpec(memory_space=pl.ANY)
 
     def whole(name):
         rows, cols = args[name].shape
         return shape((devices * rows, cols), bf)
 
-    outs = dict(
+    def by_owner(n):
+        return (depth, 2, 2, 2, n // devices, frames)
+
+    def quarter(n):
+        return (4, depth, 2, n // devices, frames)
+
+    units = 2 * depth * 128
+    rows_up = args["w_up"].shape[0]
+    far = dict(
         skip_full=whole("w_skip"),
         qkv_full=whole("w_qkv"),
         out_full=whole("w_out"),
-        up_full=whole("w_up"),
-        down_full=whole("w_down"),
+        up_here=shape((depth, 2, 2, 2 * rows_up, units), bf),
+        down_here=shape((depth, 2, 128, model), bf),
+        cot_all=shape((4, frames, model), bf),
+        xjoined=shape(quarter(2 * model), bf),
+        xnormed=shape(quarter(model), bf),
         mixed=shape((count, HEAD_DIM, frames), bf),
+    )
+    near = dict(
         times=shape((8, 128), f32),
         mods=shape((8, model), f32),
-        b_up=shape((1, 4 * model), f32),
+        b_up=shape((1, units), f32),
         b_down=shape((1, model), f32),
         base=shape((frames, model), f32),
-        normed=shape((depth, model // depth, frames), bf),
-        joined=shape((depth, 2 * model // depth, frames), bf),
         qkv=shape((3 * HEAD_DIM, total), bf),
         lse=shape((1, total), f32),
         plain=shape((HEAD_DIM, total), f32),
     )
     dma = pltpu.SemaphoreType.DMA
-    gathers = 11
+    gathers = 6
     scratch = dict(
         own_time=pltpu.VMEM((8, 128), f32),
         other_time=pltpu.VMEM((8, 128), f32),
@@ -1835,6 +2053,11 @@
         pack_full=pltpu.VMEM((devices * 8, model + 128), f32),
         skip_here=pltpu.VMEM((2 * model, model), bf),
         qkv_here=pltpu.VMEM((model, 3 * model), bf),
+        joined=pltpu.VMEM(by_owner(2 * model), bf),
+        normed=pltpu.VMEM(by_owner(model), bf),
+        normed_here=pltpu.VMEM((frames, model), bf),
+        up_out=pltpu.VMEM((4, rows_up, units), bf),
+        up_mid=pltpu.VMEM((2, 2 * rows_up, units), bf),
         heads_in=pltpu.VMEM((count, 3 * HEAD_DIM, frames), bf),
         got=pltpu.VMEM((count, 3 * HEAD_DIM, frames), bf),
         keys=pltpu.VMEM((total, 2 * HEAD_DIM), bf),
@@ -1842,7 +2065,11 @@
         mixed_out=pltpu.VMEM((count, HEAD_DIM, frames), bf),
         time_sems=dma((2,)),
         load_sems=dma((2,)),
-        own_sems=dma((5,)),
+        own_sems=dma((6,)),
+        up_sems=dma((2, 4)),
+        cot_sems=dma((2, 4)),
+        line_sems=dma((4, 16)),
+        row_sems=dma((2, 7)),
         sends=dma((gathers, Gather.SENDS)),
         recvs=dma((gathers, Gather.RECVS)),
         s1=dma((count,)),
@@ -1852,16 +2079,17 @@
         r2=dma((count,)),
         o2=dma,
     )
+    names = [*args, *far, *near, *scratch]
     made = pl.pallas_call(
-        functools.partial(front_kernel, depth, cuts),
+        functools.partial(front_kernel, depth, cuts, names),
         name="front",
-        out_shape=[outs[name] for name in FRONT_OUT],
-        in_specs=[pl.BlockSpec(memory_space=pltpu.SMEM)] + in_vmem(14),
-        out_specs=in_any(6) + in_vmem(10),
-        scratch_shapes=[scratch[name] for name in FRONT_SCRATCH],
+        out_shape=[*far.values(), *near.values()],
+        in_specs=[pl.BlockSpec(memory_space=pltpu.SMEM)] + [vmem] * (len(args) - 1),
+        out_specs=[away] * len(far) + [vmem] * len(near),
+        scratch_shapes=list(scratch.values()),
         compiler_params=kernel_params(1),
-    )(*[args[name] for name in FRONT_IN])
-    return dict(zip(FRONT_OUT, made))
+    )(*args.values())
+    return dict(zip([*far, *near], made))
 
 
 def write_kernel(count, times, sums, joined, *refs):
@@ -1930,6 +2158,7 @@
             b_skip=b_skip[None],
             b_up_part=b_up[None],
             b_down_part=b_down[None],
+            cot=cotangent[0],
             w_mod=w_mod,
             cosine=cosine,
             sine=sine,
@@ -1958,13 +2187,13 @@
             qkv=front["qkv"],
             lse=front["lse"],
             plain=front["plain"],
-            cot=cotangent[0],
-            mixed=front["mixed"].reshape(depth, model // depth, frames),
-            joined=front["joined"],
-            normed=front["normed"],
+            cot_all=front["cot_all"],
+            mixed=front["mixed"].reshape(depth, 2, 2, 2, model // devices, frames),
+            xjoined=front["xjoined"],
+            xnormed=front["xnormed"],
             w_out=front["out_full"],
-            w_up=front["up_full"],
-            w_down=front["down_full"],
+            w_up=front["up_here"].reshape(model, -1),
+            w_down=front["down_here"].reshape(-1, model),
             w_qkv=front["qkv_full"],
             w_skip=front["skip_full"],
         ),

time: 317 us -> 284 us (0.90)
  Pallas kernels: 313 us -> 279 us
    pallas_call x2, Pallas kernels: 309 us -> 275 us  [the longest x1 150 us: back_call(): pl.pallas_call(functools.partial(back_kernel, depth, shards, names), name...]
where the time goes in v3:
time: 284 us; the launch traced here: 282 us
  Pallas kernels  279 us (98%)
    pallas_call x1, Pallas kernels, back_call(): pl.pallas_call(functools.partial(back_kernel, depth, shards, names), name...  150 us
    pallas_call x1, Pallas kernels, front_call(): pl.pallas_call(functools.partial(front_kernel, depth, cuts, names), name=...  125 us

profile of v3, /device:TPU:0, one launch (start us, length us, event | category | flops | bytes accessed | tf_op | source)
XLA Modules:
  0.0 282.1 jit_solution(10845583933435608150)
XLA Ops:
  0.7 1.2 constant_dynamic-slice_fusion
  1.9 0.6 fusion
  2.6 0.8 multiply_sine_fusion
  3.3 125.2 %front.1 = (bf16[2048,1024]{1,0:T(8,128)(2,1)}, bf16[1024,3072]{1,0:T(8,128)(2,1)}, bf16[1024,1024]{1,0:T(8,128)(2,1)}, bf16[4,2,2,64,1024]{4,3,2,1,0:T(8,128)(2...) custom-call(s32[2]{0:T(128)} %bitcast.26, ...), custom_call_target="tpu_custom_call" | custom-call | tf_op jit(solution)/shard_map/front/pallas_call | solution.py:2083
  128.5 149.8 %back.1 = (bf16[128,1024]{1,0:T(8,128)(2,1)}, bf16[2,128,1024]{2,1,0:T(8,128)(2,1)}, f32[64,1024]{1,0:T(8,128)}, f32[32,3072]{1,0:T(8,128)}, f32[32,1024]{1,0:T(...) custom-call(s32[2]{0:T(128)} %bitcast.27, ...), custom_call_target="tpu_custom_call" | custom-call | tf_op jit(solution)/shard_map/back/pallas_call | solution.py:1763
  278.3 3.6 %write.1 = (bf16[128,1024]{1,0:T(8,128)(2,1)}, f32[64,1024]{1,0:T(8,128)}, f32[32,4096]{1,0:T(8,128)}, f32[32,3072]{1,0:T(8,128)}, f32[32,1024]{1,0:T(8,128)}, /...) custom-call(f32[32,8,128]{2,1,0:T(8,128)} %get-tuple-element.70.time, ...), custom_call_target="tpu_custom_call" | custom-call | tf_op jit(solution)/shard_map/write/pallas_call | solution.py:2115
  (1 shorter events, 0.0 us)

commit v4 on v3

--- a/solution.py
+++ b/solution.py
@@ -664,7 +664,7 @@
         return remote(self.src(q), self.dst(q), self.sends.at[q], self.recvs.at[q], self.to(q))
 
     def start(self):
-        for q in (3, 1, 2):
+        for q in (1, 2, 3):
             self.copy(q).start()
 
     def arrived(self):
@@ -687,6 +687,30 @@
         p = self.p
         z = (p.z + d) % p.depth
         return (p.b + 4 * (z - p.z), p.x)
+
+
+class Octet:
+    def __init__(self, place, src, dst, sends, recvs):
+        self.p, self.src, self.dst, self.sends, self.recvs = place, src, dst, sends, recvs
+        self.slot = place.y * 4 + place.c * 2 + place.x
+
+    def copy(self, k):
+        to = (self.slot + k) % 8
+        device = (self.p.z * 4 + to // 2, to % 2)
+        return remote(self.src(to), self.dst(self.slot), self.sends.at[k], self.recvs.at[k], device)
+
+    def start(self):
+        for k in range(1, 8):
+            self.copy(k).start()
+
+    def arrived(self):
+        for k in range(1, 8):
+            came = self.dst((self.slot + 8 - k) % 8)
+            remote(came, came, self.sends.at[k], self.recvs.at[k], self.p.to_x).wait_recv()
+
+    def finish(self):
+        for k in range(1, 8):
+            self.copy(k).wait_send()
 
 
 class Quad:
@@ -1015,6 +1039,21 @@
         for k in range(1, self.count):
             self.copy(k).start()
 
+    def send_to(self, device):
+        k = (device + self.count - self.p.b) % self.count
+        pl.when(k > 0)(lambda: self.copy(k).start())
+        pl.when(k == 0)(lambda: self.mine().start())
+
+    def wait_from(self, device):
+        k = (self.p.b + self.count - device) % self.count
+
+        @pl.when(k > 0)
+        def _():
+            came = self.dst.at[device]
+            remote(came, came, self.sends.at[k], self.recvs.at[k], self.p.to_x).wait_recv()
+
+        pl.when(k == 0)(lambda: self.mine().wait())
+
     def arrived(self):
         self.mine().wait()
         for k in range(1, self.count):
@@ -1066,28 +1105,37 @@
     return total.astype(jnp.bfloat16)
 
 
-def attend_open(p, lengths, got, qkv, keys, values):
-    count, _, span = got.shape
+def attend_open(p, lengths, got_kv, qkv, keys, values):
+    count, _, span = got_kv.shape
     frames = count * span
     for k in range(count):
-        qkv[:, k * span : (k + 1) * span] = got[k]
+        qkv[HEAD_DIM:, k * span : (k + 1) * span] = got_kv[k]
     position = lax.broadcasted_iota(jnp.int32, (1, frames), 1)
     hidden_key = jnp.where(position < lengths[p.x], 0.0, -1e30)
     keys[...] = jnp.concatenate([qkv[HEAD_DIM : 2 * HEAD_DIM, :], extra_rows([hidden_key], HEAD_DIM, frames)], 0).T
     values[...] = jnp.concatenate([qkv[2 * HEAD_DIM :, :], extra_rows([1.0], 16, frames)], 0)
 
 
-def attend(p, lengths, got, qkv, keys, values, mixed_out, lse, plain, block, lo, hi):
-    span = got.shape[2]
+def in_turn(p, i, blocks):
+    return (p.b // 2 + blocks - i) % blocks
+
+
+def attend(p, lengths, queries, qkv, keys, values, results, lse, plain, lo, hi):
+    count, _, span = queries.dst.shape
+    block = 2 * span
     length = lengths[p.x]
     ones = extra_rows([1.0], HEAD_DIM, block)
     scaling = HEAD_DIM ** (-0.5)
-    parts = block // span
 
     @pl.loop(lo, hi)
-    def _(j):
+    def _(i):
+        j = in_turn(p, i, count // 2)
         here = pl.ds(pl.multiple_of(j * block, block), block)
-        query = jnp.concatenate([qkv[:HEAD_DIM, here] * jnp.bfloat16(scaling), ones], 0)
+        for k in range(2):
+            queries.wait_from(2 * j + k)
+        query = jnp.concatenate([queries.dst[2 * j], queries.dst[2 * j + 1]], 1)
+        qkv[:HEAD_DIM, here] = query
+        query = jnp.concatenate([query * jnp.bfloat16(scaling), ones], 0)
         score = jnp.dot(keys[...], query, preferred_element_type=jnp.float32)
         peak = jnp.max(score, 0, keepdims=True)
         weights = jnp.exp(score - peak).astype(jnp.bfloat16)
@@ -1098,8 +1146,9 @@
         lse[:, here] = peak + jnp.log(total)
         column = lax.broadcasted_iota(jnp.int32, (HEAD_DIM, block), 1) + j * block
         kept = jnp.where(column < length, out, 0.0).astype(jnp.bfloat16)
-        for k in range(parts):
-            mixed_out[j * parts + k] = kept[:, k * span : (k + 1) * span]
+        for k in range(2):
+            results.src[2 * j + k] = kept[:, k * span : (k + 1) * span]
+            results.send_to(2 * j + k)
 
 
 def attend_back_open(p, lengths, qkv, keys, values, sums):
@@ -1116,16 +1165,19 @@
     sums[...] = jnp.zeros_like(sums)
 
 
-def attend_back(got, qkv, lse, plain, keys, values, sums, grads_out, block, lo, hi):
-    span = got.shape[2]
+def attend_back(p, upstreams, qkv, lse, plain, keys, values, sums, results, lo, hi):
+    count, _, span = upstreams.dst.shape
+    block = 2 * span
     scaling = HEAD_DIM ** (-0.5)
-    parts = block // span
 
     @pl.loop(lo, hi)
-    def _(j):
+    def _(i):
+        j = in_turn(p, i, count // 2)
         here = pl.ds(pl.multiple_of(j * block, block), block)
+        for k in range(2):
+            upstreams.wait_from(2 * j + k)
         query = qkv[:HEAD_DIM, here] * jnp.bfloat16(scaling)
-        upstream = jnp.concatenate([got[j * parts + k] for k in range(parts)], 1)
+        upstream = jnp.concatenate([upstreams.dst[2 * j], upstreams.dst[2 * j + 1]], 1)
         delta = jnp.sum(upstream.astype(jnp.float32) * plain[:, here], 0, keepdims=True)
         left = jnp.concatenate(
             [query, extra_rows([1.0, *[-t for t in three_terms(lse[:, here])]], HEAD_DIM, block)], 0
@@ -1134,17 +1186,18 @@
         weights = jnp.exp(jnp.dot(keys[...], left, preferred_element_type=jnp.float32))
         slope = jnp.dot(values[...], right, preferred_element_type=jnp.float32)
         slope = (weights * slope).astype(jnp.bfloat16)
+        query_grad = (
+            jnp.dot(qkv[HEAD_DIM : 2 * HEAD_DIM, :], slope, preferred_element_type=jnp.float32) * scaling
+        ).astype(jnp.bfloat16)
+        for k in range(2):
+            results.src[2 * j + k] = query_grad[:, k * span : (k + 1) * span]
+            results.send_to(2 * j + k)
         sums[:, HEAD_DIM:] += lax.dot_general(
             weights.astype(jnp.bfloat16), upstream, (((1,), (1,)), ((), ())), preferred_element_type=jnp.float32
         )
         sums[:, :HEAD_DIM] += lax.dot_general(
             slope, query, (((1,), (1,)), ((), ())), preferred_element_type=jnp.float32
         )
-        query_grad = (
-            jnp.dot(qkv[HEAD_DIM : 2 * HEAD_DIM, :], slope, preferred_element_type=jnp.float32) * scaling
-        ).astype(jnp.bfloat16)
-        for k in range(parts):
-            grads_out[j * parts + k, :HEAD_DIM, :] = query_grad[:, k * span : (k + 1) * span]
 
 
 def attend_back_close(sums, grads_out):
@@ -1153,7 +1206,7 @@
     @pl.loop(0, count)
     def _(k):
         rows = pl.ds(pl.multiple_of(k * span, span), span)
-        grads_out[k, HEAD_DIM:, :] = sums[rows, :].T.astype(jnp.bfloat16)
+        grads_out[k] = sums[rows, :].T.astype(jnp.bfloat16)
 
 
 def others(p, count, k):
@@ -1222,8 +1275,17 @@
     def fetch_skip(slot):
         return fetch(r.w_skip.at[pl.ds((slot // 2) * model, model), pl.ds((slot % 2) * chunk, chunk)], slot)
 
+    late_loads = [
+        pltpu.make_async_copy(src, dst, r.load_sems.at[k])
+        for k, (src, dst) in enumerate(
+            ((r.cot_far, r.cot_all), (r.qkv_far, r.qkv), (r.plain_far, r.plain), (r.xnormed_far, r.xnormed),
+             (r.xjoined_far, r.xjoined))
+        )
+    ]
     for slot in range(6):
         fetch_first(slot).start()
+    for copy in late_loads:
+        copy.start()
     pl.semaphore_wait(barrier, devices - 1)
 
     def to_sibling(src, dst, k):
@@ -1245,8 +1307,6 @@
 
     def share_late(c):
         return Quad(p, c // 6, r.glate.at[0, c], lambda k: r.glate.at[k, c], lambda k: r.late_sems.at[c, k])
-
-    pair_cot.start()
 
     length = r.lengths[p.x]
     position = p.b * frames
@@ -1266,6 +1326,9 @@
     r.bias[...] = jnp.zeros_like(r.bias)
     for slot in range(2, 6):
         fetch_first(slot).wait()
+    for copy in late_loads:
+        copy.wait()
+    pair_cot.start()
 
     @pl.loop(0, 4)
     def _(q):
@@ -1307,38 +1370,11 @@
 
             @pl.when(q == 0)
             def _():
-                r.total[:, cols] = total
+                r.own_total[:, cols] = total
 
             @pl.when(q > 0)
             def _():
                 r.part_total[q - 1, :, cols] = total.astype(bf)
-
-    pair_n2.start()
-    pair_act.start()
-    pair_gin.start()
-    plane_back.arrived()
-    middle = r.middle[...]
-    hat, rstd = normal(middle)
-    grad = r.back[...]
-    for k in range(3):
-        grad = grad + r.got_back[k].astype(jnp.float32)
-    cot = r.cot_all[0].astype(jnp.float32)
-    middle_grad = cot + normal_back(grad, hat, rstd, f_scale)
-    r.back[...] = middle_grad
-    branch_grad = middle_grad.astype(bf)
-    r.gbranch[0] = branch_grad
-    there = Exchange(p, count, r.mixed_grad, r.got, r.s1, r.r1, r.o1)
-    back = Exchange(p, count, r.grads_out, r.got_grads, r.s2, r.r2, r.o2)
-    mixed_grad = nt(r.weights[0], branch_grad[:, :half]) + nt(r.weights[1], branch_grad[:, half:])
-    r.mixed_grad[...] = (mixed_grad.astype(bf) * kept_row.astype(bf)).reshape(r.mixed_grad.shape)
-    there.start()
-    plane_total.start()
-    share_mixed.start()
-    share_branch.start()
-    for slot in range(6):
-        fetch_qkv(slot).start()
-    r.vectors[2:3, :] = jnp.sum(kept * grad * hat, 0, keepdims=True)
-    r.vectors[3:4, :] = jnp.sum(kept * grad, 0, keepdims=True)
 
     def blocks_of(first):
         return lambda j: jnp.concatenate([r.glate[k, first + j] for k in range(4)], 0)
@@ -1389,6 +1425,38 @@
             sums.append(Reduce(p, axis, x, take, rows, k * width, width, res, *rest[:5]))
             rest = rest[5:]
 
+    pair_act.start()
+    pair_n2.start()
+    pair_gin.start()
+    pair_cot.wait_recv()
+    pair_act.wait_recv()
+    down[0].begin()
+    down[0].hop(0)
+    plane_back.arrived()
+    middle = r.middle[...]
+    hat, rstd = normal(middle)
+    grad = r.back[...]
+    for k in range(3):
+        grad = grad + r.got_back[k].astype(jnp.float32)
+    cot = r.cot_all[0].astype(jnp.float32)
+    middle_grad = cot + normal_back(grad, hat, rstd, f_scale)
+    r.back[...] = middle_grad
+    branch_grad = middle_grad.astype(bf)
+    r.gbranch[0] = branch_grad
+    there = Exchange(p, count, r.mixed_grad, r.got, r.s1, r.r1, r.o1)
+    back = Exchange(p, count, r.grads_out, r.got_grads, r.s2, r.r2, r.o2)
+    queries = Exchange(p, count, r.queries_out, r.got_queries, r.s3, r.r3, r.o3)
+    mixed_grad = nt(r.weights[0], branch_grad[:, :half]) + nt(r.weights[1], branch_grad[:, half:])
+    r.mixed_grad[...] = (mixed_grad.astype(bf) * kept_row.astype(bf)).reshape(r.mixed_grad.shape)
+    there.start()
+    plane_total.start()
+    share_mixed.start()
+    share_branch.start()
+    for slot in range(6):
+        fetch_qkv(slot).start()
+    r.vectors[2:3, :] = jnp.sum(kept * grad * hat, 0, keepdims=True)
+    r.vectors[3:4, :] = jnp.sum(kept * grad, 0, keepdims=True)
+
     def end_down(k):
         def write(here, total):
             r.down_grad[:, pl.ds(pl.multiple_of(k * half + here.start, 128), here.size)] = total
@@ -1401,22 +1469,14 @@
 
         up[k].end(write)
 
-    own_slot = p.y * 4 + p.c * 2 + p.x
-
-    def up_copy(k):
-        to = (own_slot + k) % 8
-        device = (p.z * 4 + to // 2, to % 2)
-        return remote(r.up_out.at[to], r.up_got.at[own_slot], r.up_sems.at[0, k], r.up_sems.at[1, k], device)
+    ups = Octet(p, lambda to: r.up_out.at[to], lambda slot: r.up_got.at[slot], r.up_sems.at[0], r.up_sems.at[1])
 
     def up_spread():
-        for k in range(1, 8):
-            up_copy(k).start()
-        r.up_got[own_slot] = r.up_out[own_slot]
+        ups.start()
+        r.up_got[ups.slot] = r.up_out[ups.slot]
 
     def up_arrived():
-        for k in range(1, 8):
-            came = r.up_got.at[(own_slot + 8 - k) % 8]
-            remote(came, came, r.up_sems.at[0, k], r.up_sems.at[1, k], p.to_x).wait_recv()
+        ups.arrived()
         for t in range(8):
             for z in range(depth):
                 at = (z * 8 + t) * 128
@@ -1431,68 +1491,57 @@
 
     blocks = r.qkv.shape[1] // 256
     attend_back_open(p, r.lengths, r.qkv, r.keys, r.values, r.kv_sums)
-    pair_cot.wait_recv()
-    pair_act.wait_recv()
-    down[0].begin()
-    down[0].hop(0)
+    attend = functools.partial(
+        attend_back, p, there, r.qkv, r.lse, r.plain, r.keys, r.values, r.kv_sums, queries
+    )
     down[1].begin()
-    there.arrived()
-    attend = functools.partial(
-        attend_back, r.got, r.qkv, r.lse, r.plain, r.keys, r.values, r.kv_sums, r.grads_out, 256
-    )
+    down[1].hop(0)
     attend(0, blocks // 2)
     down[0].hop(1)
-    down[1].hop(0)
     attend(blocks // 2, blocks)
     attend_back_close(r.kv_sums, r.grads_out)
     back.start()
-    plane_total.arrived()
-    total = r.middle[...] + r.total[...] + r.b_down[...]
-    for k in range(3):
-        total = total + r.got_total[k].astype(jnp.float32)
-    r.output[...] = total.astype(bf)
-    down[0].hop(2)
     down[1].hop(1)
-    pair_n2.wait_recv()
-    pair_gin.wait_recv()
-    up[0].begin()
-    up[0].hop(0)
-    end_down(0)
-    down[1].hop(2)
-    up[1].begin()
-    up[0].hop(1)
-    up[1].hop(0)
-    ready([share_mixed, share_branch])
-    out[0].begin()
-    end_down(1)
-    up[0].hop(2)
-    up[1].hop(1)
-
-    back.arrived()
-
-    def unturned(at):
-        h = r.got_grads[:, at : at + HEAD_DIM, :].astype(jnp.float32)
-        first, second = h[:, : HEAD_DIM // 2, :], h[:, HEAD_DIM // 2 :, :]
-        cosine, sine = r.cosine[...][None], r.sine[...][None]
-        h = jnp.concatenate([first * cosine + second * sine, second * cosine - first * sine], 1)
-        return h.astype(bf)
-
-    for part in range(3):
-        if part < 2:
-            h = unturned(part * HEAD_DIM)
-        else:
-            h = r.got_grads[:, 2 * HEAD_DIM :, :]
+
+    cosine, sine = r.cosine[...][None], r.sine[...][None]
+
+    def send_part(part, h):
         h = h.reshape(model, frames).T
         for k in range(2):
             r.glate[0, 2 * part + k] = h[:, k * chunk : (k + 1) * chunk]
             share_late(2 * part + k).start()
-    for k in range(6):
+
+    queries.arrived()
+    send_part(0, turn(r.got_queries[...].astype(jnp.float32), cosine, -sine).astype(bf))
+    for k in range(2):
         fetch_qkv(k).wait()
         made = nt(r.glate[0, k], r.weights[k])
         if k == 0:
             r.total[...] = made
         else:
             r.total[...] += made
+    down[0].hop(2)
+    pair_n2.wait_recv()
+    pair_gin.wait_recv()
+    up[0].begin()
+    up[0].hop(0)
+    plane_total.arrived()
+    total = r.middle[...] + r.own_total[...] + r.b_down[...]
+    for k in range(3):
+        total = total + r.got_total[k].astype(jnp.float32)
+    r.output[...] = total.astype(bf)
+    ready([share_mixed, share_branch])
+    out[0].begin()
+    up[1].begin()
+    up[1].hop(0)
+    ready([share_late(0), share_late(1)])
+    qkv[0].begin()
+    back.arrived()
+    send_part(1, turn(r.got_grads[:, :HEAD_DIM, :].astype(jnp.float32), cosine, -sine).astype(bf))
+    send_part(2, r.got_grads[:, HEAD_DIM:, :])
+    for k in range(2, 6):
+        fetch_qkv(k).wait()
+        r.total[...] += nt(r.glate[0, k], r.weights[k])
     for k in range(4):
         fetch_skip(k).start()
     hat, rstd = normal(r.base[...])
@@ -1508,53 +1557,52 @@
     r.vectors[5:6, :] = jnp.sum(base_grad.astype(jnp.float32), 0, keepdims=True)
     r.vectors[6:7, :] = r.bias[...]
     r.vectors[7:8, :] = jnp.zeros((1, model), jnp.float32)
-    small = Rounds(p, r.small_sems.at[0], r.small_sems.at[1])
-
-    def small_core():
-        return small.one(0, r.vectors, r.small_got.at[0], p.to_core)
+    smalls = Octet(p, lambda to: r.vectors, lambda slot: r.plane_got.at[slot], r.small_sems.at[0], r.small_sems.at[1])
+    small = Rounds(p, r.line_sems.at[0], r.line_sems.at[1])
 
     def small_line(d):
-        return small.one(d, r.line_out, r.small_got.at[d], small.line(0, d))
-
-    def small_y():
-        return small.one(4, r.y_out, r.small_got.at[4], p.to_y)
-
-    def small_x():
-        return small.one(5, r.x_out, r.small_got.at[5], p.to_x)
-
-    def after_core():
-        small_core().wait_recv()
-        r.line_out[...] = r.vectors[...] + r.small_got[0]
+        return small.one(d, r.line_out, r.line_got.at[d], small.line(0, d))
+
+    def after_plane():
+        r.plane_got[smalls.slot] = r.vectors[...]
+        smalls.arrived()
+        halves = []
+        for x in range(2):
+            total = r.plane_got[x]
+            for k in range(1, 4):
+                total = total + r.plane_got[2 * k + x]
+            halves.append(total)
+            r.line_out[4 * x : 4 * x + 4, :] = total[0:4]
+        r.line_out[8:10, :] = halves[0][4:6] + halves[1][4:6]
+        chip = p.y * 4 + p.x
+        r.line_out[10:11, :] = r.plane_got[chip, 6:7, :] + r.plane_got[chip + 2, 6:7, :]
+        r.line_out[11:16, :] = jnp.zeros((5, model), jnp.float32)
         for d in range(1, depth):
             small_line(d).start()
 
-    def after_line():
-        total = r.line_out[...]
-        for d in range(1, depth):
-            small_line(d).wait_recv()
-            total = total + r.small_got[d]
-        r.y_out[...] = total
-        small_y().start()
-
-    def after_y():
-        small_y().wait_recv()
-        r.x_out[...] = r.y_out[...] + r.small_got[4]
-        small_x().start()
-
-    small_core().start()
-
-    def times_block(size):
-        number = p.b * 2 + p.x
-        return r.times_full.at[pl.ds(number // size * size, size)]
-
-    def times_copy(k, size, to):
-        return small.one(6 + k, times_block(size), times_block(size), to)
-
-    def times_step(k):
-        return times_copy(k, 1 << k, (p.to_x, p.to_core, p.to_y)[k])
+    smalls.start()
+    down[1].hop(2)
+    end_down(0)
+    out[0].hop(0)
+    up[0].hop(1)
+
+    number = p.b * 2 + p.x
+    timers = Octet(
+        p,
+        lambda to: r.times_full.at[number],
+        lambda slot: r.times_full.at[p.z * 8 + slot],
+        r.small_sems.at[2],
+        r.small_sems.at[3],
+    )
 
     def times_line(d):
-        return times_copy(2 + d, 8, small.line(0, d))
+        block = r.times_full.at[pl.ds(p.z * 8, 8)]
+        return small.one(3 + d, block, block, small.line(0, d))
+
+    def times_came(d):
+        z = (p.z + depth - d) % depth
+        block = r.times_full.at[pl.ds(z * 8, 8)]
+        return small.one(3 + d, block, block, small.line(0, d))
 
     for i in range(2):
         total = None
@@ -1564,29 +1612,29 @@
             total = made if total is None else total + made
         r.joined_grad[i] = total.astype(bf)
 
-    after_core()
-    end_up(0)
-    up[1].hop(2)
-    out[0].hop(0)
-    ready([share_late(0), share_late(1)])
-    qkv[0].begin()
-    end_up(1)
-    up_spread()
-    after_line()
+    qkv[0].hop(0)
+    end_down(1)
+    up[1].hop(1)
+    after_plane()
     out[0].hop(1)
     ready([share_late(6), share_late(7)])
     skip[0].begin()
-    after_y()
+    skip[1].begin()
     ready([share_late(2), share_late(3)])
     qkv[1].begin()
-    qkv[0].hop(0)
-    skip[1].begin()
+    up[0].hop(2)
+    ready([share_late(4), share_late(5)])
+    qkv[2].begin()
     out[0].hop(2)
-    up_arrived()
-
-    small_x().wait_recv()
-    mine, other = r.x_out[...], r.small_got[5]
-    first, second = jnp.where(p.x == 0, mine, other), jnp.where(p.x == 0, other, mine)
+    qkv[0].hop(1)
+    up[1].hop(2)
+
+    total = r.line_out[...]
+    for d in range(1, depth):
+        small_line(d).wait_recv()
+        total = total + r.line_got[d]
+    first, second = total[0:4], total[4:8]
+    r.line_sum[...] = total
     total = jnp.zeros((8, r.w_mod.shape[0]), jnp.float32)
     turned = r.times[...].T
     share = r.w_mod.shape[0]
@@ -1599,73 +1647,62 @@
     made = jnp.concatenate(
         [total[0:1] + total[1:2] + total[2:3], total[3:4] + total[4:5] + total[5:6], jnp.zeros((6, share), jnp.float32)]
     )
-    number = p.b * 2 + p.x
     r.times_full[number] = jnp.concatenate([made, jnp.zeros((8, 128 - share), jnp.float32)], 1)
-    times_step(0).start()
+    timers.start()
+    skip[0].hop(0)
+    qkv[1].hop(0)
+    qkv[0].hop(2)
+    end_up(0)
+    skip[1].hop(0)
+    skip[0].hop(1)
+    qkv[1].hop(1)
+    qkv[2].hop(0)
+    end_up(1)
+    up_spread()
+    timers.arrived()
+    for d in range(1, depth):
+        times_line(d).start()
     r.sums_out[...] = jnp.zeros_like(r.sums_out)
     at = pl.multiple_of((p.z * 2 + p.c) * 128, 128)
-    r.sums_out[0:1, :] = r.y_out[6:7, pl.ds(at, 128)]
+    r.sums_out[0:1, :] = r.line_sum[10:11, pl.ds(at, 128)]
     at = pl.multiple_of(number // 4 * 128, 128)
-    near = r.x_out[4:6, pl.ds(at, 128)] + r.small_got[5, 4:6, pl.ds(at, 128)]
+    near = r.line_sum[8:10, pl.ds(at, 128)]
     each = model // devices
     own = near[:, :each]
     for k in range(1, 4):
         own = jnp.where(number % 4 == k, near[:, k * each : (k + 1) * each], own)
     r.sums_out[1:2, :each] = own[0:1]
     r.sums_out[1:2, each : 2 * each] = own[1:2]
-
-    ready([share_late(4), share_late(5)])
-    qkv[2].begin()
-    qkv[0].hop(1)
-    qkv[1].hop(0)
-    skip[0].hop(0)
     out[0].end()
-    times_step(0).wait_recv()
-    times_step(1).start()
-    qkv[0].hop(2)
-    qkv[1].hop(1)
-    qkv[2].hop(0)
-    skip[0].hop(1)
-    skip[1].hop(0)
-    times_step(1).wait_recv()
-    times_step(2).start()
     qkv[0].end()
+    skip[0].hop(2)
+    skip[1].hop(1)
     qkv[1].hop(2)
     qkv[2].hop(1)
-    skip[0].hop(2)
-    skip[1].hop(1)
-    times_step(2).wait_recv()
-    for d in range(1, depth):
-        times_line(d).start()
+    skip[0].end()
+    skip[1].hop(2)
     qkv[1].end()
     qkv[2].hop(2)
-    skip[0].end()
-    skip[1].hop(2)
+    skip[1].end()
+    up_arrived()
     qkv[2].end()
-    skip[1].end()
     for d in range(1, depth):
-        times_line(d).wait_recv()
+        times_came(d).wait_recv()
     for one in [*down, *up, *out, *qkv, *skip, share_mixed, share_branch, plane_n2, plane_back, plane_total]:
         one.finish()
     for c in range(8):
         share_late(c).finish()
-    for k in range(1, 8):
-        up_copy(k).wait_send()
     for one in (pair_cot, pair_n2, pair_act, pair_gin):
         one.wait_send()
-    for one in (there, back):
+    for one in (there, back, queries, ups, smalls, timers):
         one.finish()
     for d in range(1, depth):
         small_line(d).wait_send()
         times_line(d).wait_send()
-    for k in range(3):
-        times_step(k).wait_send()
-    for one in (small_core(), small_y(), small_x()):
-        one.wait_send()
 
 
 def back_call(depth, devices, args):
-    base, qkv = args["base"], args["qkv"]
+    base, qkv = args["base"], args["qkv_far"]
     frames, model = base.shape
     count = devices // 2
     units = args["w_up"].shape[1]
@@ -1691,9 +1728,16 @@
         return pltpu.VMEM((n, *shape), kind)
 
     scratch = dict(
+        cot_all=tall(4, frames, model),
+        qkv=tall(*qkv.shape),
+        plain=tall(HEAD_DIM, qkv.shape[1], kind=f32),
+        xnormed=tall(4, depth, 2, model // devices, frames),
+        xjoined=tall(4, depth, 2, 2 * model // devices, frames),
+        load_sems=dma((5,)),
         weights=tall(6, model, 512),
         middle=tall(frames, model, kind=f32),
         total=tall(frames, model, kind=f32),
+        own_total=tall(frames, model, kind=f32),
         back=tall(frames, model, kind=f32),
         bias=tall(1, units, kind=f32),
         vectors=tall(8, model, kind=f32),
@@ -1718,12 +1762,14 @@
         keys=tall(qkv.shape[1], 2 * HEAD_DIM),
         values=tall(qkv.shape[1], 2 * HEAD_DIM),
         kv_sums=tall(qkv.shape[1], 2 * HEAD_DIM, kind=f32),
-        grads_out=tall(count, 3 * HEAD_DIM, frames),
-        got_grads=tall(count, 3 * HEAD_DIM, frames),
-        small_got=tall(6, 8, model, kind=f32),
-        line_out=tall(8, model, kind=f32),
-        y_out=tall(8, model, kind=f32),
-        x_out=tall(8, model, kind=f32),
+        grads_out=tall(count, 2 * HEAD_DIM, frames),
+        got_grads=tall(count, 2 * HEAD_DIM, frames),
+        queries_out=tall(count, HEAD_DIM, frames),
+        got_queries=tall(count, HEAD_DIM, frames),
+        plane_got=tall(8, 8, model, kind=f32),
+        line_out=tall(16, model, kind=f32),
+        line_got=tall(depth, 16, model, kind=f32),
+        line_sum=tall(16, model, kind=f32),
         weight_sems=dma((6,)),
         pair_sems=dma((2, 4)),
         n2_sems=dma((2, 4)),
@@ -1739,7 +1785,11 @@
         s2=dma((count,)),
         r2=dma((count,)),
         o2=dma,
-        small_sems=dma((2, 12)),
+        s3=dma((count,)),
+        r3=dma((count,)),
+        o3=dma,
+        small_sems=dma((4, 8)),
+        line_sems=dma((2, 8)),
     )
     shape = jax.ShapeDtypeStruct
     outs = dict(
@@ -1758,8 +1808,9 @@
     vmem = pl.BlockSpec(memory_space=pltpu.VMEM)
     specs = dict.fromkeys(args, vmem)
     specs["lengths"] = pl.BlockSpec(memory_space=pltpu.SMEM)
-    for name in ("w_out", "w_up", "w_down", "w_qkv", "w_skip"):
-        specs[name] = pl.BlockSpec(memory_space=pl.ANY)
+    for name in args:
+        if name.startswith("w_") and name != "w_mod" or name.endswith("_far"):
+            specs[name] = pl.BlockSpec(memory_space=pl.ANY)
     made = pl.pallas_call(
         functools.partial(back_kernel, depth, shards, names),
         name="back",
@@ -1790,6 +1841,14 @@
             picked = jnp.where(slot == k, part[:, k * share : (k + 1) * share], picked)
         picked = jnp.concatenate([picked, jnp.zeros((1, 128 - share), jnp.float32)], 1)
         ref[...] = jnp.where(mark, picked, 0.0)
+    half = HEAD_DIM // 2
+    position = p.b * frames + lax.broadcasted_iota(jnp.int32, (half, frames), 1)
+    length = r.lengths[p.x]
+    offset = jnp.where(position < length, position, position - length).astype(jnp.float32)
+    index = lax.broadcasted_iota(jnp.int32, (half, frames), 0).astype(jnp.float32)
+    angle = offset * jnp.exp(index * (-math.log(10000.0) / half))
+    r.cosine[...] = jnp.cos(angle)
+    r.sine[...] = jnp.sin(angle)
     greet_plane(p, count, (p.to_across, p.to_far_x))
     ask = remote(r.other_time, r.got_time, r.time_sems.at[0], r.time_sems.at[1], p.to_x)
     ask.start()
@@ -1849,7 +1908,8 @@
         for line in lines:
             line.own()
 
-    there = Exchange(p, count, r.heads_in, r.got, r.s1, r.r1, r.o1)
+    queries = Exchange(p, count, r.queries_in, r.got_queries, r.s1, r.r1, r.o1)
+    there = Exchange(p, count, r.heads_in, r.got, r.s3, r.r3, r.o3)
     back = Exchange(p, count, r.mixed_out, r.mixed, r.s2, r.r2, r.o2)
 
     def products():
@@ -1864,12 +1924,39 @@
                 left, r.w_mod[:, part * model : (part + 1) * model], preferred_element_type=jnp.float32
             )
             total = jnp.where(row == part, made, total)
-        r.pack[:, :model] = total
+        r.mods_part[0] = total
+        small.one(0, r.mods_part.at[0], r.mods_got.at[0], p.to_core).start()
+
+    def bias_tile():
         each = r.b_skip.shape[1]
-        r.pack[:, model:] = jnp.zeros((8, 128), jnp.float32)
-        r.pack[0:1, model:] = r.b_up_part[...].astype(jnp.float32)
-        r.pack[1:2, model : model + each] = r.b_skip[...].astype(jnp.float32)
-        r.pack[1:2, model + each : model + 2 * each] = r.b_down_part[...].astype(jnp.float32)
+        r.pack[...] = jnp.zeros((8, 128), jnp.float32)
+        r.pack[0:1, :] = r.b_up_part[...].astype(jnp.float32)
+        r.pack[1:2, :each] = r.b_skip[...].astype(jnp.float32)
+        r.pack[1:2, each : 2 * each] = r.b_down_part[...].astype(jnp.float32)
+
+    small = Rounds(p, r.small_sems.at[0], r.small_sems.at[1])
+
+    def small_line(d):
+        return small.one(d, r.mods_part.at[1], r.mods_got.at[d], small.line(0, d))
+
+    def after_core():
+        small.one(0, r.mods_part.at[0], r.mods_got.at[0], p.to_core).wait_recv()
+        r.mods_part[1] = r.mods_part[0] + r.mods_got[0]
+        for d in range(1, depth):
+            small_line(d).start()
+
+    def after_line():
+        total = r.mods_part[1]
+        for d in range(1, depth):
+            small_line(d).wait_recv()
+            total = total + r.mods_got[d]
+        r.mods_part[2] = total
+        small.one(4, r.mods_part.at[2], r.mods_got.at[4], p.to_y).start()
+
+    def after_y():
+        small.one(4, r.mods_part.at[2], r.mods_got.at[4], p.to_y).wait_recv()
+        r.mods_part[3] = r.mods_part[2] + r.mods_got[4]
+        small.one(5, r.mods_part.at[3], r.mods_got.at[5], p.to_x).start()
 
     def turned_inputs():
         half = depth // 2
@@ -1895,19 +1982,18 @@
         at = pl.multiple_of(p.shard(p.z, p.y, p.c, p.x) * 8, 8)
         r.pack_full[pl.ds(at, 8), :] = r.pack[...]
         packs.shared()
-        total = r.pack_full[0:8, :model]
-        for k in range(1, devices):
-            total = total + r.pack_full[k * 8 : (k + 1) * 8, :model]
+        small.one(5, r.mods_part.at[3], r.mods_got.at[5], p.to_x).wait_recv()
+        total = r.mods_part[3] + r.mods_got[5]
         mods = jnp.where(p.x == 0, total[0:4], total[4:8])
         r.mods[0:4, :] = mods
         r.mods[4:8, :] = mods
         each = model // devices
-        tiles = [r.pack_full[k * 8 : k * 8 + 2, model:] for k in range(devices)]
+        tiles = [r.pack_full[k * 8 : k * 8 + 2, :] for k in range(devices)]
         for z in range(depth):
             for c in range(2):
                 at = pl.multiple_of(p.shard(z, p.y, c, p.x) * 8, 8)
                 here = (z * 2 + c) * 128
-                r.b_up[:, here : here + 128] = r.pack_full[pl.ds(at, 8), model:][0:1]
+                r.b_up[:, here : here + 128] = r.pack_full[pl.ds(at, 8), :][0:1]
         b_skip = jnp.concatenate([t[1:2, :each] for t in tiles], 1)
         r.b_down[...] = jnp.concatenate([t[1:2, each : 2 * each] for t in tiles], 1)
         length = r.lengths[p.x]
@@ -1929,20 +2015,25 @@
         normed = r.normed_here[...]
         load_qkv().wait()
         cosine, sine = r.cosine[...][None], r.sine[...][None]
-        for part in range(3):
+        for part in (1, 2, 0):
             made = jnp.dot(
                 normed, r.qkv_here[:, part * model : (part + 1) * model], preferred_element_type=jnp.float32
             )
             made = made.T.reshape(HEADS, HEAD_DIM, frames)
             if part < 2:
                 made = turn(made, cosine, sine)
-            r.heads_in[:, part * HEAD_DIM : (part + 1) * HEAD_DIM, :] = made.astype(bf)
-        there.start()
+            if part == 0:
+                r.queries_in[...] = made.astype(bf)
+                queries.start()
+            else:
+                r.heads_in[:, (part - 1) * HEAD_DIM : part * HEAD_DIM, :] = made.astype(bf)
+            if part == 2:
+                there.start()
 
     def attention(lo, hi):
-        attend(p, r.lengths, r.got, r.qkv, r.keys, r.values, r.mixed_out, r.lse, r.plain, 256, lo, hi)
-
-    blocks = 2048 // 256
+        attend(p, r.lengths, queries, r.qkv, r.keys, r.values, back, r.lse, r.plain, lo, hi)
+
+    blocks = count // 2
 
     def first_half():
         there.arrived()
@@ -1951,22 +2042,26 @@
 
     def second_half():
         attention(blocks // 2, blocks)
-        back.start()
 
     events = []
     for k, name in enumerate(("skip", "qkv")):
         events += [(t + 1.5 * k, k, f) for g in groups[name] for t, f in g.steps()]
     events.append((0.3, 0, products))
+    events.append((0.31, 0, bias_tile))
     events.append((0.35, 0, turned_inputs))
     events.append((0.36, 0, spread_up))
+    events.append((0.9, 0, after_core))
+    events.append((2.05, 9, after_line))
+    events.append((3.05, 9, after_y))
     events += [(t + 0.5, 9, f) for t, f in packs.steps()]
     events.append((3.2, 5, lines_own))
     for g in groups["out"]:
-        events += [((5.56 if t == 0 else 6.2 + t), 2, f) for t, f in g.steps()]
+        times = {0: 3.25, 1: 5.56, 2: 7.0, 3: 7.16, 4: 8.73, 5: 9.45}
+        events += [(times[t], 2, f) for t, f in g.steps()]
     for k, line in enumerate(lines):
         events.append((5.55, 5 + k, functools.partial(line.line, 1)))
-        events.append((8.72, 5 + k, functools.partial(line.line, 2)))
-        events.append((9.6, 5 + k, functools.partial(line.line, 3)))
+        events.append((7.15, 5 + k, functools.partial(line.line, 2)))
+        events.append((8.72, 5 + k, functools.partial(line.line, 3)))
     events.append((5.6, 0, first_norm))
     events.append((5.65, 0, plane_cot.start))
     events.append((5.66, 0, share_joined.start))
@@ -1986,7 +2081,7 @@
         for g in group:
             g.sent()
     packs.sent()
-    for one in (plane_up, there):
+    for one in (plane_up, there, queries):
         one.finish()
     plane_cot.arrived()
     plane_cot.finish()
@@ -1998,6 +2093,11 @@
     for copy in (own_copies[2], own_up, own_down, own_cot):
         copy.wait()
     ask.wait_send()
+    small.one(0, r.mods_part.at[0], r.mods_got.at[0], p.to_core).wait_send()
+    for d in range(1, depth):
+        small_line(d).wait_send()
+    small.one(4, r.mods_part.at[2], r.mods_got.at[4], p.to_y).wait_send()
+    small.one(5, r.mods_part.at[3], r.mods_got.at[5], p.to_x).wait_send()
 
 
 def front_call(depth, devices, args):
@@ -2033,7 +2133,10 @@
         xnormed=shape(quarter(model), bf),
         mixed=shape((count, HEAD_DIM, frames), bf),
     )
+    half = HEAD_DIM // 2
     near = dict(
+        cosine=shape((half, frames), f32),
+        sine=shape((half, frames), f32),
         times=shape((8, 128), f32),
         mods=shape((8, model), f32),
         b_up=shape((1, units), f32),
@@ -2049,8 +2152,11 @@
         own_time=pltpu.VMEM((8, 128), f32),
         other_time=pltpu.VMEM((8, 128), f32),
         got_time=pltpu.VMEM((8, 128), f32),
-        pack=pltpu.VMEM((8, model + 128), f32),
-        pack_full=pltpu.VMEM((devices * 8, model + 128), f32),
+        pack=pltpu.VMEM((8, 128), f32),
+        pack_full=pltpu.VMEM((devices * 8, 128), f32),
+        mods_part=pltpu.VMEM((4, 8, model), f32),
+        mods_got=pltpu.VMEM((6, 8, model), f32),
+        small_sems=dma((2, 6)),
         skip_here=pltpu.VMEM((2 * model, model), bf),
         qkv_here=pltpu.VMEM((model, 3 * model), bf),
         joined=pltpu.VMEM(by_owner(2 * model), bf),
@@ -2058,8 +2164,10 @@
         normed_here=pltpu.VMEM((frames, model), bf),
         up_out=pltpu.VMEM((4, rows_up, units), bf),
         up_mid=pltpu.VMEM((2, 2 * rows_up, units), bf),
-        heads_in=pltpu.VMEM((count, 3 * HEAD_DIM, frames), bf),
-        got=pltpu.VMEM((count, 3 * HEAD_DIM, frames), bf),
+        queries_in=pltpu.VMEM((count, HEAD_DIM, frames), bf),
+        got_queries=pltpu.VMEM((count, HEAD_DIM, frames), bf),
+        heads_in=pltpu.VMEM((count, 2 * HEAD_DIM, frames), bf),
+        got=pltpu.VMEM((count, 2 * HEAD_DIM, frames), bf),
         keys=pltpu.VMEM((total, 2 * HEAD_DIM), bf),
         values=pltpu.VMEM((HEAD_DIM + 16, total), bf),
         mixed_out=pltpu.VMEM((count, HEAD_DIM, frames), bf),
@@ -2078,6 +2186,9 @@
         s2=dma((count,)),
         r2=dma((count,)),
         o2=dma,
+        s3=dma((count,)),
+        r3=dma((count,)),
+        o3=dma,
     )
     names = [*args, *far, *near, *scratch]
     made = pl.pallas_call(
@@ -2137,18 +2248,9 @@
 
 def on_device(hidden, skip_in, time_embed, lengths, cotangent, w_skip, b_skip, w_mod, w_qkv, w_out, w_up, b_up,
               w_down, b_down):
-    block, row = lax.axis_index("blk"), lax.axis_index("uly")
     blocks, rows = lax.axis_size("blk"), lax.axis_size("uly")
     devices, depth = blocks * rows, blocks // 4
     _, frames, model = hidden.shape
-    position = block * frames + jnp.arange(frames, dtype=jnp.int32)
-    length = lax.dynamic_index_in_dim(lengths, row, 0, keepdims=False)[0]
-    valid = position < length
-    half = HEAD_DIM // 2
-    freq = 10000.0 ** (-jnp.arange(half, dtype=jnp.float32) / half)
-    offsets = jnp.where(valid, position, position - length).astype(jnp.float32)
-    angle = freq[:, None] * offsets[None, :]
-    cosine, sine = jnp.cos(angle), jnp.sin(angle)
     front = front_call(
         depth,
         devices,
@@ -2160,8 +2262,6 @@
             b_down_part=b_down[None],
             cot=cotangent[0],
             w_mod=w_mod,
-            cosine=cosine,
-            sine=sine,
             hidden=hidden[0],
             skip_in=skip_in[0],
             w_skip=w_skip,
@@ -2180,17 +2280,17 @@
             mods=front["mods"],
             b_up=front["b_up"],
             b_down=front["b_down"],
-            cosine=cosine,
-            sine=sine,
+            cosine=front["cosine"],
+            sine=front["sine"],
             w_mod=w_mod,
             times=front["times"],
-            qkv=front["qkv"],
+            qkv_far=front["qkv"],
             lse=front["lse"],
-            plain=front["plain"],
-            cot_all=front["cot_all"],
+            plain_far=front["plain"],
+            cot_far=front["cot_all"],
             mixed=front["mixed"].reshape(depth, 2, 2, 2, model // devices, frames),
-            xjoined=front["xjoined"],
-            xnormed=front["xnormed"],
+            xjoined_far=front["xjoined"],
+            xnormed_far=front["xnormed"],
             w_out=front["out_full"],
             w_up=front["up_here"].reshape(model, -1),
             w_down=front["down_here"].reshape(-1, model),

time: 284 us -> 252 us (0.89)
  Pallas kernels: 279 us -> 251 us
    pallas_call x1, Pallas kernels: 150 us -> 128 us  [back_call(): pl.pallas_call(functools.partial(back_kernel, depth, shards, names), name...]
    pallas_call x1, Pallas kernels: 125 us -> 120 us  [front_call(): pl.pallas_call(functools.partial(front_kernel, depth, cuts, names), name=...]
where the time goes in v4:
time: 252 us
  Pallas kernels  251 us (100%)
    pallas_call x1, Pallas kernels, back_call(): pl.pallas_call(functools.partial(back_kernel, depth, shards, names), name...  128 us
    pallas_call x1, Pallas kernels, front_call(): pl.pallas_call(functools.partial(front_kernel, depth, cuts, names), name=...  120 us

profile of v4, /device:TPU:0, one launch (start us, length us, event | category | flops | bytes accessed | tf_op | source)
XLA Modules:
  0.0 251.6 jit_solution(17530160121633372468)
XLA Ops:
  0.6 119.6 %front.1 = (bf16[2048,1024]{1,0:T(8,128)(2,1)}, bf16[1024,3072]{1,0:T(8,128)(2,1)}, bf16[1024,1024]{1,0:T(8,128)(2,1)}, bf16[4,2,2,64,1024]{4,3,2,1,0:T(8,128)(2...) custom-call(s32[2]{0:T(128)} %bitcast.25, ...), custom_call_target="tpu_custom_call" | custom-call | tf_op jit(solution)/shard_map/front/pallas_call | solution.py:2194
  120.2 127.5 %back.1 = (bf16[128,1024]{1,0:T(8,128)(2,1)}, bf16[2,128,1024]{2,1,0:T(8,128)(2,1)}, f32[64,1024]{1,0:T(8,128)}, f32[32,3072]{1,0:T(8,128)}, f32[32,1024]{1,0:T(...) custom-call(s32[2]{0:T(128)} %bitcast.26, ...), custom_call_target="tpu_custom_call" | custom-call | tf_op jit(solution)/shard_map/back/pallas_call | solution.py:1814
  247.8 3.6 %write.1 = (bf16[128,1024]{1,0:T(8,128)(2,1)}, f32[64,1024]{1,0:T(8,128)}, f32[32,4096]{1,0:T(8,128)}, f32[32,3072]{1,0:T(8,128)}, f32[32,1024]{1,0:T(8,128)}, /...) custom-call(f32[32,8,128]{2,1,0:T(8,128)} %get-tuple-element.74.time, ...), custom_call_target="tpu_custom_call" | custom-call | tf_op jit(solution)/shard_map/write/pallas_call | solution.py:2226

commit v5 on v4

--- a/solution.py
+++ b/solution.py
@@ -1857,8 +1857,8 @@
     number = 0
     owns = []
     for name, src, dst in (
-        ("skip", r.w_skip, r.skip_full),
-        ("qkv", r.w_qkv, r.qkv_full),
+        ("skip", r.w_skip, r.skip_here),
+        ("qkv", r.w_qkv, r.qkv_here),
         ("out", r.w_out, r.out_full),
     ):
         groups[name] = []
@@ -1963,11 +1963,11 @@
         for k, ref in enumerate((r.hidden, r.skip_in)):
             r.joined[k * half : (k + 1) * half] = ref[...].T.reshape(half, *r.joined.shape[1:])
 
-    def load_skip():
-        return pltpu.make_async_copy(r.skip_full, r.skip_here, r.load_sems.at[0])
-
-    def load_qkv():
-        return pltpu.make_async_copy(r.qkv_full, r.qkv_here, r.load_sems.at[1])
+    def keep_skip():
+        return pltpu.make_async_copy(r.skip_here, r.skip_full, r.load_sems.at[0])
+
+    def keep_qkv():
+        return pltpu.make_async_copy(r.qkv_here, r.qkv_full, r.load_sems.at[1])
 
     own_copies = []
 
@@ -1978,7 +1978,6 @@
     def first_norm():
         own_copies[0].wait()
         complete("skip")
-        load_skip().start()
         at = pl.multiple_of(p.shard(p.z, p.y, p.c, p.x) * 8, 8)
         r.pack_full[pl.ds(at, 8), :] = r.pack[...]
         packs.shared()
@@ -1998,7 +1997,6 @@
         r.b_down[...] = jnp.concatenate([t[1:2, each : 2 * each] for t in tiles], 1)
         length = r.lengths[p.x]
         kept = (p.b * frames + lax.broadcasted_iota(jnp.int32, (frames, 1), 0) < length).astype(jnp.float32)
-        load_skip().wait()
         base = jnp.dot(r.hidden[...], r.skip_here[:model, :], preferred_element_type=jnp.float32)
         base = base + jnp.dot(r.skip_in[...], r.skip_here[model:, :], preferred_element_type=jnp.float32) + b_skip
         r.base[...] = base
@@ -2010,10 +2008,8 @@
     def projections():
         own_copies[1].wait()
         complete("qkv")
-        load_qkv().start()
         share_normed.start()
         normed = r.normed_here[...]
-        load_qkv().wait()
         cosine, sine = r.cosine[...][None], r.sine[...][None]
         for part in (1, 2, 0):
             made = jnp.dot(
@@ -2025,6 +2021,8 @@
             if part == 0:
                 r.queries_in[...] = made.astype(bf)
                 queries.start()
+                keep_skip().start()
+                keep_qkv().start()
             else:
                 r.heads_in[:, (part - 1) * HEAD_DIM : part * HEAD_DIM, :] = made.astype(bf)
             if part == 2:
@@ -2090,7 +2088,7 @@
         share.finish()
     back.arrived()
     back.finish()
-    for copy in (own_copies[2], own_up, own_down, own_cot):
+    for copy in (own_copies[2], own_up, own_down, own_cot, keep_skip(), keep_qkv()):
         copy.wait()
     ask.wait_send()
     small.one(0, r.mods_part.at[0], r.mods_got.at[0], p.to_core).wait_send()

time: 252 us -> 250 us (level)
  no operation moved by 1% of the time
where the time goes in v5:
time: 250 us
  Pallas kernels  249 us (100%)
    pallas_call x1, Pallas kernels, back_call(): pl.pallas_call(functools.partial(back_kernel, depth, shards, names), name...  128 us
    pallas_call x1, Pallas kernels, front_call(): pl.pallas_call(functools.partial(front_kernel, depth, cuts, names), name=...  118 us

profile of v5, /device:TPU:0, one launch (start us, length us, event | category | flops | bytes accessed | tf_op | source)
XLA Modules:
  0.0 249.7 jit_solution(7315832193674012605)
XLA Ops:
  0.6 117.5 %front.1 = (bf16[2048,1024]{1,0:T(8,128)(2,1)}, bf16[1024,3072]{1,0:T(8,128)(2,1)}, bf16[1024,1024]{1,0:T(8,128)(2,1)}, bf16[4,2,2,64,1024]{4,3,2,1,0:T(8,128)(2...) custom-call(s32[2]{0:T(128)} %bitcast.25, ...), custom_call_target="tpu_custom_call" | custom-call | tf_op jit(solution)/shard_map/front/pallas_call | solution.py:2192
  118.2 127.8 %back.1 = (bf16[128,1024]{1,0:T(8,128)(2,1)}, bf16[2,128,1024]{2,1,0:T(8,128)(2,1)}, f32[64,1024]{1,0:T(8,128)}, f32[32,3072]{1,0:T(8,128)}, f32[32,1024]{1,0:T(...) custom-call(s32[2]{0:T(128)} %bitcast.26, ...), custom_call_target="tpu_custom_call" | custom-call | tf_op jit(solution)/shard_map/back/pallas_call | solution.py:1814
  245.9 3.6 %write.1 = (bf16[128,1024]{1,0:T(8,128)(2,1)}, f32[64,1024]{1,0:T(8,128)}, f32[32,4096]{1,0:T(8,128)}, f32[32,3072]{1,0:T(8,128)}, f32[32,1024]{1,0:T(8,128)}, /...) custom-call(f32[32,8,128]{2,1,0:T(8,128)} %get-tuple-element.74.time, ...), custom_call_target="tpu_custom_call" | custom-call | tf_op jit(solution)/shard_map/write/pallas_call | solution.py:2224

commit v6 on v5

--- a/solution.py
+++ b/solution.py
@@ -2061,8 +2061,8 @@
         events.append((7.15, 5 + k, functools.partial(line.line, 2)))
         events.append((8.72, 5 + k, functools.partial(line.line, 3)))
     events.append((5.6, 0, first_norm))
-    events.append((5.65, 0, plane_cot.start))
-    events.append((5.66, 0, share_joined.start))
+    events.append((7.11, 0, plane_cot.start))
+    events.append((7.12, 0, share_joined.start))
     events.append((7.1, 0, projections))
     events.append((8.4, 0, first_half))
     events.append((9.4, 0, second_half))

time: 250 us -> 248 us (level)
    pallas_call x1, Pallas kernels: 118 us -> 114 us  [front_call(): pl.pallas_call(functools.partial(front_kernel, depth, cuts, names), name=...]
where the time goes in v6:
time: 248 us
  Pallas kernels  247 us (100%)
    pallas_call x1, Pallas kernels, back_call(): pl.pallas_call(functools.partial(back_kernel, depth, shards, names), name...  129 us
    pallas_call x1, Pallas kernels, front_call(): pl.pallas_call(functools.partial(front_kernel, depth, cuts, names), name=...  114 us

profile of v6, /device:TPU:0, one launch (start us, length us, event | category | flops | bytes accessed | tf_op | source)
XLA Modules:
  0.0 247.6 jit_solution(17957611209551629149)
XLA Ops:
  0.6 114.4 %front.1 = (bf16[2048,1024]{1,0:T(8,128)(2,1)}, bf16[1024,3072]{1,0:T(8,128)(2,1)}, bf16[1024,1024]{1,0:T(8,128)(2,1)}, bf16[4,2,2,64,1024]{4,3,2,1,0:T(8,128)(2...) custom-call(s32[2]{0:T(128)} %bitcast.25, ...), custom_call_target="tpu_custom_call" | custom-call | tf_op jit(solution)/shard_map/front/pallas_call | solution.py:2192
  115.1 128.8 %back.1 = (bf16[128,1024]{1,0:T(8,128)(2,1)}, bf16[2,128,1024]{2,1,0:T(8,128)(2,1)}, f32[64,1024]{1,0:T(8,128)}, f32[32,3072]{1,0:T(8,128)}, f32[32,1024]{1,0:T(...) custom-call(s32[2]{0:T(128)} %bitcast.26, ...), custom_call_target="tpu_custom_call" | custom-call | tf_op jit(solution)/shard_map/back/pallas_call | solution.py:1814
  243.8 3.6 %write.1 = (bf16[128,1024]{1,0:T(8,128)(2,1)}, f32[64,1024]{1,0:T(8,128)}, f32[32,4096]{1,0:T(8,128)}, f32[32,3072]{1,0:T(8,128)}, f32[32,1024]{1,0:T(8,128)}, /...) custom-call(f32[32,8,128]{2,1,0:T(8,128)} %get-tuple-element.74.time, ...), custom_call_target="tpu_custom_call" | custom-call | tf_op jit(solution)/shard_map/write/pallas_call | solution.py:2224
